TPU v7x, 32 devices: a whole 2x2x4 slice. The times are simulated.
32 devices in a mesh: groups: 2 (over x), gx: 16 (over z, y, core).
Axes of the slice: x: 2, y: 2, z: 4, core: 2. Of those that a mesh axis runs over, the one named last changes fastest.
Arguments:
- wave_state: float32 [2, 2, 64, 320, 256], P(None, 'groups', 'gx'), parts along dimension 1, may hold values from -6 to 6
- adjoint_state: float32 [2, 2, 64, 320, 256], P(None, 'groups', 'gx'), parts along dimension 1, may hold values from -6 to 6
- velocity: float32 [64, 640, 256], P('gx', 'groups'), parts along dimension 1, may hold values from 0.15 to 0.45
- wavelet: float32 [2, 32], P('groups'), parts along dimension 0, may hold values from -12 to 12
- traces: float32 [2, 32, 256], P('groups', None, 'gx'), parts along dimension 0, may hold values from -6 to 6
- source_cells: int32 [2, 3], P('groups'), parts along dimension 0, may hold values from 0 to 63, as said below
- receiver_cells: int32 [2, 3, 256], P('groups'), parts along dimension 0, may hold values from 0 to 63, as said below
- start_step: int32 [2], P('groups'), parts along dimension 0, may hold values from 0 to 27
Outputs:
- gradient: float32 [64, 640, 256], P('gx', 'groups'), parts along dimension 1
- earlier_adjoint: float32 [2, 2, 64, 320, 256], P(None, 'groups', 'gx'), parts along dimension 1
There are 2 independent parts, one for each index of `groups`. A program takes and returns all parts, laid end to end along the dimension named above; each array names one. Nothing has to cross between parts.
Inputs may be any that keep to these rules, and one draw needn't show every extreme that they name: `source_cells`: every component of a cell index is below min(64, 320, 256). `receiver_cells`: every component of a cell index is below min(64, 320, 256).
All inputs are finite; a program needn't handle non-finite values.
Results may differ from a plain program's by a relative error of at most 0.0002.
Values sent between devices are 32-bit elements; how exact they have to be, the bound alone decides.
No kernel may reach another device: no remote copies, remote signals or barrier semaphores. Data moves between devices by JAX's collectives and lax.ppermute only.
A program may use at most 128 MiB of HBM per device.

v0:
```python
import jax
import jax.numpy as jnp
from jax import lax
from jax.sharding import PartitionSpec as P

STEPS = 4


WEIGHTS = (-205.0 / 72.0, 8.0 / 5.0, -1.0 / 5.0, 8.0 / 315.0, -1.0 / 560.0)


def padded(cells, sides, width):
    for axis, dim in sides:
        count = lax.axis_size(axis)
        ends = count - 1
        head = lax.slice_in_dim(cells, 0, width, axis=dim)
        tail = lax.slice_in_dim(cells, cells.shape[dim] - width, cells.shape[dim], axis=dim)
        cells = jnp.concatenate(
            [
                lax.ppermute(tail, axis, [(i, (i + 1) % count) for i in range(ends)]),
                cells,
                lax.ppermute(head, axis, [((i + 1) % count, i) for i in range(ends)]),
            ],
            axis=dim,
        )
    return cells


def laplace_wide(widened):
    rows = widened.shape[1] - 8
    width_y = widened.shape[2] - 8
    width_z = widened.shape[3]
    middle = widened[:, 4 : 4 + rows, 4 : 4 + width_y]
    deep = jnp.pad(middle, ((0, 0), (0, 0), (0, 0), (4, 4)))
    summed = 3.0 * WEIGHTS[0] * middle
    for offset in range(1, 5):
        paired = (
            widened[:, 4 + offset : 4 + offset + rows, 4 : 4 + width_y]
            + widened[:, 4 - offset : 4 - offset + rows, 4 : 4 + width_y]
        )
        paired = (
            paired
            + widened[:, 4 : 4 + rows, 4 + offset : 4 + offset + width_y]
            + widened[:, 4 : 4 + rows, 4 - offset : 4 - offset + width_y]
        )
        paired = (
            paired
            + deep[:, :, :, 4 + offset : 4 + offset + width_z]
            + deep[:, :, :, 4 - offset : 4 - offset + width_z]
        )
        summed = summed + WEIGHTS[offset] * paired
    return summed


def inject(field, first_row, first_col, cell_x, cell_y, cell_z, values):
    shots_count, rows, cols, depth = field.shape
    row_ids = jnp.arange(rows, dtype=jnp.int32)
    col_ids = jnp.arange(cols, dtype=jnp.int32)
    depth_ids = jnp.arange(depth, dtype=jnp.int32)
    row_hit = ((cell_x - first_row)[:, :, None] == row_ids).astype(jnp.float32)
    col_hit = ((cell_y - first_col)[:, :, None] == col_ids).astype(jnp.float32)
    plane = (row_hit[:, :, :, None] * col_hit[:, :, None, :]).reshape(
        shots_count, cell_x.shape[1], rows * cols
    )
    depth_hit = jnp.where(
        cell_z[:, :, None] == depth_ids, values[:, :, None], jnp.zeros_like(values[:, :, None])
    )
    added = jnp.einsum("skp,skz->spz", plane, depth_hit, precision=lax.Precision.HIGHEST)
    return field + added.reshape(shots_count, rows, cols, depth)


def on_device(
    wave_state, adjoint_state, velocity, wavelet, traces, source_cells, receiver_cells, start_step
):
    start = start_step[0]
    slab_rows = wave_state.shape[2]
    position = lax.axis_index("gx")
    recent = lax.dynamic_slice_in_dim(traces, start + 1, STEPS, 1)
    every_trace = lax.all_gather(recent, "gx", axis=2, tiled=True)
    before = wave_state[0]
    current = wave_state[1]
    later_field = adjoint_state[0]
    latest_field = adjoint_state[1]
    squared = velocity * velocity
    first_row = position * slab_rows
    images = []
    for step_no in range(1, STEPS + 1):
        widen_rows_wide = padded(current, (("gx", 1),), 4)
        image = laplace_wide(jnp.pad(widen_rows_wide, ((0, 0), (0, 0), (4, 4), (0, 0))))
        images.append(image)
        if step_no < STEPS:
            after = 2.0 * current - before + squared * image
            source_pulse = lax.dynamic_index_in_dim(wavelet, start + step_no, 1, keepdims=False)
            after = inject(
                after,
                first_row,
                0,
                source_cells[:, 0:1],
                source_cells[:, 1:2],
                source_cells[:, 2:3],
                source_pulse[:, None],
            )
            before, current = (current, after)
    gradient = jnp.zeros(velocity.shape, jnp.float32)
    for step_no in range(STEPS, 0, -1):
        gradient = gradient + 2.0 * velocity * jnp.sum(later_field * images[step_no - 1], axis=0)
        rows_wide = padded(squared * later_field, (("gx", 1),), 4)
        earlier_field = (
            2.0 * later_field
            - latest_field
            + laplace_wide(jnp.pad(rows_wide, ((0, 0), (0, 0), (4, 4), (0, 0))))
        )
        earlier_field = inject(
            earlier_field,
            first_row,
            0,
            receiver_cells[:, 0, :],
            receiver_cells[:, 1, :],
            receiver_cells[:, 2, :],
            every_trace[:, step_no - 1, :],
        )
        latest_field, later_field = (later_field, earlier_field)
    gradient, later_field, latest_field = (gradient, later_field, latest_field)
    return (gradient, jnp.stack([later_field, latest_field]))


def solution(mesh):
    in_specs = (
        P(None, "groups", "gx", None, None),
        P(None, "groups", "gx", None, None),
        P("gx", "groups", None),
        P("groups", None),
        P("groups", None, "gx"),
        P("groups", None),
        P("groups", None, None),
        P("groups"),
    )
    out_specs = (P("gx", "groups", None), P(None, "groups", "gx", None, None))
    return jax.shard_map(
        on_device, mesh=mesh, in_specs=in_specs, out_specs=out_specs, check_vma=False
    )
```

profile of v0, /device:TPU:11, one launch (start us, length us, event | category | flops | bytes accessed | tf_op | source)
XLA Modules:
  0.0 318.3 jit_solution(16727440950536314123)
XLA Ops:
  0.7 3.1 fusion.249
  11.6 3.6 %collective-permute-start.1 = (f32[1,4,320,256]{3,2,1,0:T(8,128)S(1)}, f32[1,4,320,256]{3,2,1,0:T(8,128)}, u32[]{:S(2)}, u32[]{:S(2)}) collective-permute-start(f32[1,4,320,256]{3,2,1,0:T(8,128)S(1)} %slice_bitcast_fusion), channel_id=1, source_target_pairs={{0,1},{1,2},{2,3},{3,4},{4,5},{5,6},{6,7},{7,8},{8,9},{9,10},{10,1... | collective-permute-start | bytes 3932168 | tf_op jit(solution)/shard_map/ppermute | solution.py:20
  16.0 58.6 %all_gather.3 = f32[1,4,256]{1,2,0:T(8,128)S(1)} all-gather(f32[1,4,16]{1,2,0:T(8,128)S(1)} %constant_dynamic-slice_fusion), channel_id=1, replica_groups=mesh['groups'=2,'gx'=16] {'gx'}, dimensions={2}, use_global_device_ids=true | all-gather | bytes 4352 | tf_op jit(solution)/shard_map/all_gather | solution.py:79
  81.4 4.5 %select_maximum_fusion.6 = f32[1,12,328,256]{3,2,1,0:T(8,128)} fusion(f32[1,4,320,256]{3,2,1,0:T(8,128)} %collective-permute-done.8, f32[1,4,320,256]{3,2,1,0:T(8,128)} %fusion.249, f32[1,4,320,256]{3,2,1,0:T(8,128)} %collective-permute-done.9), kind=kLoop, calls=%fused_computation.8 | loop fusion | flops 8060928 | bytes 7962624 | tf_op jit(solution)/shard_map/concatenate | solution.py:18
  85.9 16.3 %bitcast_multiply_fusion.4 = (f32[1,4,320,256]{3,2,1,0:T(8,128)}, f32[1,4,320,256]{3,2,1,0:T(8,128)}) fusion(f32[4,320,256]{2,1,0:T(8,128)S(1)} %copy-done.2, f32[256]{0:T(256)S(1)} %get-tuple-element.5, s32[256]{0:T(256)S(1)} %bitcast.175, f32[256,320]{0,1:T(8,128)S(1)} %fusion.250, f32[256,4]{0,1:T(4,128)S(1)} %fusion.271, ...), kind=kOutput, calls=%fused_computation.445 | convolution fusion | flops 1020854272 | bytes 21305344 | tf_op jit(solution)/shard_map/skp,skz->spz/dot_general | solution.py:68
  104.5 3.9 %collective-permute-start.11 = (f32[1,4,320,256]{3,2,1,0:T(8,128)}, f32[1,4,320,256]{3,2,1,0:T(8,128)}, u32[]{:S(2)}, u32[]{:S(2)}) collective-permute-start(f32[1,4,320,256]{3,2,1,0:T(8,128)} %get-tuple-element.21), channel_id=1, source_target_pairs={{0,1},{1,2},{2,3},{3,4},{4,5},{5,6},{6,7},{7,8},{8,9},{9,10},{10,1... | collective-permute-start | bytes 3932168 | tf_op jit(solution)/shard_map/ppermute | solution.py:20
  111.5 12.2 %bitcast_add_fusion.2 = (f32[1,4,320,256]{3,2,1,0:T(8,128)}, f32[1,4,320,256]{3,2,1,0:T(8,128)S(1)}) fusion(f32[2,1,4,320,256]{4,3,2,1,0:T(8,128)} %param.8, f32[4,320,256]{2,1,0:T(8,128)S(1)} %copy-done.2, f32[256]{0:T(256)S(1)} %bitcast.167, f32[4,320]{1,0:T(4,128)S(1)} %multiply_bitcast_fusion, f32[1,12,328,256]{3,2,1,0:T(8,128)S(1)} %select_maximum_fusion.14, ...), kind=kLoop, calls=%fused_computation.442 | loop fusion | flops 13762560 | bytes 20977664 | tf_op jit(solution)/shard_map/add | solution.py:69
  123.8 4.5 %collective-permute-start.2 = (f32[1,4,320,256]{3,2,1,0:T(8,128)}, f32[1,4,320,256]{3,2,1,0:T(8,128)S(1)}, u32[]{:S(2)}, u32[]{:S(2)}) collective-permute-start(f32[1,4,320,256]{3,2,1,0:T(8,128)} %get-tuple-element.10), channel_id=1, source_target_pairs={{1,0},{2,1},{3,2},{4,3},{5,4},{6,5},{7,6},{8,7},{9,8},{10,9},{11,1... | collective-permute-start | bytes 3932168 | tf_op jit(solution)/shard_map/ppermute | solution.py:22
  130.3 5.8 %collective-permute-done.10 = f32[1,4,320,256]{3,2,1,0:T(8,128)} collective-permute-done((f32[1,4,320,256]{3,2,1,0:T(8,128)}, f32[1,4,320,256]{3,2,1,0:T(8,128)}, u32[]{:S(2)}, u32[]{:S(2)}) %collective-permute-start.10) | collective-permute-done | bytes 1310752 | tf_op jit(solution)/shard_map/ppermute | solution.py:22
  136.1 14.7 %collective-permute-done.11 = f32[1,4,320,256]{3,2,1,0:T(8,128)} collective-permute-done((f32[1,4,320,256]{3,2,1,0:T(8,128)}, f32[1,4,320,256]{3,2,1,0:T(8,128)}, u32[]{:S(2)}, u32[]{:S(2)}) %collective-permute-start.11) | collective-permute-done | bytes 1310752 | tf_op jit(solution)/shard_map/ppermute | solution.py:20
  150.8 4.3 %select_maximum_fusion.4 = f32[1,12,328,256]{3,2,1,0:T(8,128)} fusion(f32[1,4,320,256]{3,2,1,0:T(8,128)} %collective-permute-done.10, f32[1,4,320,256]{3,2,1,0:T(8,128)} %get-tuple-element.21, f32[1,4,320,256]{3,2,1,0:T(8,128)} %collective-permute-done.11), kind=kLoop, calls=%fused_computation.6 | loop fusion | flops 8060928 | bytes 7962624 | tf_op jit(solution)/shard_map/concatenate | solution.py:18
  155.1 16.2 %bitcast_multiply_fusion.3 = (f32[1,4,320,256]{3,2,1,0:T(8,128)}, f32[1,4,320,256]{3,2,1,0:T(8,128)}) fusion(f32[4,320,256]{2,1,0:T(8,128)S(1)} %copy-done.2, f32[256]{0:T(256)S(1)} %get-tuple-element.4, s32[256]{0:T(256)S(1)} %bitcast.176, f32[256,320]{0,1:T(8,128)} %copy-done.16, f32[256,4]{0,1:T(4,128)S(1)} %fusion.271, ...), kind=kOutput, calls=%fused_computation.444 | convolution fusion | flops 1020526592 | bytes 21305344 | tf_op jit(solution)/shard_map/skp,skz->spz/dot_general | solution.py:68
  173.2 4.4 %collective-permute-start.13 = (f32[1,4,320,256]{3,2,1,0:T(8,128)}, f32[1,4,320,256]{3,2,1,0:T(8,128)}, u32[]{:S(2)}, u32[]{:S(2)}) collective-permute-start(f32[1,4,320,256]{3,2,1,0:T(8,128)} %get-tuple-element.23), channel_id=1, source_target_pairs={{0,1},{1,2},{2,3},{3,4},{4,5},{5,6},{6,7},{7,8},{8,9},{9,10},{10,1... | collective-permute-start | bytes 3932168 | tf_op jit(solution)/shard_map/ppermute | solution.py:20
  181.4 13.0 %bitcast_add_fusion.1 = (f32[1,4,320,256]{3,2,1,0:T(8,128)}, f32[1,4,320,256]{3,2,1,0:T(8,128)}) fusion(f32[4,320,256]{2,1,0:T(8,128)S(1)} %copy-done.2, f32[256]{0:T(256)S(1)} %bitcast.170, f32[4,320]{1,0:T(4,128)S(1)} %multiply_bitcast_fusion, f32[256]{0:T(256)S(1)} %bitcast.168, f32[1,4,320,256]{3,2,1,0:T(8,128)S(1)} %get-tuple-element.11, ...), kind=kLoop, calls=%fused_computation.441 | loop fusion | flops 15728640 | bytes 22289408 | tf_op jit(solution)/shard_map/add | solution.py:69
  196.3 4.6 %collective-permute-start.5 = (f32[1,4,320,256]{3,2,1,0:T(8,128)}, f32[1,4,320,256]{3,2,1,0:T(8,128)}, u32[]{:S(2)}, u32[]{:S(2)}) collective-permute-start(f32[1,4,320,256]{3,2,1,0:T(8,128)} %get-tuple-element.8), channel_id=1, source_target_pairs={{0,1},{1,2},{2,3},{3,4},{4,5},{5,6},{6,7},{7,8},{8,9},{9,10},{10,1... | collective-permute-start | bytes 3932168 | tf_op jit(solution)/shard_map/ppermute | solution.py:20
  200.9 18.5 %collective-permute-done.12 = f32[1,4,320,256]{3,2,1,0:T(8,128)} collective-permute-done((f32[1,4,320,256]{3,2,1,0:T(8,128)}, f32[1,4,320,256]{3,2,1,0:T(8,128)}, u32[]{:S(2)}, u32[]{:S(2)}) %collective-permute-start.12) | collective-permute-done | bytes 1310752 | tf_op jit(solution)/shard_map/ppermute | solution.py:22
  221.9 12.8 %bitcast_multiply_fusion.2 = (f32[1,4,320,256]{3,2,1,0:T(8,128)}, f32[1,4,320,256]{3,2,1,0:T(8,128)}) fusion(f32[4,320,256]{2,1,0:T(8,128)S(1)} %copy-done.2, f32[256]{0:T(256)S(1)} %get-tuple-element.3, s32[256]{0:T(256)S(1)} %bitcast.177, f32[256,320]{0,1:T(8,128)} %copy-done.16, f32[256,4]{0,1:T(4,128)S(1)} %fusion.271, ...), kind=kOutput, calls=%fused_computation.443 | convolution fusion | flops 1020526592 | bytes 21305344 | tf_op jit(solution)/shard_map/skp,skz->spz/dot_general | solution.py:68
  239.0 8.4 %collective-permute-done.4 = f32[1,4,320,256]{3,2,1,0:T(8,128)S(1)} collective-permute-done((f32[1,4,320,256]{3,2,1,0:T(8,128)}, f32[1,4,320,256]{3,2,1,0:T(8,128)S(1)}, u32[]{:S(2)}, u32[]{:S(2)}) %collective-permute-start.4) | collective-permute-done | bytes 1310752 | tf_op jit(solution)/shard_map/ppermute | solution.py:22
  250.8 14.1 %bitcast_add_fusion = (f32[1,4,320,256]{3,2,1,0:T(8,128)}, f32[1,4,320,256]{3,2,1,0:T(8,128)}) fusion(f32[4,320,256]{2,1,0:T(8,128)} %param.10, f32[256]{0:T(256)S(1)} %bitcast.172, f32[4,320]{1,0:T(4,128)S(1)} %multiply_bitcast_fusion, f32[256]{0:T(256)S(1)} %bitcast.171, f32[1,4,320,256]{3,2,1,0:T(8,128)} %get-tuple-element.9, f32[256]{0:T(256)S(1)} %bitcast.169, ...), kind=kLoop, calls=%fused_computation.440 | loop fusion | flops 17694720 | bytes 23601152 | tf_op jit(solution)/shard_map/add | solution.py:69
  267.0 3.6 %collective-permute-start.7 = (f32[1,4,320,256]{3,2,1,0:T(8,128)}, f32[1,4,320,256]{3,2,1,0:T(8,128)S(1)}, u32[]{:S(2)}, u32[]{:S(2)}) collective-permute-start(f32[1,4,320,256]{3,2,1,0:T(8,128)} %get-tuple-element.6), channel_id=1, source_target_pairs={{0,1},{1,2},{2,3},{3,4},{4,5},{5,6},{6,7},{7,8},{8,9},{9,10},{10,1... | collective-permute-start | bytes 3932168 | tf_op jit(solution)/shard_map/ppermute | solution.py:20
  270.6 8.9 %collective-permute-done.15 = f32[1,4,320,256]{3,2,1,0:T(8,128)} collective-permute-done((f32[1,4,320,256]{3,2,1,0:T(8,128)}, f32[1,4,320,256]{3,2,1,0:T(8,128)}, u32[]{:S(2)}, u32[]{:S(2)}) %collective-permute-start.15) | collective-permute-done | bytes 1310752 | tf_op jit(solution)/shard_map/ppermute | solution.py:20
  282.0 11.9 %fusion.5 = f32[1,1,4,320,256]{4,3,2,1,0:T(8,128)} fusion(f32[1,4,320,256]{3,2,1,0:T(8,128)} %collective-permute-done.15, f32[1,4,320,256]{3,2,1,0:T(8,128)} %get-tuple-element.25, f32[1,4,320,256]{3,2,1,0:T(8,128)} %collective-permute-done.14, f32[1,12,328,256]{3,2,1,0:T(8,128)S(1)} %select_maximum_fusion, f32[1,4,320,256]{3,2,1,0:T(8,128)} %get-tuple-element.24, ...), kind=kOutput, calls=%fused_computation.156 | convolution fusion | flops 1019871232 | bytes 18683904 | tf_op jit(solution)/shard_map/skp,skz->spz/dot_general | solution.py:68
  293.9 3.2 pad_maximum_fusion
  300.7 17.4 %bitcast_multiply_fusion = f32[4,320,256]{2,1,0:T(8,128)} fusion(f32[4,320,256]{2,1,0:T(8,128)S(1)} %copy-done.3, f32[1,4,320,256]{3,2,1,0:T(8,128)} %get-tuple-element.26, f32[1,4,320,256]{3,2,1,0:T(8,128)S(1)} %copy-done.6, f32[1,4,320,256]{3,2,1,0:T(8,128)} %get-tuple-element.24, f32[1,4,320,256]{3,2,1,0:T(8,128)} %get-tuple-element.9, ...), kind=kLoop, calls=%fused_computation.429 | loop fusion | flops 14417920 | bytes 26214400 | tf_op jit(solution)/shard_map/add | solution.py:106
  (83 shorter events, 47.2 us)
Async XLA Ops:
  3.7 70.8 %copy-start.18 = (s32[1,3]{1,0:T(1,128)S(1)}, s32[1,3]{1,0:T(1,128)}, u32[]{:S(2)}) copy-start(s32[1,3]{1,0:T(1,128)} %param.13) | copy-start | bytes 40
  3.8 71.4 %copy-start.19 = (f32[1,32]{1,0:T(1,128)S(1)}, f32[1,32]{1,0:T(1,128)}, u32[]{:S(2)}) copy-start(f32[1,32]{1,0:T(1,128)} %param.11) | copy-start | bytes 388
  3.8 77.5 %copy-start.20 = (s32[1,3,256]{2,0,1:T(1,128)S(1)}, s32[1,3,256]{2,0,1:T(1,128)}, u32[]{:S(2)}) copy-start(s32[1,3,256]{2,0,1:T(1,128)} %param.14) | copy-start | bytes 9220
  3.8 77.7 %collective-permute-start.8 = (f32[1,4,320,256]{3,2,1,0:T(8,128)}, f32[1,4,320,256]{3,2,1,0:T(8,128)}, u32[]{:S(2)}, u32[]{:S(2)}) collective-permute-start(f32[1,4,320,256]{3,2,1,0:T(8,128)} %fusion.249), channel_id=1, source_target_pairs={{1,0},{2,1},{3,2},{4,3},{5,4},{6,5},{7,6},{8,7},{9,8},{10,9},{11,1... | collective-permute-start | bytes 3932168 | tf_op jit(solution)/shard_map/ppermute | solution.py:22
  6.5 75.0 %collective-permute-start.9 = (f32[1,4,320,256]{3,2,1,0:T(8,128)}, f32[1,4,320,256]{3,2,1,0:T(8,128)}, u32[]{:S(2)}, u32[]{:S(2)}) collective-permute-start(f32[1,4,320,256]{3,2,1,0:T(8,128)} %fusion.249), channel_id=1, source_target_pairs={{0,1},{1,2},{2,3},{3,4},{4,5},{5,6},{6,7},{7,8},{8,9},{9,10},{10,1... | collective-permute-start | bytes 3932168 | tf_op jit(solution)/shard_map/ppermute | solution.py:20
  9.6 99.8 %copy-start.8 = (f32[1,4,320,256]{3,2,1,0:T(8,128)}, f32[1,4,320,256]{3,2,1,0:T(8,128)S(1)}, u32[]{:S(2)}) copy-start(f32[1,4,320,256]{3,2,1,0:T(8,128)S(1)} %slice_bitcast_fusion) | copy-start | bytes 3932164
  9.6 98.7 %collective-permute-start = (f32[1,4,320,256]{3,2,1,0:T(8,128)S(1)}, f32[1,4,320,256]{3,2,1,0:T(8,128)S(1)}, u32[]{:S(2)}, u32[]{:S(2)}) collective-permute-start(f32[1,4,320,256]{3,2,1,0:T(8,128)S(1)} %slice_bitcast_fusion), channel_id=1, source_target_pairs={{1,0},{2,1},{3,2},{4,3},{5,4},{6,5},{7,6},{8,7},{9,8},{10,9},{11,1... | collective-permute-start | bytes 3932168 | tf_op jit(solution)/shard_map/ppermute | solution.py:22
  11.6 97.9 %collective-permute-start.1 = (f32[1,4,320,256]{3,2,1,0:T(8,128)S(1)}, f32[1,4,320,256]{3,2,1,0:T(8,128)}, u32[]{:S(2)}, u32[]{:S(2)}) collective-permute-start(f32[1,4,320,256]{3,2,1,0:T(8,128)S(1)} %slice_bitcast_fusion), channel_id=1, source_target_pairs={{0,1},{1,2},{2,3},{3,4},{4,5},{5,6},{6,7},{7,8},{8,9},{9,10},{10,1... | collective-permute-start | bytes 3932168 | tf_op jit(solution)/shard_map/ppermute | solution.py:20
  102.3 33.8 %collective-permute-start.10 = (f32[1,4,320,256]{3,2,1,0:T(8,128)}, f32[1,4,320,256]{3,2,1,0:T(8,128)}, u32[]{:S(2)}, u32[]{:S(2)}) collective-permute-start(f32[1,4,320,256]{3,2,1,0:T(8,128)} %get-tuple-element.21), channel_id=1, source_target_pairs={{1,0},{2,1},{3,2},{4,3},{5,4},{6,5},{7,6},{8,7},{9,8},{10,9},{11,1... | collective-permute-start | bytes 3932168 | tf_op jit(solution)/shard_map/ppermute | solution.py:22
  104.5 46.3 %collective-permute-start.11 = (f32[1,4,320,256]{3,2,1,0:T(8,128)}, f32[1,4,320,256]{3,2,1,0:T(8,128)}, u32[]{:S(2)}, u32[]{:S(2)}) collective-permute-start(f32[1,4,320,256]{3,2,1,0:T(8,128)} %get-tuple-element.21), channel_id=1, source_target_pairs={{0,1},{1,2},{2,3},{3,4},{4,5},{5,6},{6,7},{7,8},{8,9},{9,10},{10,1... | collective-permute-start | bytes 3932168 | tf_op jit(solution)/shard_map/ppermute | solution.py:20
  123.8 57.6 %copy-start.5 = (f32[1,4,320,256]{3,2,1,0:T(8,128)}, f32[1,4,320,256]{3,2,1,0:T(8,128)S(1)}, u32[]{:S(2)}) copy-start(f32[1,4,320,256]{3,2,1,0:T(8,128)S(1)} %get-tuple-element.11) | copy-start | bytes 3932164
  123.8 31.4 %copy-start.15 = (f32[2,1,4,320,256]{4,3,2,1,0:T(8,128)S(1)}, f32[2,1,4,320,256]{4,3,2,1,0:T(8,128)}, u32[]{:S(2)}) copy-start(f32[2,1,4,320,256]{4,3,2,1,0:T(8,128)} %param.9) | copy-start | bytes 7864324
  123.8 53.9 %collective-permute-start.2 = (f32[1,4,320,256]{3,2,1,0:T(8,128)}, f32[1,4,320,256]{3,2,1,0:T(8,128)S(1)}, u32[]{:S(2)}, u32[]{:S(2)}) collective-permute-start(f32[1,4,320,256]{3,2,1,0:T(8,128)} %get-tuple-element.10), channel_id=1, source_target_pairs={{1,0},{2,1},{3,2},{4,3},{5,4},{6,5},{7,6},{8,7},{9,8},{10,9},{11,1... | collective-permute-start | bytes 3932168 | tf_op jit(solution)/shard_map/ppermute | solution.py:22
  128.3 50.6 %collective-permute-start.3 = (f32[1,4,320,256]{3,2,1,0:T(8,128)}, f32[1,4,320,256]{3,2,1,0:T(8,128)}, u32[]{:S(2)}, u32[]{:S(2)}) collective-permute-start(f32[1,4,320,256]{3,2,1,0:T(8,128)} %get-tuple-element.10), channel_id=1, source_target_pairs={{0,1},{1,2},{2,3},{3,4},{4,5},{5,6},{6,7},{7,8},{8,9},{9,10},{10,1... | collective-permute-start | bytes 3932168 | tf_op jit(solution)/shard_map/ppermute | solution.py:20
  171.3 48.1 %collective-permute-start.12 = (f32[1,4,320,256]{3,2,1,0:T(8,128)}, f32[1,4,320,256]{3,2,1,0:T(8,128)}, u32[]{:S(2)}, u32[]{:S(2)}) collective-permute-start(f32[1,4,320,256]{3,2,1,0:T(8,128)} %get-tuple-element.23), channel_id=1, source_target_pairs={{1,0},{2,1},{3,2},{4,3},{5,4},{6,5},{7,6},{8,7},{9,8},{10,9},{11,1... | collective-permute-start | bytes 3932168 | tf_op jit(solution)/shard_map/ppermute | solution.py:22
  173.2 46.2 %collective-permute-start.13 = (f32[1,4,320,256]{3,2,1,0:T(8,128)}, f32[1,4,320,256]{3,2,1,0:T(8,128)}, u32[]{:S(2)}, u32[]{:S(2)}) collective-permute-start(f32[1,4,320,256]{3,2,1,0:T(8,128)} %get-tuple-element.23), channel_id=1, source_target_pairs={{0,1},{1,2},{2,3},{3,4},{4,5},{5,6},{6,7},{7,8},{8,9},{9,10},{10,1... | collective-permute-start | bytes 3932168 | tf_op jit(solution)/shard_map/ppermute | solution.py:20
  194.4 53.0 %collective-permute-start.4 = (f32[1,4,320,256]{3,2,1,0:T(8,128)}, f32[1,4,320,256]{3,2,1,0:T(8,128)S(1)}, u32[]{:S(2)}, u32[]{:S(2)}) collective-permute-start(f32[1,4,320,256]{3,2,1,0:T(8,128)} %get-tuple-element.8), channel_id=1, source_target_pairs={{1,0},{2,1},{3,2},{4,3},{5,4},{6,5},{7,6},{8,7},{9,8},{10,9},{11,1... | collective-permute-start | bytes 3932168 | tf_op jit(solution)/shard_map/ppermute | solution.py:22
  196.3 52.1 %collective-permute-start.5 = (f32[1,4,320,256]{3,2,1,0:T(8,128)}, f32[1,4,320,256]{3,2,1,0:T(8,128)}, u32[]{:S(2)}, u32[]{:S(2)}) collective-permute-start(f32[1,4,320,256]{3,2,1,0:T(8,128)} %get-tuple-element.8), channel_id=1, source_target_pairs={{0,1},{1,2},{2,3},{3,4},{4,5},{5,6},{6,7},{7,8},{8,9},{9,10},{10,1... | collective-permute-start | bytes 3932168 | tf_op jit(solution)/shard_map/ppermute | solution.py:20
  234.6 44.9 %collective-permute-start.15 = (f32[1,4,320,256]{3,2,1,0:T(8,128)}, f32[1,4,320,256]{3,2,1,0:T(8,128)}, u32[]{:S(2)}, u32[]{:S(2)}) collective-permute-start(f32[1,4,320,256]{3,2,1,0:T(8,128)} %get-tuple-element.25), channel_id=1, source_target_pairs={{0,1},{1,2},{2,3},{3,4},{4,5},{5,6},{6,7},{7,8},{8,9},{9,10},{10,1... | collective-permute-start | bytes 3932168 | tf_op jit(solution)/shard_map/ppermute | solution.py:20
  236.6 42.9 %collective-permute-start.14 = (f32[1,4,320,256]{3,2,1,0:T(8,128)}, f32[1,4,320,256]{3,2,1,0:T(8,128)}, u32[]{:S(2)}, u32[]{:S(2)}) collective-permute-start(f32[1,4,320,256]{3,2,1,0:T(8,128)} %get-tuple-element.25), channel_id=1, source_target_pairs={{1,0},{2,1},{3,2},{4,3},{5,4},{6,5},{7,6},{8,7},{9,8},{10,9},{11,1... | collective-permute-start | bytes 3932168 | tf_op jit(solution)/shard_map/ppermute | solution.py:22
  264.9 17.0 %copy-start.9 = (f32[1,4,320,256]{3,2,1,0:T(8,128)S(1)}, f32[1,4,320,256]{3,2,1,0:T(8,128)}, u32[]{:S(2)}) copy-start(f32[1,4,320,256]{3,2,1,0:T(8,128)} %get-tuple-element.26) | copy-start | bytes 3932164
  264.9 32.2 %collective-permute-start.6 = (f32[1,4,320,256]{3,2,1,0:T(8,128)}, f32[1,4,320,256]{3,2,1,0:T(8,128)S(1)}, u32[]{:S(2)}, u32[]{:S(2)}) collective-permute-start(f32[1,4,320,256]{3,2,1,0:T(8,128)} %get-tuple-element.6), channel_id=1, source_target_pairs={{1,0},{2,1},{3,2},{4,3},{5,4},{6,5},{7,6},{8,7},{9,8},{10,9},{11,1... | collective-permute-start | bytes 3932168 | tf_op jit(solution)/shard_map/ppermute | solution.py:22
  267.0 30.1 %collective-permute-start.7 = (f32[1,4,320,256]{3,2,1,0:T(8,128)}, f32[1,4,320,256]{3,2,1,0:T(8,128)S(1)}, u32[]{:S(2)}, u32[]{:S(2)}) collective-permute-start(f32[1,4,320,256]{3,2,1,0:T(8,128)} %get-tuple-element.6), channel_id=1, source_target_pairs={{0,1},{1,2},{2,3},{3,4},{4,5},{5,6},{6,7},{7,8},{8,9},{9,10},{10,1... | collective-permute-start | bytes 3932168 | tf_op jit(solution)/shard_map/ppermute | solution.py:20
  300.7 17.4 %copy-start.1 = (f32[1,32,16]{1,2,0:T(8,128)S(1)}, f32[1,32,16]{1,2,0:T(8,128)}, u32[]{:S(2)}) copy-start(f32[1,32,16]{1,2,0:T(8,128)} %param.12) | copy-start | bytes 6148
  (13 other events, 69.2 us)
where the time goes:
time: 320 us; the launch traced here: 318 us
  other arithmetic  90.6 us (28%)
  blocking collectives  58.6 us (18%)
  matrix products  57.2 us (18%)
  waiting for transfers between devices  56.5 us (18%)
  starting transfers between devices  46.7 us (15%)
  local copies, waits for them, and re-layouts  6.12 us (2%)
    all_gather x1, blocking collectives, on_device(): every_trace = lax.all_gather(recent, 'gx', axis=2, tiled=True)  58.6 us
    dot_general x4, matrix products, inject(): jnp.einsum('skp,skz->spz', plane, depth_hit, precision=lax.Precision.HIGH...  57.2 us
    add x3, other arithmetic, inject(): return field + added.reshape(shots_count, rows, cols, depth)  39.3 us
    ppermute x8, waiting for transfers between devices, padded(): lax.ppermute(head, axis, [((i + 1) % count, i) for i in range(ends)])  32.7 us
    ppermute x8, starting transfers between devices, padded(): lax.ppermute(tail, axis, [(i, (i + 1) % count) for i in range(ends)])  27 us
    ppermute x8, waiting for transfers between devices, padded(): lax.ppermute(tail, axis, [(i, (i + 1) % count) for i in range(ends)])  23.8 us
    concatenate x8, other arithmetic, padded(): jnp.concatenate([lax.ppermute(tail, axis, [(i, (i + 1) % count) for i in...  23.1 us
    ppermute x8, starting transfers between devices, padded(): lax.ppermute(head, axis, [((i + 1) % count, i) for i in range(ends)])  19.7 us
  transfers between devices with their start and end apart: 16, of which 6 were waited for; matrix products, arithmetic and copies ran while one was open for 40% of the time, Pallas kernels for 0%

commit v1 on v0

v1 whole, which is shorter than its diff:
```python
import functools

import jax
import jax.numpy as jnp
from jax import lax
from jax.experimental import pallas as pl
from jax.experimental.pallas import tpu as pltpu
from jax.sharding import PartitionSpec as P

STEPS = 4
WEIGHTS = (-205.0 / 72.0, 8.0 / 5.0, -1.0 / 5.0, 8.0 / 315.0, -1.0 / 560.0)
UNIT = WEIGHTS[1]
REACH = 4
EXTRA = REACH * STEPS
F32 = jnp.float32
BF16 = jnp.bfloat16
ANY = pl.BlockSpec(memory_space=pl.ANY)
VMEM = pl.BlockSpec(memory_space=pltpu.VMEM)
SMEM = pl.BlockSpec(memory_space=pltpu.SMEM)


def place():
    position = lax.axis_index("gx")
    return position // 4, (position % 4) // 2, position % 2


def banded(size):
    shape = (size, size)
    apart = jnp.abs(
        lax.broadcasted_iota(jnp.int32, shape, 0) - lax.broadcasted_iota(jnp.int32, shape, 1)
    )
    band = jnp.zeros(shape, F32)
    for offset in range(1, REACH + 1):
        band = jnp.where(apart == offset, WEIGHTS[offset] / UNIT, band)
    return band.astype(BF16)


def two_terms(value):
    high = value.astype(BF16)
    return high, (value - high.astype(F32)).astype(BF16)


def dot(left, right, contract=((1,), (0,))):
    return lax.dot_general(left, right, (contract, ((), ())), preferred_element_type=F32)


class Copies:
    def __init__(self, sems):
        self.sems, self.used, self.going = sems, 0, []

    def start(self, source, target):
        copy = pltpu.make_async_copy(source, target, self.sems.at[self.used])
        self.used += 1
        copy.start()
        self.going.append(copy)

    def wait(self):
        for copy in self.going:
            copy.wait()
        self.going = []


class Sizes:
    def __init__(self, rows, cols, depth):
        self.rows, self.cols, self.depth = rows, cols, depth
        self.half = cols // 2
        self.wide = self.half + EXTRA

    def window(self, half):
        return pl.ds(pl.multiple_of(half * (self.half - EXTRA), 16), self.wide)

    def own(self, half):
        return pl.ds(pl.multiple_of(half * EXTRA, 16), self.half)

    def final(self, half):
        return pl.ds(pl.multiple_of(half * self.half, 16), self.half)

    @property
    def pair(self):
        return (2, self.rows, self.wide, self.depth)

    @property
    def block(self):
        return (self.rows, self.wide, self.depth)

    @property
    def sent(self):
        return (self.rows, self.half, self.depth)

    @property
    def chain(self):
        return (5 * self.rows, self.wide, self.depth)


def load_split(copies, sizes, own, received, target):
    _, half, _ = place()
    copies.start(own.at[:, sizes.window(half), :], target.at[half])
    copies.start(received, target.at[1 - half])


def load_chain(copies, sizes, mine, other, beside, chain):
    _, _, core = place()
    rows = sizes.rows

    def at(index):
        return chain.at[pl.ds(index * rows, rows)]

    copies.start(mine.at[0], at(1))
    copies.start(mine.at[1], at(3))
    copies.start(other.at[0], at(2 - 2 * core))
    copies.start(other.at[1], at(4 - 2 * core))
    copies.start(beside, at(4 * core))


def differences(sizes, chain, mixed, added=None):
    rows = sizes.rows
    band_y, band_z = banded(sizes.wide), banded(sizes.depth)
    for slot in range(2):
        for row in range(rows):
            high, low = two_terms(chain[(2 * slot + 1) * rows + row])
            total = dot(high, band_z) + dot(low, band_z) + dot(band_y, high) + dot(band_y, low)
            total = UNIT * total
            if added is not None:
                total = total + added(slot, row)
            mixed[slot, row] = total


def sweep(sizes, chain, mixed, finish):
    rows = sizes.rows

    @pl.loop(0, sizes.wide // 8)
    def _(step):
        cut = pl.ds(pl.multiple_of(step * 8, 8), 8)
        for slot in range(2):
            near = [chain[2 * slot * rows + row, cut, :] for row in range(3 * rows)]
            for row in range(rows):
                centre = near[rows + row]
                total = 3.0 * WEIGHTS[0] * centre + mixed[slot, row, cut, :]
                for offset in range(1, REACH + 1):
                    total = total + WEIGHTS[offset] * (
                        near[rows + row + offset] + near[rows + row - offset]
                    )
                finish(slot, row, cut, centre, total)


def run(body, name, operands, specs, outs, scratch, aliases=None, flops=400_000_000, sems=24):
    return pl.pallas_call(
        body,
        name=name,
        out_shape=[jax.ShapeDtypeStruct(shape, F32) for shape in outs],
        in_specs=specs,
        out_specs=[ANY] * len(outs),
        scratch_shapes=[pltpu.VMEM(shape, F32) for shape in scratch]
        + [pltpu.SemaphoreType.DMA((sems,))],
        input_output_aliases=aliases or {},
        compiler_params=pltpu.CompilerParams(vmem_limit_bytes=32 * 2**20),
        cost_estimate=pl.CostEstimate(flops=flops, bytes_accessed=8_000_000, transcendentals=0),
    )(*operands)


def adjoint_begin(sizes, velocity, velocity_in, adjoint, latest_in):
    def body(v_ref, vin_ref, a_ref, ain_ref, v_out, a_out, u_out, z_out, v, a, u, sems):
        _, _, core = place()
        copies = Copies(sems)
        load_split(copies, sizes, v_ref, vin_ref, v)
        load_split(copies, sizes, a_ref.at[0, 0], ain_ref, a)
        copies.wait()

        @pl.loop(0, sizes.wide // 8)
        def _(step):
            cut = pl.ds(pl.multiple_of(step * 8, 8), 8)
            speed = v[:, :, cut, :]
            u[:, :, cut, :] = speed * speed * a[:, :, cut, :]

        copies.start(u.at[core], z_out)
        copies.start(u, u_out)
        copies.start(v, v_out)
        copies.start(a, a_out)
        copies.wait()

    return run(
        body,
        "adjoint_begin",
        (velocity, velocity_in, adjoint, latest_in),
        [ANY] * 4,
        [sizes.pair, sizes.pair, sizes.pair, sizes.block],
        [sizes.pair] * 3,
    )


def adjoint_step(sizes, step_no, scaled, other, beside, later, latest, speed, cells, samples, whole):
    split = isinstance(latest, tuple)
    more = step_no > 1
    ends = step_no <= 2
    carried = whole is not None
    n_in = 8 + split + carried

    def body(*refs):
        u_ref, other_ref, beside_ref, later_ref, v_ref, cells_ref, samples_ref = refs[:7]
        latest_refs = refs[7 : 8 + split]
        rest = list(refs[n_in:])
        if more:
            next_out, scaled_out, z_out = rest[:3]
            rest = rest[3:]
        if ends:
            whole_out, sent_out = rest[:2]
            rest = rest[2:]
        chain, mixed, late, last, v, u, sems = rest
        level, half, core = place()
        copies = Copies(sems)
        load_chain(copies, sizes, u_ref, other_ref, beside_ref, chain)
        copies.start(later_ref, late)
        if split:
            load_split(copies, sizes, latest_refs[0].at[1, 0], latest_refs[1], last)
        else:
            copies.start(latest_refs[0], last)
        if more:
            copies.start(v_ref, v)
        where_x, where_y, where_z = (cells_ref[0, axis : axis + 1, :] for axis in range(3))
        count = where_x.shape[1]
        depth_ids = lax.broadcasted_iota(jnp.int32, (sizes.depth, count), 0)
        values = jnp.where(where_z == depth_ids, samples_ref[0, step_no - 1 : step_no, :], 0.0)
        value_high, value_low = two_terms(values)
        first_col = half * (sizes.half - EXTRA)
        col_ids = lax.broadcasted_iota(jnp.int32, (sizes.wide, count), 0) + first_col

        def added(slot, row):
            this_row = ((level * 2 + slot) * 2 + core) * sizes.rows + row
            col_of = jnp.where(where_x == this_row, where_y, -1)
            hit = jnp.where(col_of == col_ids, 1.0, 0.0).astype(BF16)
            across = ((1,), (1,))
            return dot(hit, value_high, across) + dot(hit, value_low, across)

        copies.wait()
        differences(sizes, chain, mixed, added)

        def finish(slot, row, cut, centre, total):
            value = 2.0 * late[slot, row, cut, :] - last[slot, row, cut, :] + total
            last[slot, row, cut, :] = value
            if more:
                here = v[slot, row, cut, :]
                u[slot, row, cut, :] = here * here * value

        sweep(sizes, chain, mixed, finish)
        if more:
            copies.start(u.at[core], z_out)
            copies.start(u, scaled_out)
            copies.start(last, next_out)
        if ends:
            copies.start(last.at[1 - half, :, sizes.own(half), :], sent_out)
            copies.start(
                last.at[half, :, sizes.own(half), :],
                whole_out.at[step_no - 1, 0, :, sizes.final(half), :],
            )
        copies.wait()

    latest = latest if split else (latest,)
    operands = (scaled, other, beside, later, speed, cells, samples, *latest)
    specs = [ANY] * 5 + [VMEM] * 2 + [ANY] * (1 + split)
    outs = []
    aliases = {}
    if more:
        outs += [sizes.pair, sizes.pair, sizes.block]
    if ends:
        outs += [(2, 1, sizes.rows, sizes.cols, sizes.depth), sizes.sent]
    if carried:
        aliases = {len(operands): len(outs) - 2}
        operands += (whole,)
        specs += [ANY]
    return run(
        body,
        f"adjoint_{step_no}",
        operands,
        specs,
        outs,
        [sizes.chain] + [sizes.pair] * 5,
        aliases,
    )


def forward_begin(sizes, wave, received):
    def body(w_ref, in_ref, c_out, z_out, c, sems):
        _, _, core = place()
        copies = Copies(sems)
        load_split(copies, sizes, w_ref.at[1, 0], in_ref, c)
        copies.wait()
        copies.start(c.at[core], z_out)
        copies.start(c, c_out)
        copies.wait()

    return run(
        body,
        "forward_begin",
        (wave, received),
        [ANY] * 2,
        [sizes.pair, sizes.block],
        [sizes.pair],
    )


def forward_step(sizes, step_no, current, other, beside, before, speed, later, gradient, source):
    split = isinstance(before, tuple)
    more = step_no < STEPS
    adds = gradient is not None
    n_before = (1 + split) if more else 0
    n_in = 5 + adds + n_before + 3 * more

    def body(*refs):
        c_ref, other_ref, beside_ref, v_ref, later_ref = refs[:5]
        g_ref = refs[5] if adds else None
        before_refs = refs[5 + adds : 5 + adds + n_before]
        rest = list(refs[n_in:])
        if more:
            cells_ref, wavelet_ref, start_ref = refs[n_in - 3 : n_in]
            next_out, z_out, g_out = rest[:3]
            rest = rest[3:]
        else:
            g_out, sent_out = rest[:2]
            rest = rest[2:]
        chain, mixed, late, last, v, g, sems = rest
        level, half, core = place()
        copies = Copies(sems)
        load_chain(copies, sizes, c_ref, other_ref, beside_ref, chain)
        copies.start(later_ref, late)
        copies.start(v_ref, v)
        if adds:
            copies.start(g_ref, g)
        if more:
            if split:
                load_split(copies, sizes, before_refs[0].at[0, 0], before_refs[1], last)
            else:
                copies.start(before_refs[0], last)
        copies.wait()
        differences(sizes, chain, mixed)

        def finish(slot, row, cut, centre, total):
            product = late[slot, row, cut, :] * total
            if adds:
                product = product + g[slot, row, cut, :]
            here = v[slot, row, cut, :]
            if more:
                g[slot, row, cut, :] = product
                last[slot, row, cut, :] = (
                    2.0 * centre - last[slot, row, cut, :] + here * here * total
                )
            else:
                g[slot, row, cut, :] = 2.0 * here * product

        sweep(sizes, chain, mixed, finish)
        if more:
            rows = sizes.rows
            along = cells_ref[0, 0] - level * (4 * rows) - core * rows
            col = cells_ref[0, 1] - half * (sizes.half - EXTRA)
            pulse = wavelet_ref[0, start_ref[0] + step_no]
            for slot in range(2):
                row = along - slot * 2 * rows

                @pl.when((row >= 0) & (row < rows) & (col >= 0) & (col < sizes.wide))
                def _():
                    depth_ids = lax.broadcasted_iota(jnp.int32, (1, sizes.depth), 1)
                    at = (slot, row, pl.ds(col, 1), slice(None))
                    last[at] = last[at] + jnp.where(depth_ids == cells_ref[0, 2], pulse, 0.0)

            copies.start(last.at[core], z_out)
            copies.start(last, next_out)
            copies.start(g, g_out)
        else:
            copies.start(g.at[1 - half, :, sizes.own(half), :], sent_out)
            copies.start(
                g.at[half, :, sizes.own(half), :], g_out.at[:, sizes.final(half), :]
            )
        copies.wait()

    operands = (current, other, beside, speed, later)
    if adds:
        operands += (gradient,)
    if more:
        operands += before if split else (before,)
    specs = [ANY] * len(operands)
    if more:
        operands += source
        specs += [SMEM] * 3
        outs = [sizes.pair, sizes.block, sizes.pair]
    else:
        outs = [(sizes.rows, sizes.cols, sizes.depth), sizes.sent]
    return run(
        body,
        f"forward_{step_no}",
        operands,
        specs,
        outs,
        [sizes.chain] + [sizes.pair] * 5,
    )


def fill(sizes, whole, received, name):
    shape = whole.shape

    def body(*refs):
        in_refs, out, sems = refs[: len(received)], refs[-2], refs[-1]
        _, half, _ = place()
        copies = Copies(sems)
        for index, ref in enumerate(in_refs):
            target = out.at[index, 0] if len(shape) == 5 else out
            copies.start(ref, target.at[:, sizes.final(1 - half), :])
        copies.wait()

    return run(
        body,
        name,
        (*received, whole),
        [ANY] * (len(received) + 1),
        [shape],
        [],
        {len(received): 0},
        flops=0,
    )[0]


def on_device(
    wave_state, adjoint_state, velocity, wavelet, traces, source_cells, receiver_cells, start_step
):
    count = lax.axis_size("gx")
    sizes = Sizes(*velocity.shape)
    across = [(i, i ^ 2) for i in range(count)]
    cores = [(i, i ^ 1) for i in range(count)]
    levels = []
    for level in range(count // 4 - 1):
        for half in range(2):
            low, high = 4 * level + 2 * half + 1, 4 * level + 4 + 2 * half
            levels += [(low, high), (high, low)]
    _, half, _ = place()
    start = start_step[0]
    recent = lax.dynamic_slice_in_dim(traces, start + 1, STEPS, 1)
    samples = lax.all_gather(recent, "gx", axis=2, tiled=True)

    def over(field):
        return lax.ppermute(field, "gx", across)

    def theirs(field):
        first = (1 - half) * (sizes.half - EXTRA)
        return over(lax.dynamic_slice_in_dim(field, first, sizes.wide, 1))

    def exchange(mine, edge):
        return lax.ppermute(mine, "gx", cores), lax.ppermute(edge, "gx", levels)

    velocity_in = theirs(velocity)
    later_in = theirs(adjoint_state[0, 0])
    latest_in = theirs(adjoint_state[1, 0])
    current_in = theirs(wave_state[1, 0])
    before_in = theirs(wave_state[0, 0])

    speed, later4, scaled, edge = adjoint_begin(
        sizes, velocity, velocity_in, adjoint_state, later_in
    )
    adjoint = functools.partial(adjoint_step, sizes)
    common = (speed, receiver_cells, samples)
    later3, scaled, edge = adjoint(
        4, scaled, *exchange(scaled, edge), later4, (adjoint_state, latest_in), *common, None
    )
    later2, scaled, edge = adjoint(
        3, scaled, *exchange(scaled, edge), later3, later4, *common, None
    )
    later1, scaled, edge, whole, sent1 = adjoint(
        2, scaled, *exchange(scaled, edge), later2, later3, *common, None
    )
    got1 = over(sent1)
    whole, sent0 = adjoint(
        1, scaled, *exchange(scaled, edge), later1, later2, *common, whole
    )
    got0 = over(sent0)

    forward = functools.partial(forward_step, sizes)
    source = (source_cells, wavelet, start_step)
    current1, edge = forward_begin(sizes, wave_state, current_in)
    current2, edge, gradient = forward(
        1, current1, *exchange(current1, edge), (wave_state, before_in), speed, later1, None, source
    )
    current3, edge, gradient = forward(
        2, current2, *exchange(current2, edge), current1, speed, later2, gradient, source
    )
    current4, edge, gradient = forward(
        3, current3, *exchange(current3, edge), current2, speed, later3, gradient, source
    )
    gradient, sent = forward(
        4, current4, *exchange(current4, edge), None, speed, later4, gradient, None
    )
    got = over(sent)
    return fill(sizes, gradient, [got], "fill_gradient"), fill(
        sizes, whole, [got0, got1], "fill_adjoint"
    )


def solution(mesh):
    in_specs = (
        P(None, "groups", "gx", None, None),
        P(None, "groups", "gx", None, None),
        P("gx", "groups", None),
        P("groups", None),
        P("groups", None, "gx"),
        P("groups", None),
        P("groups", None, None),
        P("groups"),
    )
    out_specs = (P("gx", "groups", None), P(None, "groups", "gx", None, None))
    return jax.shard_map(
        on_device, mesh=mesh, in_specs=in_specs, out_specs=out_specs, check_vma=False
    )
```

time: 320 us -> 222 us (0.69)
  other arithmetic: 90.6 us -> 0 us
  matrix products: 57.2 us -> 0 us
  Pallas kernels: 0 us -> 54.6 us
  waiting for transfers between devices: 56.5 us -> 98.3 us
  blocking collectives: 58.6 us -> 25.8 us
  starting transfers between devices: 46.7 us -> 32.9 us
    dot_general x4 -> x0, matrix products: 57.2 us -> none  [inject(): jnp.einsum('skp,skz->spz', plane, depth_hit, precision=lax.Precision.HIGH...]
    add x4 -> x0, other arithmetic: 56.7 us -> none  [the longest x3 39.3 us: inject(): return field + added.reshape(shots_count, rows, cols, depth)]
    pallas_call x0 -> x12, Pallas kernels: none -> 54.6 us  [run(): pl.pallas_call(body, name=name, out_shape=[jax.ShapeDtypeStruct(shape, F3...]
    ppermute x16 -> x24, waiting for transfers between devices: 56.5 us -> 98.3 us  [the longest x8 52.7 us: over(): return lax.ppermute(field, 'gx', across)]
    all_gather x1, blocking collectives: 58.6 us -> 25.8 us  [on_device(): samples = lax.all_gather(recent, 'gx', axis=2, tiled=True)]
    concatenate x8 -> x0, other arithmetic: 23.1 us -> none  [padded(): jnp.concatenate([lax.ppermute(tail, axis, [(i, (i + 1) % count) for i in...]
    ppermute x16 -> x24, starting transfers between devices: 46.7 us -> 32.9 us  [the longest x16 26.8 us: exchange(): return (lax.ppermute(mine, 'gx', cores), lax.ppermute(edge, 'gx', levels))]
    select_n x3 -> x0, other arithmetic: 3.86 us -> none  [inject(): jnp.where(cell_z[:, :, None] == depth_ids, values[:, :, None], jnp.zeros_...]
  transfers between devices with their start and end apart: 16 -> 24, of which waited for: 6 -> 11; matrix products, arithmetic and copies ran while one was open for 40% -> 1% of each run, Pallas kernels for 0% -> 15%
where the time goes in v1:
time: 222 us; the launch traced here: 221 us
  waiting for transfers between devices  98.3 us (44%)
  Pallas kernels  54.6 us (25%)
  starting transfers between devices  32.9 us (15%)
  blocking collectives  25.8 us (12%)
  local copies, waits for them, and re-layouts  7.72 us (3%)
    pallas_call x12, Pallas kernels, run(): pl.pallas_call(body, name=name, out_shape=[jax.ShapeDtypeStruct(shape, F3...  54.6 us
    ppermute x8, waiting for transfers between devices, over(): return lax.ppermute(field, 'gx', across)  52.7 us
    ppermute x16, waiting for transfers between devices, exchange(): return (lax.ppermute(mine, 'gx', cores), lax.ppermute(edge, 'gx', levels))  45.6 us
    ppermute x16, starting transfers between devices, exchange(): return (lax.ppermute(mine, 'gx', cores), lax.ppermute(edge, 'gx', levels))  26.8 us
    all_gather x1, blocking collectives, on_device(): samples = lax.all_gather(recent, 'gx', axis=2, tiled=True)  25.8 us
    ppermute x8, starting transfers between devices, over(): return lax.ppermute(field, 'gx', across)  6.09 us
  transfers between devices with their start and end apart: 24, of which 11 were waited for; matrix products, arithmetic and copies ran while one was open for 1% of the time, Pallas kernels for 15%

profile of v1, /device:TPU:11, one launch (start us, length us, event | category | flops | bytes accessed | tf_op | source)
XLA Modules:
  0.0 221.1 jit_solution(9030903884249659277)
XLA Ops:
  0.7 3.1 %fusion.1 = (f32[1,1,4,320,256]{4,3,2,1,0:T(8,128)}, f32[1,1,4,320,256]{4,3,2,1,0:T(8,128)S(1)}) fusion(f32[2,1,4,320,256]{4,3,2,1,0:T(8,128)} %refs_7_.4), kind=kLoop, calls=%fused_computation.7 | loop fusion | bytes 5242880 | tf_op jit(solution)/shard_map/slice | solution.py:449
  5.5 15.4 %collective-permute-done.4.ain_ref = f32[4,176,256]{2,1,0:T(8,128)S(1)} collective-permute-done((f32[4,176,256]{2,1,0:T(8,128)S(1)}, f32[4,176,256]{2,1,0:T(8,128)S(1)}, u32[]{:S(2)}, u32[]{:S(2)}) %collective-permute-start.4) | collective-permute-done | bytes 720928 | tf_op jit(solution)/shard_map/ppermute | solution.py:438
  21.0 15.4 %collective-permute-done.3.vin_ref = f32[4,176,256]{2,1,0:T(8,128)S(1)} collective-permute-done((f32[4,176,256]{2,1,0:T(8,128)S(1)}, f32[4,176,256]{2,1,0:T(8,128)S(1)}, u32[]{:S(2)}, u32[]{:S(2)}) %collective-permute-start.3) | collective-permute-done | bytes 720928 | tf_op jit(solution)/shard_map/ppermute | solution.py:438
  37.7 2.6 %adjoint_begin.1 = (f32[2,4,176,256]{3,2,1,0:T(8,128)S(1)}, f32[2,4,176,256]{3,2,1,0:T(8,128)S(1)}, f32[2,4,176,256]{3,2,1,0:T(8,128)}, f32[4,176,256]{2,1,0:T(8,128)}) custom-call(f32[4,320,256]{2,1,0:T(8,128)S(1)} %copy-done.6, f32[4,176,256]{2,1,0:T(8,128)S(1)} %collective-permute-done.3.vin_ref, f32[2,1,4,320,256]{4,3,2,1,0:T(8,128)S(1)} %copy-done.2, ...), custom_call_target="tpu_custom_call" | custom-call | flops 400000000 | bytes 8000000 | tf_op jit(solution)/shard_map/adjoint_begin/pallas_call | solution.py:147
  44.1 3.4 %collective-permute-start.6 = (f32[4,176,256]{2,1,0:T(8,128)}, f32[4,176,256]{2,1,0:T(8,128)}, u32[]{:S(2)}, u32[]{:S(2)}) collective-permute-start(f32[4,176,256]{2,1,0:T(8,128)} %get-tuple-element.36), channel_id=1, source_target_pairs={{1,4},{4,1},{3,6},{6,3},{5,8},{8,5},{7,10},{10,7},{9,12},{12,9},{1... | collective-permute-start | bytes 2162696 | tf_op jit(solution)/shard_map/ppermute | solution.py:445
  48.3 25.8 %all_gather.3 = f32[1,4,256]{1,0,2:T(1,128)S(1)} all-gather(f32[1,4,16]{1,0,2:T(1,128)S(1)} %constant_dynamic-slice_fusion), channel_id=1, replica_groups=mesh['groups'=2,'gx'=16] {'gx'}, dimensions={2}, use_global_device_ids=true | all-gather | bytes 4352 | tf_op jit(solution)/shard_map/all_gather | solution.py:435
  75.9 6.1 %adjoint_4.1 = (f32[2,4,176,256]{3,2,1,0:T(8,128)S(1)}, f32[2,4,176,256]{3,2,1,0:T(8,128)S(1)}, f32[4,176,256]{2,1,0:T(8,128)S(1)}) custom-call(f32[2,4,176,256]{3,2,1,0:T(8,128)} %get-tuple-element.35.refs_0_, f32[2,4,176,256]{3,2,1,0:T(8,128)} %collective-permute-done.5.refs_1_, f32[4,176,256]{2,1,0:T(8,128)} %collective-permute-done.6.refs_2_, ...), custom_call_target="tpu_custom_call" | custom-call | flops 400000000 | bytes 8000000 | tf_op jit(solution)/shard_map/adjoint_4/pallas_call | solution.py:147
  84.5 10.8 %collective-permute-done.9.refs_2_ = f32[4,176,256]{2,1,0:T(8,128)S(1)} collective-permute-done((f32[4,176,256]{2,1,0:T(8,128)S(1)}, f32[4,176,256]{2,1,0:T(8,128)S(1)}, u32[]{:S(2)}, u32[]{:S(2)}) %collective-permute-start.9) | collective-permute-done | bytes 720928 | tf_op jit(solution)/shard_map/ppermute | solution.py:445
  95.3 6.0 %adjoint_3.1 = (f32[2,4,176,256]{3,2,1,0:T(8,128)S(1)}, f32[2,4,176,256]{3,2,1,0:T(8,128)S(1)}, f32[4,176,256]{2,1,0:T(8,128)S(1)}) custom-call(f32[2,4,176,256]{3,2,1,0:T(8,128)S(1)} %get-tuple-element.38.refs_0_, f32[2,4,176,256]{3,2,1,0:T(8,128)S(1)} %collective-permute-done.8.refs_1_, f32[4,176,256]{2,1,0:T(8,128)S(1)} %collective-permute-done.9.refs_2_, ...), custom_call_target="tpu_custom_call" | custom-call | flops 400000000 | bytes 8000000 | tf_op jit(solution)/shard_map/adjoint_3/pallas_call | solution.py:147
  104.3 2.6 %collective-permute-start.11 = (f32[4,176,256]{2,1,0:T(8,128)S(1)}, f32[4,176,256]{2,1,0:T(8,128)S(1)}, u32[]{:S(2)}, u32[]{:S(2)}) collective-permute-start(f32[4,176,256]{2,1,0:T(8,128)S(1)} %get-tuple-element.42), channel_id=1, source_target_pairs={{1,4},{4,1},{3,6},{6,3},{5,8},{8,5},{7,10},{10,7},{9,12},{12,9},{1... | collective-permute-start | bytes 2162696 | tf_op jit(solution)/shard_map/ppermute | solution.py:445
  110.2 6.9 %collective-permute-done.11.refs_2_ = f32[4,176,256]{2,1,0:T(8,128)S(1)} collective-permute-done((f32[4,176,256]{2,1,0:T(8,128)S(1)}, f32[4,176,256]{2,1,0:T(8,128)S(1)}, u32[]{:S(2)}, u32[]{:S(2)}) %collective-permute-start.11) | collective-permute-done | bytes 720928 | tf_op jit(solution)/shard_map/ppermute | solution.py:445
  117.2 6.9 %adjoint_2.1 = (f32[2,4,176,256]{3,2,1,0:T(8,128)S(1)}, f32[2,4,176,256]{3,2,1,0:T(8,128)S(1)}, f32[4,176,256]{2,1,0:T(8,128)S(1)}, f32[2,1,4,320,256]{4,3,2,1,0:T(8,128)}, f32[4,160,256]{2,1,0:T(8,128)S(1)}) custom-call(f32[2,4,176,256]{3,2,1,0:T(8,128)S(1)} %get-tuple-element.41.refs_0_, f32[2,4,176,256]{3,2,1,0:T(8,128)S(1)} %collective-permute-done.10.refs_1_, ...), custom_call_target="tpu_custom_call" | custom-call | flops 400000000 | bytes 8000000 | tf_op jit(solution)/shard_map/adjoint_2/pallas_call | solution.py:147
  124.9 6.1 %forward_1.1 = (f32[2,4,176,256]{3,2,1,0:T(8,128)S(1)}, f32[4,176,256]{2,1,0:T(8,128)S(1)}, f32[2,4,176,256]{3,2,1,0:T(8,128)S(1)}) custom-call(f32[2,4,176,256]{3,2,1,0:T(8,128)S(1)} %get-tuple-element.32.refs_0_.refs_6_, f32[2,4,176,256]{3,2,1,0:T(8,128)S(1)} %collective-permute-done.1.refs_1_, f32[4,176,256]{2,1,0:T(8,128)S(1)} %collective-permute-done.2.refs_2_, ...), custom_call_target="tpu_custom_call" | custom-call | flops 400000000 | bytes 8000000 | tf_op jit(solution)/shard_map/forward_1/pallas_call | solution.py:147
  133.8 10.5 %collective-permute-done.14.refs_2_ = f32[4,176,256]{2,1,0:T(8,128)S(1)} collective-permute-done((f32[4,176,256]{2,1,0:T(8,128)S(1)}, f32[4,176,256]{2,1,0:T(8,128)S(1)}, u32[]{:S(2)}, u32[]{:S(2)}) %collective-permute-start.14) | collective-permute-done | bytes 720928 | tf_op jit(solution)/shard_map/ppermute | solution.py:445
  144.3 6.2 %forward_2.1 = (f32[2,4,176,256]{3,2,1,0:T(8,128)S(1)}, f32[4,176,256]{2,1,0:T(8,128)S(1)}, f32[2,4,176,256]{3,2,1,0:T(8,128)S(1)}) custom-call(f32[2,4,176,256]{3,2,1,0:T(8,128)S(1)} %get-tuple-element.45.refs_0_.refs_6_, f32[2,4,176,256]{3,2,1,0:T(8,128)S(1)} %collective-permute-done.13.refs_1_, f32[4,176,256]{2,1,0:T(8,128)S(1)} %collective-permute-done.14.refs_2_, ...), custom_call_target="tpu_custom_call" | custom-call | flops 400000000 | bytes 8000000 | tf_op jit(solution)/shard_map/forward_2/pallas_call | solution.py:147
  150.6 2.5 %collective-permute-start.16 = (f32[4,176,256]{2,1,0:T(8,128)S(1)}, f32[4,176,256]{2,1,0:T(8,128)S(1)}, u32[]{:S(2)}, u32[]{:S(2)}) collective-permute-start(f32[4,176,256]{2,1,0:T(8,128)S(1)} %get-tuple-element.49), channel_id=1, source_target_pairs={{1,4},{4,1},{3,6},{6,3},{5,8},{8,5},{7,10},{10,7},{9,12},{12,9},{1... | collective-permute-start | bytes 2162696 | tf_op jit(solution)/shard_map/ppermute | solution.py:445
  154.4 8.8 %collective-permute-done.16.refs_2_ = f32[4,176,256]{2,1,0:T(8,128)S(1)} collective-permute-done((f32[4,176,256]{2,1,0:T(8,128)S(1)}, f32[4,176,256]{2,1,0:T(8,128)S(1)}, u32[]{:S(2)}, u32[]{:S(2)}) %collective-permute-start.16) | collective-permute-done | bytes 720928 | tf_op jit(solution)/shard_map/ppermute | solution.py:445
  163.3 6.2 %forward_3.1 = (f32[2,4,176,256]{3,2,1,0:T(8,128)S(1)}, f32[4,176,256]{2,1,0:T(8,128)S(1)}, f32[2,4,176,256]{3,2,1,0:T(8,128)S(1)}) custom-call(f32[2,4,176,256]{3,2,1,0:T(8,128)S(1)} %get-tuple-element.48.refs_0_, f32[2,4,176,256]{3,2,1,0:T(8,128)S(1)} %collective-permute-done.15.refs_1_, f32[4,176,256]{2,1,0:T(8,128)S(1)} %collective-permute-done.16.refs_2_, ...), custom_call_target="tpu_custom_call" | custom-call | flops 400000000 | bytes 8000000 | tf_op jit(solution)/shard_map/forward_3/pallas_call | solution.py:147
  172.1 3.5 %collective-permute-start.18 = (f32[4,176,256]{2,1,0:T(8,128)S(1)}, f32[4,176,256]{2,1,0:T(8,128)S(1)}, u32[]{:S(2)}, u32[]{:S(2)}) collective-permute-start(f32[4,176,256]{2,1,0:T(8,128)S(1)} %get-tuple-element.52), channel_id=1, source_target_pairs={{1,4},{4,1},{3,6},{6,3},{5,8},{8,5},{7,10},{10,7},{9,12},{12,9},{1... | collective-permute-start | bytes 2162696 | tf_op jit(solution)/shard_map/ppermute | solution.py:445
  176.3 6.5 %collective-permute-done.21.refs_2_ = f32[4,176,256]{2,1,0:T(8,128)S(1)} collective-permute-done((f32[4,176,256]{2,1,0:T(8,128)S(1)}, f32[4,176,256]{2,1,0:T(8,128)S(1)}, u32[]{:S(2)}, u32[]{:S(2)}) %collective-permute-start.21) | collective-permute-done | bytes 720928 | tf_op jit(solution)/shard_map/ppermute | solution.py:445
  182.9 5.7 %adjoint_1.1 = (f32[2,1,4,320,256]{4,3,2,1,0:T(8,128)}, f32[4,160,256]{2,1,0:T(8,128)S(1)}) custom-call(f32[2,4,176,256]{3,2,1,0:T(8,128)S(1)} %get-tuple-element.56.refs_0_, f32[2,4,176,256]{3,2,1,0:T(8,128)S(1)} %collective-permute-done.20.refs_1_, f32[4,176,256]{2,1,0:T(8,128)S(1)} %collective-permute-done.21.refs_2_, ...), custom_call_target="tpu_custom_call", output_to_operand_aliasing={{0}: (8, {})} | custom-call | flops 400000000 | bytes 8000000 | tf_op jit(solution)/shard_map/adjoint_1/pallas_call | solution.py:147
  190.6 5.4 %forward_4.1 = (f32[4,320,256]{2,1,0:T(8,128)}, f32[4,160,256]{2,1,0:T(8,128)S(1)}) custom-call(f32[2,4,176,256]{3,2,1,0:T(8,128)S(1)} %get-tuple-element.51.refs_0_, f32[2,4,176,256]{3,2,1,0:T(8,128)S(1)} %collective-permute-done.17.refs_1_, f32[4,176,256]{2,1,0:T(8,128)S(1)} %collective-permute-done.18.refs_2_, ...), custom_call_target="tpu_custom_call" | custom-call | flops 400000000 | bytes 8000000 | tf_op jit(solution)/shard_map/forward_4/pallas_call | solution.py:147
  196.8 9.1 %collective-permute-done.22.refs_0_ = f32[4,160,256]{2,1,0:T(8,128)S(1)} collective-permute-done((f32[4,160,256]{2,1,0:T(8,128)S(1)}, f32[4,160,256]{2,1,0:T(8,128)S(1)}, u32[]{:S(2)}, u32[]{:S(2)}) %collective-permute-start.22) | collective-permute-done | bytes 655392 | tf_op jit(solution)/shard_map/ppermute | solution.py:438
  207.1 12.8 %collective-permute-done.19.refs_0_ = f32[4,160,256]{2,1,0:T(8,128)S(1)} collective-permute-done((f32[4,160,256]{2,1,0:T(8,128)S(1)}, f32[4,160,256]{2,1,0:T(8,128)S(1)}, u32[]{:S(2)}, u32[]{:S(2)}) %collective-permute-start.19) | collective-permute-done | bytes 655392 | tf_op jit(solution)/shard_map/ppermute | solution.py:438
  (69 shorter events, 30.9 us)
Async XLA Ops:
  3.9 17.1 %collective-permute-start.4 = (f32[4,176,256]{2,1,0:T(8,128)S(1)}, f32[4,176,256]{2,1,0:T(8,128)S(1)}, u32[]{:S(2)}, u32[]{:S(2)}) collective-permute-start(f32[4,176,256]{2,1,0:T(8,128)S(1)} %dynamic-slice_bitcast_fusion.2), channel_id=1, source_target_pairs={{0,2},{1,3},{2,0},{3,1},{4,6},{5,7},{6,4},{7,5},{8,10},{9,11},{10,... | collective-permute-start | bytes 2162696 | tf_op jit(solution)/shard_map/ppermute | solution.py:438
  5.2 31.2 %collective-permute-start.3 = (f32[4,176,256]{2,1,0:T(8,128)S(1)}, f32[4,176,256]{2,1,0:T(8,128)S(1)}, u32[]{:S(2)}, u32[]{:S(2)}) collective-permute-start(f32[4,176,256]{2,1,0:T(8,128)S(1)} %constant_dynamic-slice_fusion.1), channel_id=1, source_target_pairs={{0,2},{1,3},{2,0},{3,1},{4,6},{5,7},{6,4},{7,5},{8,10},{9,11},{10,... | collective-permute-start | bytes 2162696 | tf_op jit(solution)/shard_map/ppermute | solution.py:438
  40.4 33.8 %collective-permute-start.5 = (f32[2,4,176,256]{3,2,1,0:T(8,128)}, f32[2,4,176,256]{3,2,1,0:T(8,128)}, u32[]{:S(2)}, u32[]{:S(2)}) collective-permute-start(f32[2,4,176,256]{3,2,1,0:T(8,128)} %get-tuple-element.35.refs_0_), channel_id=1, source_target_pairs={{0,1},{1,0},{2,3},{3,2},{4,5},{5,4},{6,7},{7,6},{8,9},{9,8},{10,11... | collective-permute-start | bytes 4325384 | tf_op jit(solution)/shard_map/ppermute | solution.py:445
  42.9 31.2 %collective-permute-start.7 = (f32[4,176,256]{2,1,0:T(8,128)}, f32[4,176,256]{2,1,0:T(8,128)}, u32[]{:S(2)}, u32[]{:S(2)}) collective-permute-start(f32[4,176,256]{2,1,0:T(8,128)} %dynamic-slice_bitcast_fusion.1), channel_id=1, source_target_pairs={{0,2},{1,3},{2,0},{3,1},{4,6},{5,7},{6,4},{7,5},{8,10},{9,11},{10,... | collective-permute-start | bytes 2162696 | tf_op jit(solution)/shard_map/ppermute | solution.py:438
  44.1 30.0 %collective-permute-start.6 = (f32[4,176,256]{2,1,0:T(8,128)}, f32[4,176,256]{2,1,0:T(8,128)}, u32[]{:S(2)}, u32[]{:S(2)}) collective-permute-start(f32[4,176,256]{2,1,0:T(8,128)} %get-tuple-element.36), channel_id=1, source_target_pairs={{1,4},{4,1},{3,6},{6,3},{5,8},{8,5},{7,10},{10,7},{9,12},{12,9},{1... | collective-permute-start | bytes 2162696 | tf_op jit(solution)/shard_map/ppermute | solution.py:445
  82.0 13.3 %collective-permute-start.8 = (f32[2,4,176,256]{3,2,1,0:T(8,128)S(1)}, f32[2,4,176,256]{3,2,1,0:T(8,128)S(1)}, u32[]{:S(2)}, u32[]{:S(2)}) collective-permute-start(f32[2,4,176,256]{3,2,1,0:T(8,128)S(1)} %get-tuple-element.38.refs_0_), channel_id=1, source_target_pairs={{0,1},{1,0},{2,3},{3,2},{4,5},{5,4},{6,7},{7,6},{8,9},{9,8},{10,11... | collective-permute-start | bytes 4325384 | tf_op jit(solution)/shard_map/ppermute | solution.py:445
  82.4 12.9 %collective-permute-start.9 = (f32[4,176,256]{2,1,0:T(8,128)S(1)}, f32[4,176,256]{2,1,0:T(8,128)S(1)}, u32[]{:S(2)}, u32[]{:S(2)}) collective-permute-start(f32[4,176,256]{2,1,0:T(8,128)S(1)} %get-tuple-element.39), channel_id=1, source_target_pairs={{1,4},{4,1},{3,6},{6,3},{5,8},{8,5},{7,10},{10,7},{9,12},{12,9},{1... | collective-permute-start | bytes 2162696 | tf_op jit(solution)/shard_map/ppermute | solution.py:445
  84.4 18.3 %collective-permute-start = (f32[4,176,256]{2,1,0:T(8,128)S(1)}, f32[4,176,256]{2,1,0:T(8,128)S(1)}, u32[]{:S(2)}, u32[]{:S(2)}) collective-permute-start(f32[4,176,256]{2,1,0:T(8,128)S(1)} %dynamic-slice_bitcast_fusion.3), channel_id=1, source_target_pairs={{0,2},{1,3},{2,0},{3,1},{4,6},{5,7},{6,4},{7,5},{8,10},{9,11},{10,... | collective-permute-start | bytes 2162696 | tf_op jit(solution)/shard_map/ppermute | solution.py:438
  101.3 15.8 %collective-permute-start.10 = (f32[2,4,176,256]{3,2,1,0:T(8,128)S(1)}, f32[2,4,176,256]{3,2,1,0:T(8,128)S(1)}, u32[]{:S(2)}, u32[]{:S(2)}) collective-permute-start(f32[2,4,176,256]{3,2,1,0:T(8,128)S(1)} %get-tuple-element.41.refs_0_), channel_id=1, source_target_pairs={{0,1},{1,0},{2,3},{3,2},{4,5},{5,4},{6,7},{7,6},{8,9},{9,8},{10,11... | collective-permute-start | bytes 4325384 | tf_op jit(solution)/shard_map/ppermute | solution.py:445
  103.9 21.0 %collective-permute-start.1 = (f32[2,4,176,256]{3,2,1,0:T(8,128)S(1)}, f32[2,4,176,256]{3,2,1,0:T(8,128)S(1)}, u32[]{:S(2)}, u32[]{:S(2)}) collective-permute-start(f32[2,4,176,256]{3,2,1,0:T(8,128)S(1)} %get-tuple-element.32.refs_0_.refs_6_), channel_id=1, source_target_pairs={{0,1},{1,0},{2,3},{3,2},{4,5},{5,4},{6,7},{7,6},{8,9},{9,8},{10,11... | collective-permute-start | bytes 4325384 | tf_op jit(solution)/shard_map/ppermute | solution.py:445
  104.3 12.9 %collective-permute-start.11 = (f32[4,176,256]{2,1,0:T(8,128)S(1)}, f32[4,176,256]{2,1,0:T(8,128)S(1)}, u32[]{:S(2)}, u32[]{:S(2)}) collective-permute-start(f32[4,176,256]{2,1,0:T(8,128)S(1)} %get-tuple-element.42), channel_id=1, source_target_pairs={{1,4},{4,1},{3,6},{6,3},{5,8},{8,5},{7,10},{10,7},{9,12},{12,9},{1... | collective-permute-start | bytes 2162696 | tf_op jit(solution)/shard_map/ppermute | solution.py:445
  106.9 17.2 %collective-permute-start.12 = (f32[4,176,256]{2,1,0:T(8,128)S(1)}, f32[4,176,256]{2,1,0:T(8,128)S(1)}, u32[]{:S(2)}, u32[]{:S(2)}) collective-permute-start(f32[4,176,256]{2,1,0:T(8,128)S(1)} %dynamic-slice_bitcast_fusion), channel_id=1, source_target_pairs={{0,2},{1,3},{2,0},{3,1},{4,6},{5,7},{6,4},{7,5},{8,10},{9,11},{10,... | collective-permute-start | bytes 2162696 | tf_op jit(solution)/shard_map/ppermute | solution.py:438
  107.7 17.1 %collective-permute-start.2 = (f32[4,176,256]{2,1,0:T(8,128)S(1)}, f32[4,176,256]{2,1,0:T(8,128)S(1)}, u32[]{:S(2)}, u32[]{:S(2)}) collective-permute-start(f32[4,176,256]{2,1,0:T(8,128)S(1)} %get-tuple-element.33), channel_id=1, source_target_pairs={{1,4},{4,1},{3,6},{6,3},{5,8},{8,5},{7,10},{10,7},{9,12},{12,9},{1... | collective-permute-start | bytes 2162696 | tf_op jit(solution)/shard_map/ppermute | solution.py:445
  131.0 13.4 %collective-permute-start.13 = (f32[2,4,176,256]{3,2,1,0:T(8,128)S(1)}, f32[2,4,176,256]{3,2,1,0:T(8,128)S(1)}, u32[]{:S(2)}, u32[]{:S(2)}) collective-permute-start(f32[2,4,176,256]{3,2,1,0:T(8,128)S(1)} %get-tuple-element.45.refs_0_.refs_6_), channel_id=1, source_target_pairs={{0,1},{1,0},{2,3},{3,2},{4,5},{5,4},{6,7},{7,6},{8,9},{9,8},{10,11... | collective-permute-start | bytes 4325384 | tf_op jit(solution)/shard_map/ppermute | solution.py:445
  131.7 12.6 %collective-permute-start.14 = (f32[4,176,256]{2,1,0:T(8,128)S(1)}, f32[4,176,256]{2,1,0:T(8,128)S(1)}, u32[]{:S(2)}, u32[]{:S(2)}) collective-permute-start(f32[4,176,256]{2,1,0:T(8,128)S(1)} %get-tuple-element.46), channel_id=1, source_target_pairs={{1,4},{4,1},{3,6},{6,3},{5,8},{8,5},{7,10},{10,7},{9,12},{12,9},{1... | collective-permute-start | bytes 2162696 | tf_op jit(solution)/shard_map/ppermute | solution.py:445
  150.5 12.8 %collective-permute-start.15 = (f32[2,4,176,256]{3,2,1,0:T(8,128)S(1)}, f32[2,4,176,256]{3,2,1,0:T(8,128)S(1)}, u32[]{:S(2)}, u32[]{:S(2)}) collective-permute-start(f32[2,4,176,256]{3,2,1,0:T(8,128)S(1)} %get-tuple-element.48.refs_0_), channel_id=1, source_target_pairs={{0,1},{1,0},{2,3},{3,2},{4,5},{5,4},{6,7},{7,6},{8,9},{9,8},{10,11... | collective-permute-start | bytes 4325384 | tf_op jit(solution)/shard_map/ppermute | solution.py:445
  150.6 12.7 %collective-permute-start.16 = (f32[4,176,256]{2,1,0:T(8,128)S(1)}, f32[4,176,256]{2,1,0:T(8,128)S(1)}, u32[]{:S(2)}, u32[]{:S(2)}) collective-permute-start(f32[4,176,256]{2,1,0:T(8,128)S(1)} %get-tuple-element.49), channel_id=1, source_target_pairs={{1,4},{4,1},{3,6},{6,3},{5,8},{8,5},{7,10},{10,7},{9,12},{12,9},{1... | collective-permute-start | bytes 2162696 | tf_op jit(solution)/shard_map/ppermute | solution.py:445
  153.2 29.7 %collective-permute-start.20 = (f32[2,4,176,256]{3,2,1,0:T(8,128)S(1)}, f32[2,4,176,256]{3,2,1,0:T(8,128)S(1)}, u32[]{:S(2)}, u32[]{:S(2)}) collective-permute-start(f32[2,4,176,256]{3,2,1,0:T(8,128)S(1)} %get-tuple-element.56.refs_0_), channel_id=1, source_target_pairs={{0,1},{1,0},{2,3},{3,2},{4,5},{5,4},{6,7},{7,6},{8,9},{9,8},{10,11... | collective-permute-start | bytes 4325384 | tf_op jit(solution)/shard_map/ppermute | solution.py:445
  169.5 21.1 %collective-permute-start.17 = (f32[2,4,176,256]{3,2,1,0:T(8,128)S(1)}, f32[2,4,176,256]{3,2,1,0:T(8,128)S(1)}, u32[]{:S(2)}, u32[]{:S(2)}) collective-permute-start(f32[2,4,176,256]{3,2,1,0:T(8,128)S(1)} %get-tuple-element.51.refs_0_), channel_id=1, source_target_pairs={{0,1},{1,0},{2,3},{3,2},{4,5},{5,4},{6,7},{7,6},{8,9},{9,8},{10,11... | collective-permute-start | bytes 4325384 | tf_op jit(solution)/shard_map/ppermute | solution.py:445
  170.0 12.9 %collective-permute-start.21 = (f32[4,176,256]{2,1,0:T(8,128)S(1)}, f32[4,176,256]{2,1,0:T(8,128)S(1)}, u32[]{:S(2)}, u32[]{:S(2)}) collective-permute-start(f32[4,176,256]{2,1,0:T(8,128)S(1)} %get-tuple-element.57), channel_id=1, source_target_pairs={{1,4},{4,1},{3,6},{6,3},{5,8},{8,5},{7,10},{10,7},{9,12},{12,9},{1... | collective-permute-start | bytes 2162696 | tf_op jit(solution)/shard_map/ppermute | solution.py:445
  172.1 18.5 %collective-permute-start.18 = (f32[4,176,256]{2,1,0:T(8,128)S(1)}, f32[4,176,256]{2,1,0:T(8,128)S(1)}, u32[]{:S(2)}, u32[]{:S(2)}) collective-permute-start(f32[4,176,256]{2,1,0:T(8,128)S(1)} %get-tuple-element.52), channel_id=1, source_target_pairs={{1,4},{4,1},{3,6},{6,3},{5,8},{8,5},{7,10},{10,7},{9,12},{12,9},{1... | collective-permute-start | bytes 2162696 | tf_op jit(solution)/shard_map/ppermute | solution.py:445
  175.5 21.2 %collective-permute-start.23 = (f32[4,160,256]{2,1,0:T(8,128)S(1)}, f32[4,160,256]{2,1,0:T(8,128)S(1)}, u32[]{:S(2)}, u32[]{:S(2)}) collective-permute-start(f32[4,160,256]{2,1,0:T(8,128)S(1)} %get-tuple-element.60), channel_id=1, source_target_pairs={{0,2},{1,3},{2,0},{3,1},{4,6},{5,7},{6,4},{7,5},{8,10},{9,11},{10,... | collective-permute-start | bytes 1966088 | tf_op jit(solution)/shard_map/ppermute | solution.py:438
  188.6 17.3 %collective-permute-start.22 = (f32[4,160,256]{2,1,0:T(8,128)S(1)}, f32[4,160,256]{2,1,0:T(8,128)S(1)}, u32[]{:S(2)}, u32[]{:S(2)}) collective-permute-start(f32[4,160,256]{2,1,0:T(8,128)S(1)} %get-tuple-element.59), channel_id=1, source_target_pairs={{0,2},{1,3},{2,0},{3,1},{4,6},{5,7},{6,4},{7,5},{8,10},{9,11},{10,... | collective-permute-start | bytes 1966088 | tf_op jit(solution)/shard_map/ppermute | solution.py:438
  196.0 23.9 %collective-permute-start.19 = (f32[4,160,256]{2,1,0:T(8,128)S(1)}, f32[4,160,256]{2,1,0:T(8,128)S(1)}, u32[]{:S(2)}, u32[]{:S(2)}) collective-permute-start(f32[4,160,256]{2,1,0:T(8,128)S(1)} %get-tuple-element.54), channel_id=1, source_target_pairs={{0,2},{1,3},{2,0},{3,1},{4,6},{5,7},{6,4},{7,5},{8,10},{9,11},{10,... | collective-permute-start | bytes 1966088 | tf_op jit(solution)/shard_map/ppermute | solution.py:438
  (11 other events, 148.6 us)

commit v2 on v0

v2 whole, which is shorter than its diff:
```python
import functools

import jax
import jax.numpy as jnp
from jax import lax
from jax.experimental import pallas as pl
from jax.experimental.pallas import tpu as pltpu
from jax.sharding import PartitionSpec as P

STEPS = 4
WEIGHTS = (-205.0 / 72.0, 8.0 / 5.0, -1.0 / 5.0, 8.0 / 315.0, -1.0 / 560.0)
UNIT = WEIGHTS[1]
REACH = 4
EXTRA = REACH * STEPS
F32 = jnp.float32
BF16 = jnp.bfloat16
ANY = pl.BlockSpec(memory_space=pl.ANY)
VMEM = pl.BlockSpec(memory_space=pltpu.VMEM)
SMEM = pl.BlockSpec(memory_space=pltpu.SMEM)
MIB = 2**20
PACK_LIMIT = 56


def place():
    position = lax.axis_index("gx")
    return position // 4, (position % 4) // 2, position % 2


def banded(apart):
    band = jnp.zeros(apart.shape, F32)
    for offset in range(1, REACH + 1):
        band = jnp.where(jnp.abs(apart) == offset, WEIGHTS[offset] / UNIT, band)
    return band.astype(BF16)


def iota(shape, axis):
    return lax.broadcasted_iota(jnp.int32, shape, axis)


def two_terms(value):
    high = value.astype(BF16)
    return high, (value - high.astype(F32)).astype(BF16)


def dot(left, right, contract=((1,), (0,))):
    return lax.dot_general(left, right, (contract, ((), ())), preferred_element_type=F32)


class Copies:
    def __init__(self, sems):
        self.sems, self.going = sems, []

    def start(self, source, target):
        copy = pltpu.make_async_copy(source, target, self.sems.at[len(self.going)])
        copy.start()
        self.going.append(copy)

    def wait(self):
        for copy in self.going:
            copy.wait()


class Sizes:
    def __init__(self, rows, cols, depth):
        self.rows, self.cols, self.depth = rows, cols, depth
        self.half = cols // 2
        self.wide = self.half + EXTRA
        self.pair = (2, rows, self.wide, depth)
        self.block = (rows, self.wide, depth)
        self.moved = (rows * self.wide + 8, depth)
        self.moved_first = (rows * self.wide + 16, depth)
        self.sent = (rows, self.half, depth)
        self.whole = (rows, cols, depth)

    def window(self, half):
        return pl.ds(pl.multiple_of(half * (self.half - EXTRA), 16), self.wide)

    def own(self, half):
        return pl.ds(pl.multiple_of(half * EXTRA, 16), self.half)

    def final(self, half):
        return pl.ds(pl.multiple_of(half * self.half, 16), self.half)

    def moved_row(self, row):
        return pl.ds(row * self.wide, self.wide)

    @property
    def moved_tail(self):
        return pl.ds(self.rows * self.wide, 16)


def over_columns(sizes, body):
    @pl.loop(0, sizes.wide // 16)
    def _(step):
        for part in range(2):
            body(pl.multiple_of(step * 16 + part * 8, 8))


def cut(first):
    return pl.ds(first, 8)


def merged(sizes, own, moved, slot, row, first):
    _, half, _ = place()
    received = moved[pl.ds(pl.multiple_of(first + row * sizes.wide, 8), 8), :]
    return jnp.where(half == slot, own[row, cut(first), :], received)


def differences(sizes, blocks, mixed, added=None):
    wide, depth = sizes.wide, sizes.depth
    shape = (wide, 2 * wide)
    column = iota(shape, 1)
    column = jnp.where(column >= wide, column - wide, column)
    band_y = banded(iota(shape, 0) - column)
    shape = (2 * depth, depth)
    layer = iota(shape, 0)
    layer = jnp.where(layer >= depth, layer - depth, layer)
    band_z = banded(layer - iota(shape, 1))
    for slot in range(2):
        for row in range(sizes.rows):
            terms = two_terms(blocks[slot][row])
            total = dot(jnp.concatenate(terms, 1), band_z)
            total = UNIT * (total + dot(band_y, jnp.concatenate(terms, 0)))
            if added is not None:
                total = total + added(slot, row)
            mixed[slot, row] = total


def sweep(sizes, refs, mixed, finish):
    mine0, mine1, other0, other1, beside = refs
    rows = sizes.rows
    _, _, core = place()
    orders = (
        (beside, mine0, other0, mine1, other1),
        (other0, mine0, other1, mine1, beside),
    )
    for which, order in enumerate(orders):

        @pl.when(core == which)
        def _():
            for slot in range(2):

                def columns(first):
                    near = [
                        block[row, cut(first), :]
                        for block in order[2 * slot : 2 * slot + 3]
                        for row in range(rows)
                    ]
                    for row in range(rows):
                        centre = near[rows + row]
                        parts = [
                            WEIGHTS[offset]
                            * (near[rows + row + offset] + near[rows + row - offset])
                            for offset in range(1, REACH + 1)
                        ]
                        total = (parts[0] + parts[1]) + (parts[2] + parts[3])
                        total = total + (
                            3.0 * WEIGHTS[0] * centre + mixed[slot, row, cut(first), :]
                        )
                        finish(which, slot, row, first, centre, total)

                over_columns(sizes, columns)


def run(body, name, operands, specs, outs, scratch=(), aliases=None, limit=24, sems=0):
    return pl.pallas_call(
        body,
        name=name,
        out_shape=[jax.ShapeDtypeStruct(shape, F32) for shape, _ in outs],
        in_specs=specs,
        out_specs=[spec for _, spec in outs],
        scratch_shapes=[pltpu.VMEM(shape, F32) for shape in scratch]
        + ([pltpu.SemaphoreType.DMA((sems,))] if sems else []),
        input_output_aliases=aliases or {},
        compiler_params=pltpu.CompilerParams(vmem_limit_bytes=limit * MIB),
        cost_estimate=pl.CostEstimate(flops=0, bytes_accessed=0, transcendentals=0),
    )(*operands)


def pack(sizes, velocity, adjoint, wave, traces):
    def body(v_ref, a_ref, w_ref, traces_ref, *rest):
        outs, sems = rest[:5], rest[5]
        _, half, _ = place()
        copies = Copies(sems)
        fields = (v_ref, a_ref.at[0, 0], a_ref.at[1, 0], w_ref.at[1, 0], w_ref.at[0, 0])
        for field, out in zip(fields, outs):
            for row in range(sizes.rows):
                copies.start(
                    field.at[row, sizes.window(1 - half), :], out.at[sizes.moved_row(row)]
                )
        each, steps = traces_ref.shape
        for out in outs[1:]:
            out[sizes.rows * sizes.wide :, :] = jnp.zeros((8, sizes.depth), F32)
        outs[0][sizes.rows * sizes.wide :, :] = jnp.zeros((16, sizes.depth), F32)
        outs[0][pl.ds(sizes.rows * sizes.wide, each), :steps] = traces_ref[...]
        copies.wait()

    return run(
        body,
        "pack",
        (velocity, adjoint, wave, traces),
        [ANY] * 3 + [VMEM],
        [(sizes.moved_first, VMEM)] + [(sizes.moved, VMEM)] * 4,
        limit=PACK_LIMIT,
        sems=20,
    )


def keep(sizes, velocity, adjoint, wave):
    def body(v_ref, a_ref, w_ref, *rest):
        outs, sems = rest[:5], rest[5]
        _, half, _ = place()
        copies = Copies(sems)
        fields = (v_ref, a_ref.at[0, 0], a_ref.at[1, 0], w_ref.at[1, 0], w_ref.at[0, 0])
        for field, out in zip(fields, outs):
            copies.start(field.at[:, sizes.window(half), :], out)
        copies.wait()

    return run(
        body,
        "keep",
        (velocity, adjoint, wave),
        [ANY] * 3,
        [(sizes.block, VMEM)] * 5,
        limit=PACK_LIMIT,
        sems=5,
    )


def speed_begin(sizes, own, moved, sent):
    def body(own_ref, moved_ref, sent_ref, v_out, tail_out):
        _, half, _ = place()
        tail_out[half] = sent_ref[sizes.moved_tail, :]
        tail_out[1 - half] = moved_ref[sizes.moved_tail, :]

        def columns(first):
            for slot in range(2):
                for row in range(sizes.rows):
                    v_out[slot, row, cut(first), :] = merged(
                        sizes, own_ref, moved_ref, slot, row, first
                    )

        over_columns(sizes, columns)

    return run(
        body,
        "speed_begin",
        (own, moved, sent),
        [VMEM] * 3,
        [(sizes.pair, VMEM), ((2, 16, sizes.depth), VMEM)],
    )


def adjoint_begin(sizes, speed, own, moved, settled):
    def body(v_ref, own_ref, moved_ref, _, a_out, u0_out, u1_out, z_out):
        _, _, core = place()

        def columns(first):
            for slot, u_out in enumerate((u0_out, u1_out)):
                for row in range(sizes.rows):
                    value = merged(sizes, own_ref, moved_ref, slot, row, first)
                    a_out[slot, row, cut(first), :] = value
                    here = v_ref[slot, row, cut(first), :]
                    u_out[row, cut(first), :] = here * here * value
            for row in range(sizes.rows):
                z_out[row, cut(first), :] = jnp.where(
                    core == 0, u0_out[row, cut(first), :], u1_out[row, cut(first), :]
                )

        over_columns(sizes, columns)

    return run(
        body,
        "adjoint_begin",
        (speed, own, moved, settled),
        [VMEM] * 3 + [ANY],
        [(sizes.pair, VMEM)] + [(sizes.block, VMEM)] * 3,
    )


def adjoint_step(sizes, step_no, scaled, later, latest, speed, cells, samples, settled=()):
    split = len(latest) == 2
    more = step_no > 1
    ends = step_no <= 2

    def body(*refs):
        refs = list(refs)
        u_refs, (later_ref, v_ref, cells_ref, samples_ref) = refs[:5], refs[5:9]
        latest_refs, refs = refs[9 : 9 + len(latest)], refs[9 + len(latest) + len(settled) :]
        if more:
            (next_out, u0_out, u1_out, z_out), refs = refs[:4], refs[4:]
        if ends:
            (kept_out, sent_out), refs = refs[:2], refs[2:]
        mixed = refs.pop(0)
        if not more:
            next_out = refs.pop(0)
        level, half, core = place()
        where_x, where_y, where_z = (cells_ref[0, axis : axis + 1, :] for axis in range(3))
        count = where_x.shape[1]
        values = jnp.where(
            where_z == iota((sizes.depth, count), 0),
            samples_ref[0, step_no - 1 : step_no, :],
            0.0,
        )
        values = jnp.concatenate(two_terms(values), 1)
        col_ids = iota((sizes.wide, count), 0) + half * (sizes.half - EXTRA)

        def added(slot, row):
            this_row = ((level * 2 + slot) * 2 + core) * sizes.rows + row
            col_of = jnp.where(where_x == this_row, where_y, -1)
            hit = jnp.where(col_of == col_ids, 1.0, 0.0).astype(BF16)
            return dot(jnp.concatenate((hit, hit), 1), values, ((1,), (1,)))

        differences(sizes, u_refs, mixed, added)

        def finish(which, slot, row, first, centre, total):
            at = (slot, row, cut(first), slice(None))
            if split:
                last = merged(sizes, *latest_refs, slot, row, first)
            else:
                last = latest_refs[0][at]
            value = 2.0 * later_ref[at] - last + total
            next_out[at] = value
            if more:
                here = v_ref[at]
                value = here * here * value
                (u0_out, u1_out)[slot][row, cut(first), :] = value
                if which == slot:
                    z_out[row, cut(first), :] = value

        sweep(sizes, u_refs, mixed, finish)
        if ends:
            kept_out[...] = next_out[half, :, sizes.own(half), :]
            sent_out[...] = next_out[1 - half, :, sizes.own(half), :]

    outs = []
    if more:
        outs += [(sizes.pair, VMEM)] + [(sizes.block, VMEM)] * 3
    if ends:
        outs += [(sizes.sent, VMEM)] * 2
    return run(
        body,
        f"adjoint_{step_no}",
        (*scaled, later, speed, cells, samples, *latest, *settled),
        [VMEM] * (9 + len(latest)) + [ANY] * len(settled),
        outs,
        [sizes.pair] * (1 if more else 2),
    )


def forward_begin(sizes, own, moved):
    def body(own_ref, moved_ref, c0_out, c1_out, z_out):
        _, _, core = place()

        def columns(first):
            for row in range(sizes.rows):
                pair = [merged(sizes, own_ref, moved_ref, slot, row, first) for slot in range(2)]
                c0_out[row, cut(first), :] = pair[0]
                c1_out[row, cut(first), :] = pair[1]
                z_out[row, cut(first), :] = jnp.where(core == 0, *pair)

        over_columns(sizes, columns)

    return run(
        body, "forward_begin", (own, moved), [VMEM] * 2, [(sizes.block, VMEM)] * 3
    )


def forward_step(sizes, step_no, current, before, speed, later, gradient, source, settled=()):
    first_step = step_no == 1
    more = step_no < STEPS

    def body(*refs):
        refs = list(refs)
        c_refs, v_ref, refs = refs[:5], refs[5], refs[6:]
        late, refs = refs[: len(later)], refs[len(later) :]
        if not first_step:
            g_ref, refs = refs[0], refs[1:]
        if more:
            before_refs, refs = refs[:2], refs[2:]
            (cells_ref, wavelet_ref, start_ref), refs = refs[:3], refs[3:]
        refs = refs[len(settled) :]
        if more:
            (c0_out, c1_out, z_out, g_out), refs = refs[:4], refs[4:]
        else:
            (kept_out, sent_out), refs = refs[:2], refs[2:]
        mixed = refs.pop(0)
        if not more:
            g_out = refs.pop(0)
        level, half, core = place()
        differences(sizes, c_refs, mixed)

        def finish(which, slot, row, first, centre, total):
            at = (slot, row, cut(first), slice(None))
            if first_step:
                g_out[at] = total
            elif step_no == 2:
                g_out[at] = late[0][at] * g_ref[at] + late[1][at] * total
            elif more:
                g_out[at] = g_ref[at] + late[0][at] * total
            else:
                g_out[at] = 2.0 * v_ref[at] * (g_ref[at] + late[0][at] * total)
            if more:
                if first_step:
                    last = merged(sizes, *before_refs, slot, row, first)
                else:
                    last = before_refs[slot][row, cut(first), :]
                here = v_ref[at]
                value = 2.0 * centre - last + here * here * total
                (c0_out, c1_out)[slot][row, cut(first), :] = value
                if which == slot:
                    z_out[row, cut(first), :] = value

        sweep(sizes, c_refs, mixed, finish)
        if not more:
            kept_out[...] = g_out[half, :, sizes.own(half), :]
            sent_out[...] = g_out[1 - half, :, sizes.own(half), :]
            return
        col = cells_ref[0, 1] - half * (sizes.half - EXTRA)
        pulse = wavelet_ref[0, start_ref[0] + step_no]
        for slot, c_out in enumerate((c0_out, c1_out)):
            row = cells_ref[0, 0] - ((level * 2 + slot) * 2 + core) * sizes.rows
            inside = (row >= 0) & (row < sizes.rows) & (col >= 0) & (col < sizes.wide)

            def put(out):
                at = (row, pl.ds(col, 1), slice(None))
                hit = iota((1, sizes.depth), 1) == cells_ref[0, 2]
                out[at] = out[at] + jnp.where(hit, pulse, 0.0)

            pl.when(inside)(functools.partial(put, c_out))
            pl.when(inside & (core == slot))(functools.partial(put, z_out))

    operands = (*current, speed, *later)
    if not first_step:
        operands += (gradient,)
    if more:
        operands += before
    specs = [VMEM] * len(operands)
    if more:
        operands += source
        specs += [SMEM] * 3
        outs = [(sizes.block, VMEM)] * 3 + [(sizes.pair, VMEM)]
    else:
        outs = [(sizes.sent, VMEM)] * 2
    return run(
        body,
        f"forward_{step_no}",
        (*operands, *settled),
        specs + [ANY] * len(settled),
        outs,
        [sizes.pair] * (1 if more else 2),
    )


def fill(sizes, shape, parts, name):
    def body(*refs):
        out, sems = refs[-2], refs[-1]
        _, half, _ = place()
        copies = Copies(sems)
        for index, ref in enumerate(refs[:-2]):
            target = out.at[index // 2, 0] if len(shape) == 5 else out
            side = half if index % 2 == 0 else 1 - half
            copies.start(ref, target.at[:, sizes.final(side), :])
        copies.wait()

    return run(
        body, name, parts, [ANY] * len(parts), [(shape, ANY)], sems=len(parts)
    )[0]


def on_device(
    wave_state, adjoint_state, velocity, wavelet, traces, source_cells, receiver_cells, start_step
):
    count = lax.axis_size("gx")
    sizes = Sizes(*velocity.shape)
    across = [(i, i ^ 2) for i in range(count)]
    cores = [(i, i ^ 1) for i in range(count)]
    levels = []
    for level in range(count // 4 - 1):
        for half in range(2):
            low, high = 4 * level + 2 * half + 1, 4 * level + 4 + 2 * half
            levels += [(low, high), (high, low)]
    halves = [[i for i in range(count) if (i % 4) // 2 == half] for half in range(2)]

    def over(field):
        return lax.ppermute(field, "gx", across)

    def exchange(block0, block1, edge):
        return (
            block0,
            block1,
            lax.ppermute(block0, "gx", cores),
            lax.ppermute(block1, "gx", cores),
            lax.ppermute(edge, "gx", levels),
        )

    each, steps = traces.shape[2], traces.shape[1]
    sent = pack(sizes, velocity, adjoint_state, wave_state, traces[0].T)
    velocity_in, later_in, latest_in, current_in, before_in = map(over, sent)
    kept = keep(sizes, velocity, adjoint_state, wave_state)

    speed, tails = speed_begin(sizes, kept[0], velocity_in, sent[0])
    tails = lax.all_gather(tails, "gx", axis_index_groups=halves)
    tails = tails[:, :, :each, :steps].reshape(count // 4, 2, 2, each, steps)
    samples = tails.transpose(4, 0, 2, 1, 3).reshape(1, steps, count * each)
    samples = lax.dynamic_slice_in_dim(samples, start_step[0] + 1, STEPS, 1)

    adjoint = functools.partial(adjoint_step, sizes)
    common = (speed, receiver_cells, samples)
    forward = functools.partial(forward_step, sizes)
    source = (source_cells, wavelet, start_step)
    later4, *scaled = adjoint_begin(sizes, speed, kept[1], later_in, samples)
    later3, *scaled = adjoint(4, exchange(*scaled), later4, (kept[2], latest_in), *common)
    current1 = forward_begin(sizes, kept[3], current_in)
    later2, *scaled = adjoint(3, exchange(*scaled), later3, (later4,), *common)
    scaled2 = exchange(*scaled)
    *current2, image = forward(
        1, exchange(*current1), (kept[4], before_in), speed, (), None, source, scaled2[2:]
    )
    later1, *scaled, mine1, sent1 = adjoint(
        2, scaled2, later2, (later3,), *common, tuple(current2[2:])
    )
    got1 = over(sent1)
    *current3, gradient = forward(
        2, exchange(*current2), tuple(current1[:2]), speed, (later1, later2), image, source
    )
    mine0, sent0 = adjoint(
        1, exchange(*scaled), later1, (later2,), *common, tuple(current3[2:])
    )
    got0 = over(sent0)
    *current4, gradient = forward(
        3,
        exchange(*current3),
        tuple(current2[:2]),
        speed,
        (later3,),
        gradient,
        source,
        (mine0, got1),
    )
    mine, sent = forward(4, exchange(*current4), (), speed, (later4,), gradient, None, (got0,))
    got = over(sent)
    return fill(sizes, sizes.whole, [mine, got], "fill_gradient"), fill(
        sizes, adjoint_state.shape, [mine0, got0, mine1, got1], "fill_adjoint"
    )


def solution(mesh):
    in_specs = (
        P(None, "groups", "gx", None, None),
        P(None, "groups", "gx", None, None),
        P("gx", "groups", None),
        P("groups", None),
        P("groups", None, "gx"),
        P("groups", None),
        P("groups", None, None),
        P("groups"),
    )
    out_specs = (P("gx", "groups", None), P(None, "groups", "gx", None, None))
    return jax.shard_map(
        on_device, mesh=mesh, in_specs=in_specs, out_specs=out_specs, check_vma=False
    )
```

time: 320 us -> 182 us (0.57)
  other arithmetic: 90.6 us -> 0 us
  matrix products: 57.2 us -> 0 us
  blocking collectives: 58.6 us -> 17.1 us
  Pallas kernels: 0 us -> 37.4 us
  waiting for transfers between devices: 56.5 us -> 79.5 us
  local copies, waits for them, and re-layouts: 6.12 us -> 1.35 us
    dot_general x4 -> x0, matrix products: 57.2 us -> none  [inject(): jnp.einsum('skp,skz->spz', plane, depth_hit, precision=lax.Precision.HIGH...]
    add x4 -> x0, other arithmetic: 56.7 us -> none  [the longest x3 39.3 us: inject(): return field + added.reshape(shots_count, rows, cols, depth)]
    all_gather x1, blocking collectives: 58.6 us -> 17.1 us  [on_device(): tails = lax.all_gather(tails, 'gx', axis_index_groups=halves)]
    pallas_call x0 -> x15, Pallas kernels: none -> 37.4 us  [run(): pl.pallas_call(body, name=name, out_shape=[jax.ShapeDtypeStruct(shape, F3...]
    concatenate x8 -> x0, other arithmetic: 23.1 us -> none  [padded(): jnp.concatenate([lax.ppermute(tail, axis, [(i, (i + 1) % count) for i in...]
    ppermute x16 -> x32, waiting for transfers between devices: 56.5 us -> 79.5 us  [the longest x8 65.6 us: over(): return lax.ppermute(field, 'gx', across)]
    select_n x3 -> x0, other arithmetic: 3.86 us -> none  [inject(): jnp.where(cell_z[:, :, None] == depth_ids, values[:, :, None], jnp.zeros_...]
    ppermute x16 -> x32, starting transfers between devices: 46.7 us -> 43.8 us  [the longest x8 26.5 us: exchange(): lax.ppermute(edge, 'gx', levels)]
  transfers between devices with their start and end apart: 16 -> 32, of which waited for: 6 -> 10; matrix products, arithmetic and copies ran while one was open for 40% -> 0% of each run, Pallas kernels for 0% -> 13%
where the time goes in v2:
time: 182 us; the launch traced here: 181 us
  waiting for transfers between devices  79.5 us (44%)
  starting transfers between devices  43.8 us (24%)
  Pallas kernels  37.4 us (21%)
  blocking collectives  17.1 us (9%)
  between operations  1.82 us (1%)
    ppermute x8, waiting for transfers between devices, over(): return lax.ppermute(field, 'gx', across)  65.6 us
    pallas_call x15, Pallas kernels, run(): pl.pallas_call(body, name=name, out_shape=[jax.ShapeDtypeStruct(shape, F3...  37.4 us
    ppermute x8, starting transfers between devices, exchange(): lax.ppermute(edge, 'gx', levels)  26.5 us
    all_gather x1, blocking collectives, on_device(): tails = lax.all_gather(tails, 'gx', axis_index_groups=halves)  17.1 us
    ppermute x8, waiting for transfers between devices, exchange(): lax.ppermute(edge, 'gx', levels)  13.9 us
    ppermute x8, starting transfers between devices, over(): return lax.ppermute(field, 'gx', across)  8.15 us
    ppermute x8, starting transfers between devices, exchange(): lax.ppermute(block0, 'gx', cores)  5.41 us
    ppermute x8, starting transfers between devices, exchange(): lax.ppermute(block1, 'gx', cores)  3.83 us
  transfers between devices with their start and end apart: 32, of which 10 were waited for; matrix products, arithmetic and copies ran while one was open for 0% of the time, Pallas kernels for 13%

profile of v2, /device:TPU:11, one launch (start us, length us, event | category | flops | bytes accessed | tf_op | source)
XLA Modules:
  0.0 181.0 jit_solution(11342646361845686794)
XLA Ops:
  0.6 4.8 %pack.1 = (f32[720,256]{1,0:T(8,128)}, f32[712,256]{1,0:T(8,128)}, f32[712,256]{1,0:T(8,128)}, f32[712,256]{1,0:T(8,128)}, f32[712,256]{1,0:T(8,128)}) custom-call(f32[4,320,256]{2,1,0:T(8,128)} %v_ref.3, f32[2,1,4,320,256]{4,3,2,1,0:T(8,128)} %a_ref.3, f32[2,1,4,320,256]{4,3,2,1,0:T(8,128)} %w_ref.3, f32[16,32]{1,0:T(8,128)} %bitcast.13), custom_call_target="tpu_custom_call" | custom-call | tf_op jit(solution)/shard_map/pack/pallas_call | solution.py:166
  8.4 3.8 %keep.1 = (f32[4,176,256]{2,1,0:T(8,128)}, f32[4,176,256]{2,1,0:T(8,128)}, f32[4,176,256]{2,1,0:T(8,128)}, f32[4,176,256]{2,1,0:T(8,128)}, f32[4,176,256]{2,1,0:T(8,128)}) custom-call(f32[4,320,256]{2,1,0:T(8,128)} %v_ref.3, f32[2,1,4,320,256]{4,3,2,1,0:T(8,128)} %a_ref.3, f32[2,1,4,320,256]{4,3,2,1,0:T(8,128)} %w_ref.3), custom_call_target="tpu_custom_call" | custom-call | tf_op jit(solution)/shard_map/keep/pallas_call | solution.py:166
  12.9 10.2 %collective-permute-done.4.moved_ref = f32[720,256]{1,0:T(8,128)S(1)} collective-permute-done((f32[720,256]{1,0:T(8,128)}, f32[720,256]{1,0:T(8,128)S(1)}, u32[]{:S(2)}, u32[]{:S(2)}) %collective-permute-start.4) | collective-permute-done | bytes 737312 | tf_op jit(solution)/shard_map/ppermute | solution.py:486
  24.4 17.1 %all-gather = f32[16,16,256]{2,1,0:T(8,128)S(1)} all-gather(f32[2,16,256]{2,1,0:T(8,128)S(1)} %get-tuple-element.63), channel_id=2, replica_groups={{0,1,4,5,8,9,12,13},{2,3,6,7,10,11,14,15},{16,17,20,21,24,25,28,29},{18..., dimensions={0}, use_global_device_ids=true | all-gather | bytes 294912 | tf_op jit(solution)/shard_map/all_gather | solution.py:503
  43.9 2.8 %collective-permute-start.9 = (f32[4,176,256]{2,1,0:T(8,128)S(1)}, f32[4,176,256]{2,1,0:T(8,128)S(1)}, u32[]{:S(2)}, u32[]{:S(2)}) collective-permute-start(f32[4,176,256]{2,1,0:T(8,128)S(1)} %get-tuple-element.66), channel_id=1, source_target_pairs={{1,4},{4,1},{3,6},{6,3},{5,8},{8,5},{7,10},{10,7},{9,12},{12,9},{1... | collective-permute-start | bytes 2162696 | tf_op jit(solution)/shard_map/ppermute | solution.py:494
  46.7 7.7 %collective-permute-done.10.refs_10_ = f32[712,256]{1,0:T(8,128)} collective-permute-done((f32[712,256]{1,0:T(8,128)}, f32[712,256]{1,0:T(8,128)}, u32[]{:S(2)}, u32[]{:S(2)}) %collective-permute-start.10) | collective-permute-done | bytes 729120 | tf_op jit(solution)/shard_map/ppermute | solution.py:486
  56.9 4.0 %adjoint_4.1 = (f32[2,4,176,256]{3,2,1,0:T(8,128)S(1)}, f32[4,176,256]{2,1,0:T(8,128)S(1)}, f32[4,176,256]{2,1,0:T(8,128)S(1)}, f32[4,176,256]{2,1,0:T(8,128)S(1)}) custom-call(f32[4,176,256]{2,1,0:T(8,128)S(1)} %get-tuple-element.64.refs_0_, f32[4,176,256]{2,1,0:T(8,128)S(1)} %get-tuple-element.65.refs_1_, ...), custom_call_target="tpu_custom_call" | custom-call | tf_op jit(solution)/shard_map/adjoint_4/pallas_call | solution.py:166
  62.8 3.5 %collective-permute-start.13 = (f32[4,176,256]{2,1,0:T(8,128)S(1)}, f32[4,176,256]{2,1,0:T(8,128)S(1)}, u32[]{:S(2)}, u32[]{:S(2)}) collective-permute-start(f32[4,176,256]{2,1,0:T(8,128)S(1)} %get-tuple-element.72), channel_id=1, source_target_pairs={{1,4},{4,1},{3,6},{6,3},{5,8},{8,5},{7,10},{10,7},{9,12},{12,9},{1... | collective-permute-start | bytes 2162696 | tf_op jit(solution)/shard_map/ppermute | solution.py:494
  66.4 3.7 %collective-permute-done.moved_ref = f32[712,256]{1,0:T(8,128)} collective-permute-done((f32[712,256]{1,0:T(8,128)}, f32[712,256]{1,0:T(8,128)}, u32[]{:S(2)}, u32[]{:S(2)}) %collective-permute-start) | collective-permute-done | bytes 729120 | tf_op jit(solution)/shard_map/ppermute | solution.py:486
  74.3 3.5 %collective-permute-start.3 = (f32[4,176,256]{2,1,0:T(8,128)S(1)}, f32[4,176,256]{2,1,0:T(8,128)S(1)}, u32[]{:S(2)}, u32[]{:S(2)}) collective-permute-start(f32[4,176,256]{2,1,0:T(8,128)S(1)} %get-tuple-element.55), channel_id=1, source_target_pairs={{1,4},{4,1},{3,6},{6,3},{5,8},{8,5},{7,10},{10,7},{9,12},{12,9},{1... | collective-permute-start | bytes 2162696 | tf_op jit(solution)/shard_map/ppermute | solution.py:494
  80.7 4.8 %collective-permute-done.5.refs_7_ = f32[712,256]{1,0:T(8,128)S(1)} collective-permute-done((f32[712,256]{1,0:T(8,128)S(1)}, f32[712,256]{1,0:T(8,128)S(1)}, u32[]{:S(2)}, u32[]{:S(2)}) %collective-permute-start.5) | collective-permute-done | bytes 729120 | tf_op jit(solution)/shard_map/ppermute | solution.py:486
  87.1 3.1 %collective-permute-start.16 = (f32[4,176,256]{2,1,0:T(8,128)S(1)}, f32[4,176,256]{2,1,0:T(8,128)S(1)}, u32[]{:S(2)}, u32[]{:S(2)}) collective-permute-start(f32[4,176,256]{2,1,0:T(8,128)S(1)} %get-tuple-element.76), channel_id=1, source_target_pairs={{1,4},{4,1},{3,6},{6,3},{5,8},{8,5},{7,10},{10,7},{9,12},{12,9},{1... | collective-permute-start | bytes 2162696 | tf_op jit(solution)/shard_map/ppermute | solution.py:494
  90.2 9.5 %collective-permute-done.16.refs_13_.refs_4_ = f32[4,176,256]{2,1,0:T(8,128)S(1)} collective-permute-done((f32[4,176,256]{2,1,0:T(8,128)S(1)}, f32[4,176,256]{2,1,0:T(8,128)S(1)}, u32[]{:S(2)}, u32[]{:S(2)}) %collective-permute-start.16) | collective-permute-done | bytes 720928 | tf_op jit(solution)/shard_map/ppermute | solution.py:494
  103.0 3.2 %collective-permute-start.19 = (f32[4,176,256]{2,1,0:T(8,128)S(1)}, f32[4,176,256]{2,1,0:T(8,128)S(1)}, u32[]{:S(2)}, u32[]{:S(2)}) collective-permute-start(f32[4,176,256]{2,1,0:T(8,128)S(1)} %get-tuple-element.79.refs_10_), channel_id=1, source_target_pairs={{1,4},{4,1},{3,6},{6,3},{5,8},{8,5},{7,10},{10,7},{9,12},{12,9},{1... | collective-permute-start | bytes 2162696 | tf_op jit(solution)/shard_map/ppermute | solution.py:494
  106.2 2.9 %adjoint_2.1 = (f32[2,4,176,256]{3,2,1,0:T(8,128)S(1)}, f32[4,176,256]{2,1,0:T(8,128)S(1)}, f32[4,176,256]{2,1,0:T(8,128)S(1)}, f32[4,176,256]{2,1,0:T(8,128)S(1...) custom-call(f32[4,176,256]{2,1,0:T(8,128)S(1)} %get-tuple-element.74.refs_0_, ...), custom_call_target="tpu_custom_call" | custom-call | tf_op jit(solution)/shard_map/adjoint_2/pallas_call | solution.py:166
  109.6 3.1 %collective-permute-start.25 = (f32[4,176,256]{2,1,0:T(8,128)S(1)}, f32[4,176,256]{2,1,0:T(8,128)S(1)}, u32[]{:S(2)}, u32[]{:S(2)}) collective-permute-start(f32[4,176,256]{2,1,0:T(8,128)S(1)} %get-tuple-element.89), channel_id=1, source_target_pairs={{1,4},{4,1},{3,6},{6,3},{5,8},{8,5},{7,10},{10,7},{9,12},{12,9},{1... | collective-permute-start | bytes 2162696 | tf_op jit(solution)/shard_map/ppermute | solution.py:494
  112.7 3.2 %collective-permute-done.19.refs_4_ = f32[4,176,256]{2,1,0:T(8,128)S(1)} collective-permute-done((f32[4,176,256]{2,1,0:T(8,128)S(1)}, f32[4,176,256]{2,1,0:T(8,128)S(1)}, u32[]{:S(2)}, u32[]{:S(2)}) %collective-permute-start.19) | collective-permute-done | bytes 720928 | tf_op jit(solution)/shard_map/ppermute | solution.py:494
  115.9 2.8 %forward_2.1 = (f32[4,176,256]{2,1,0:T(8,128)S(1)}, f32[4,176,256]{2,1,0:T(8,128)S(1)}, f32[4,176,256]{2,1,0:T(8,128)S(1)}, f32[2,4,176,256]{3,2,1,0:T(8,128)S(1)}) custom-call(f32[4,176,256]{2,1,0:T(8,128)S(1)} %get-tuple-element.77.refs_0_.refs_8_, f32[4,176,256]{2,1,0:T(8,128)S(1)} %get-tuple-element.78.refs_1_.refs_9_, ...), custom_call_target="tpu_custom_call" | custom-call | tf_op jit(solution)/shard_map/forward_2/pallas_call | solution.py:166
  119.3 3.3 %collective-permute-start.22 = (f32[4,176,256]{2,1,0:T(8,128)S(1)}, f32[4,176,256]{2,1,0:T(8,128)S(1)}, u32[]{:S(2)}, u32[]{:S(2)}) collective-permute-start(f32[4,176,256]{2,1,0:T(8,128)S(1)} %get-tuple-element.85.refs_10_), channel_id=1, source_target_pairs={{1,4},{4,1},{3,6},{6,3},{5,8},{8,5},{7,10},{10,7},{9,12},{12,9},{1... | collective-permute-start | bytes 2162696 | tf_op jit(solution)/shard_map/ppermute | solution.py:494
  124.0 2.8 %adjoint_1.1 = (f32[4,160,256]{2,1,0:T(8,128)S(1)}, f32[4,160,256]{2,1,0:T(8,128)S(1)}) custom-call(f32[4,176,256]{2,1,0:T(8,128)S(1)} %get-tuple-element.87.refs_0_, f32[4,176,256]{2,1,0:T(8,128)S(1)} %get-tuple-element.88.refs_1_, f32[4,176,256]{2,1,0:T(8,128)S(1)} %collective-permute-done.23.refs_2_, f32[4,176,256]{2,1,0:T(8,128)S(1)} %collective-permute-done.24.refs_3_, ...), custom_call_target="tpu_custom_call" | custom-call | tf_op jit(solution)/shard_map/adjoint_1/pallas_call | solution.py:166
  126.8 11.9 %collective-permute-done.26.refs_14_.refs_3_ = f32[4,160,256]{2,1,0:T(8,128)S(1)} collective-permute-done((f32[4,160,256]{2,1,0:T(8,128)S(1)}, f32[4,160,256]{2,1,0:T(8,128)S(1)}, u32[]{:S(2)}, u32[]{:S(2)}) %collective-permute-start.26) | collective-permute-done | bytes 655392 | tf_op jit(solution)/shard_map/ppermute | solution.py:486
  142.1 3.9 %collective-permute-start.29 = (f32[4,176,256]{2,1,0:T(8,128)S(1)}, f32[4,176,256]{2,1,0:T(8,128)S(1)}, u32[]{:S(2)}, u32[]{:S(2)}) collective-permute-start(f32[4,176,256]{2,1,0:T(8,128)S(1)} %get-tuple-element.94), channel_id=1, source_target_pairs={{1,4},{4,1},{3,6},{6,3},{5,8},{8,5},{7,10},{10,7},{9,12},{12,9},{1... | collective-permute-start | bytes 2162696 | tf_op jit(solution)/shard_map/ppermute | solution.py:494
  147.3 13.9 %collective-permute-done.30.refs_8_.refs_1_ = f32[4,160,256]{2,1,0:T(8,128)S(1)} collective-permute-done((f32[4,160,256]{2,1,0:T(8,128)S(1)}, f32[4,160,256]{2,1,0:T(8,128)S(1)}, u32[]{:S(2)}, u32[]{:S(2)}) %collective-permute-start.30) | collective-permute-done | bytes 655392 | tf_op jit(solution)/shard_map/ppermute | solution.py:486
  166.3 13.5 %collective-permute-done.31.refs_1_ = f32[4,160,256]{2,1,0:T(8,128)S(1)} collective-permute-done((f32[4,160,256]{2,1,0:T(8,128)S(1)}, f32[4,160,256]{2,1,0:T(8,128)S(1)}, u32[]{:S(2)}, u32[]{:S(2)}) %collective-permute-start.31) | collective-permute-done | bytes 655392 | tf_op jit(solution)/shard_map/ppermute | solution.py:486
  (81 shorter events, 36.3 us)
Async XLA Ops:
  5.4 17.6 %collective-permute-start.4 = (f32[720,256]{1,0:T(8,128)}, f32[720,256]{1,0:T(8,128)S(1)}, u32[]{:S(2)}, u32[]{:S(2)}) collective-permute-start(f32[720,256]{1,0:T(8,128)} %get-tuple-element.57.sent_ref), channel_id=1, source_target_pairs={{0,2},{1,3},{2,0},{3,1},{4,6},{5,7},{6,4},{7,5},{8,10},{9,11},{10,... | collective-permute-start | bytes 2211848 | tf_op jit(solution)/shard_map/ppermute | solution.py:486
  6.7 35.0 %collective-permute-start.6 = (f32[712,256]{1,0:T(8,128)}, f32[712,256]{1,0:T(8,128)}, u32[]{:S(2)}, u32[]{:S(2)}) collective-permute-start(f32[712,256]{1,0:T(8,128)} %get-tuple-element.62), channel_id=1, source_target_pairs={{0,2},{1,3},{2,0},{3,1},{4,6},{5,7},{6,4},{7,5},{8,10},{9,11},{10,... | collective-permute-start | bytes 2187272 | tf_op jit(solution)/shard_map/ppermute | solution.py:486
  6.9 47.5 %collective-permute-start.10 = (f32[712,256]{1,0:T(8,128)}, f32[712,256]{1,0:T(8,128)}, u32[]{:S(2)}, u32[]{:S(2)}) collective-permute-start(f32[712,256]{1,0:T(8,128)} %get-tuple-element.69), channel_id=1, source_target_pairs={{0,2},{1,3},{2,0},{3,1},{4,6},{5,7},{6,4},{7,5},{8,10},{9,11},{10,... | collective-permute-start | bytes 2187272 | tf_op jit(solution)/shard_map/ppermute | solution.py:486
  8.2 61.8 %collective-permute-start = (f32[712,256]{1,0:T(8,128)}, f32[712,256]{1,0:T(8,128)}, u32[]{:S(2)}, u32[]{:S(2)}) collective-permute-start(f32[712,256]{1,0:T(8,128)} %get-tuple-element.52), channel_id=1, source_target_pairs={{0,2},{1,3},{2,0},{3,1},{4,6},{5,7},{6,4},{7,5},{8,10},{9,11},{10,... | collective-permute-start | bytes 2187272 | tf_op jit(solution)/shard_map/ppermute | solution.py:486
  43.9 13.0 %collective-permute-start.9 = (f32[4,176,256]{2,1,0:T(8,128)S(1)}, f32[4,176,256]{2,1,0:T(8,128)S(1)}, u32[]{:S(2)}, u32[]{:S(2)}) collective-permute-start(f32[4,176,256]{2,1,0:T(8,128)S(1)} %get-tuple-element.66), channel_id=1, source_target_pairs={{1,4},{4,1},{3,6},{6,3},{5,8},{8,5},{7,10},{10,7},{9,12},{12,9},{1... | collective-permute-start | bytes 2162696 | tf_op jit(solution)/shard_map/ppermute | solution.py:494
  54.4 31.1 %collective-permute-start.5 = (f32[712,256]{1,0:T(8,128)S(1)}, f32[712,256]{1,0:T(8,128)S(1)}, u32[]{:S(2)}, u32[]{:S(2)}) collective-permute-start(f32[712,256]{1,0:T(8,128)S(1)} %copy-done.9), channel_id=1, source_target_pairs={{0,2},{1,3},{2,0},{3,1},{4,6},{5,7},{6,4},{7,5},{8,10},{9,11},{10,... | collective-permute-start | bytes 2187272 | tf_op jit(solution)/shard_map/ppermute | solution.py:486
  60.9 13.3 %collective-permute-start.11 = (f32[4,176,256]{2,1,0:T(8,128)S(1)}, f32[4,176,256]{2,1,0:T(8,128)S(1)}, u32[]{:S(2)}, u32[]{:S(2)}) collective-permute-start(f32[4,176,256]{2,1,0:T(8,128)S(1)} %get-tuple-element.70.refs_0_), channel_id=1, source_target_pairs={{0,1},{1,0},{2,3},{3,2},{4,5},{5,4},{6,7},{7,6},{8,9},{9,8},{10,11... | collective-permute-start | bytes 2162696 | tf_op jit(solution)/shard_map/ppermute | solution.py:492
  62.8 15.0 %collective-permute-start.13 = (f32[4,176,256]{2,1,0:T(8,128)S(1)}, f32[4,176,256]{2,1,0:T(8,128)S(1)}, u32[]{:S(2)}, u32[]{:S(2)}) collective-permute-start(f32[4,176,256]{2,1,0:T(8,128)S(1)} %get-tuple-element.72), channel_id=1, source_target_pairs={{1,4},{4,1},{3,6},{6,3},{5,8},{8,5},{7,10},{10,7},{9,12},{12,9},{1... | collective-permute-start | bytes 2162696 | tf_op jit(solution)/shard_map/ppermute | solution.py:494
  71.4 15.6 %collective-permute-start.1 = (f32[4,176,256]{2,1,0:T(8,128)S(1)}, f32[4,176,256]{2,1,0:T(8,128)S(1)}, u32[]{:S(2)}, u32[]{:S(2)}) collective-permute-start(f32[4,176,256]{2,1,0:T(8,128)S(1)} %get-tuple-element.53.refs_0_.refs_9_), channel_id=1, source_target_pairs={{0,1},{1,0},{2,3},{3,2},{4,5},{5,4},{6,7},{7,6},{8,9},{9,8},{10,11... | collective-permute-start | bytes 2162696 | tf_op jit(solution)/shard_map/ppermute | solution.py:492
  74.2 16.0 %collective-permute-start.2 = (f32[4,176,256]{2,1,0:T(8,128)S(1)}, f32[4,176,256]{2,1,0:T(8,128)S(1)}, u32[]{:S(2)}, u32[]{:S(2)}) collective-permute-start(f32[4,176,256]{2,1,0:T(8,128)S(1)} %get-tuple-element.54.refs_1_.refs_10_), channel_id=1, source_target_pairs={{0,1},{1,0},{2,3},{3,2},{4,5},{5,4},{6,7},{7,6},{8,9},{9,8},{10,11... | collective-permute-start | bytes 2162696 | tf_op jit(solution)/shard_map/ppermute | solution.py:493
  74.3 15.9 %collective-permute-start.3 = (f32[4,176,256]{2,1,0:T(8,128)S(1)}, f32[4,176,256]{2,1,0:T(8,128)S(1)}, u32[]{:S(2)}, u32[]{:S(2)}) collective-permute-start(f32[4,176,256]{2,1,0:T(8,128)S(1)} %get-tuple-element.55), channel_id=1, source_target_pairs={{1,4},{4,1},{3,6},{6,3},{5,8},{8,5},{7,10},{10,7},{9,12},{12,9},{1... | collective-permute-start | bytes 2162696 | tf_op jit(solution)/shard_map/ppermute | solution.py:494
  87.1 12.6 %collective-permute-start.16 = (f32[4,176,256]{2,1,0:T(8,128)S(1)}, f32[4,176,256]{2,1,0:T(8,128)S(1)}, u32[]{:S(2)}, u32[]{:S(2)}) collective-permute-start(f32[4,176,256]{2,1,0:T(8,128)S(1)} %get-tuple-element.76), channel_id=1, source_target_pairs={{1,4},{4,1},{3,6},{6,3},{5,8},{8,5},{7,10},{10,7},{9,12},{12,9},{1... | collective-permute-start | bytes 2162696 | tf_op jit(solution)/shard_map/ppermute | solution.py:494
  103.0 12.9 %collective-permute-start.19 = (f32[4,176,256]{2,1,0:T(8,128)S(1)}, f32[4,176,256]{2,1,0:T(8,128)S(1)}, u32[]{:S(2)}, u32[]{:S(2)}) collective-permute-start(f32[4,176,256]{2,1,0:T(8,128)S(1)} %get-tuple-element.79.refs_10_), channel_id=1, source_target_pairs={{1,4},{4,1},{3,6},{6,3},{5,8},{8,5},{7,10},{10,7},{9,12},{12,9},{1... | collective-permute-start | bytes 2162696 | tf_op jit(solution)/shard_map/ppermute | solution.py:494
  109.1 13.6 %collective-permute-start.24 = (f32[4,176,256]{2,1,0:T(8,128)S(1)}, f32[4,176,256]{2,1,0:T(8,128)S(1)}, u32[]{:S(2)}, u32[]{:S(2)}) collective-permute-start(f32[4,176,256]{2,1,0:T(8,128)S(1)} %get-tuple-element.88.refs_1_), channel_id=1, source_target_pairs={{0,1},{1,0},{2,3},{3,2},{4,5},{5,4},{6,7},{7,6},{8,9},{9,8},{10,11... | collective-permute-start | bytes 2162696 | tf_op jit(solution)/shard_map/ppermute | solution.py:493
  109.6 14.4 %collective-permute-start.25 = (f32[4,176,256]{2,1,0:T(8,128)S(1)}, f32[4,176,256]{2,1,0:T(8,128)S(1)}, u32[]{:S(2)}, u32[]{:S(2)}) collective-permute-start(f32[4,176,256]{2,1,0:T(8,128)S(1)} %get-tuple-element.89), channel_id=1, source_target_pairs={{1,4},{4,1},{3,6},{6,3},{5,8},{8,5},{7,10},{10,7},{9,12},{12,9},{1... | collective-permute-start | bytes 2162696 | tf_op jit(solution)/shard_map/ppermute | solution.py:494
  118.8 19.9 %collective-permute-start.20 = (f32[4,176,256]{2,1,0:T(8,128)S(1)}, f32[4,176,256]{2,1,0:T(8,128)S(1)}, u32[]{:S(2)}, u32[]{:S(2)}) collective-permute-start(f32[4,176,256]{2,1,0:T(8,128)S(1)} %get-tuple-element.83.refs_0_), channel_id=1, source_target_pairs={{0,1},{1,0},{2,3},{3,2},{4,5},{5,4},{6,7},{7,6},{8,9},{9,8},{10,11... | collective-permute-start | bytes 2162696 | tf_op jit(solution)/shard_map/ppermute | solution.py:492
  118.8 19.9 %collective-permute-start.21 = (f32[4,176,256]{2,1,0:T(8,128)S(1)}, f32[4,176,256]{2,1,0:T(8,128)S(1)}, u32[]{:S(2)}, u32[]{:S(2)}) collective-permute-start(f32[4,176,256]{2,1,0:T(8,128)S(1)} %get-tuple-element.84.refs_1_), channel_id=1, source_target_pairs={{0,1},{1,0},{2,3},{3,2},{4,5},{5,4},{6,7},{7,6},{8,9},{9,8},{10,11... | collective-permute-start | bytes 2162696 | tf_op jit(solution)/shard_map/ppermute | solution.py:493
  119.3 19.4 %collective-permute-start.22 = (f32[4,176,256]{2,1,0:T(8,128)S(1)}, f32[4,176,256]{2,1,0:T(8,128)S(1)}, u32[]{:S(2)}, u32[]{:S(2)}) collective-permute-start(f32[4,176,256]{2,1,0:T(8,128)S(1)} %get-tuple-element.85.refs_10_), channel_id=1, source_target_pairs={{1,4},{4,1},{3,6},{6,3},{5,8},{8,5},{7,10},{10,7},{9,12},{12,9},{1... | collective-permute-start | bytes 2162696 | tf_op jit(solution)/shard_map/ppermute | solution.py:494
  122.7 16.0 %collective-permute-start.26 = (f32[4,160,256]{2,1,0:T(8,128)S(1)}, f32[4,160,256]{2,1,0:T(8,128)S(1)}, u32[]{:S(2)}, u32[]{:S(2)}) collective-permute-start(f32[4,160,256]{2,1,0:T(8,128)S(1)} %get-tuple-element.91), channel_id=1, source_target_pairs={{0,2},{1,3},{2,0},{3,1},{4,6},{5,7},{6,4},{7,5},{8,10},{9,11},{10,... | collective-permute-start | bytes 1966088 | tf_op jit(solution)/shard_map/ppermute | solution.py:486
  141.5 19.7 %collective-permute-start.27 = (f32[4,176,256]{2,1,0:T(8,128)S(1)}, f32[4,176,256]{2,1,0:T(8,128)S(1)}, u32[]{:S(2)}, u32[]{:S(2)}) collective-permute-start(f32[4,176,256]{2,1,0:T(8,128)S(1)} %get-tuple-element.92.refs_0_), channel_id=1, source_target_pairs={{0,1},{1,0},{2,3},{3,2},{4,5},{5,4},{6,7},{7,6},{8,9},{9,8},{10,11... | collective-permute-start | bytes 2162696 | tf_op jit(solution)/shard_map/ppermute | solution.py:492
  141.8 19.4 %collective-permute-start.28 = (f32[4,176,256]{2,1,0:T(8,128)S(1)}, f32[4,176,256]{2,1,0:T(8,128)S(1)}, u32[]{:S(2)}, u32[]{:S(2)}) collective-permute-start(f32[4,176,256]{2,1,0:T(8,128)S(1)} %get-tuple-element.93.refs_1_), channel_id=1, source_target_pairs={{0,1},{1,0},{2,3},{3,2},{4,5},{5,4},{6,7},{7,6},{8,9},{9,8},{10,11... | collective-permute-start | bytes 2162696 | tf_op jit(solution)/shard_map/ppermute | solution.py:493
  142.1 19.1 %collective-permute-start.29 = (f32[4,176,256]{2,1,0:T(8,128)S(1)}, f32[4,176,256]{2,1,0:T(8,128)S(1)}, u32[]{:S(2)}, u32[]{:S(2)}) collective-permute-start(f32[4,176,256]{2,1,0:T(8,128)S(1)} %get-tuple-element.94), channel_id=1, source_target_pairs={{1,4},{4,1},{3,6},{6,3},{5,8},{8,5},{7,10},{10,7},{9,12},{12,9},{1... | collective-permute-start | bytes 2162696 | tf_op jit(solution)/shard_map/ppermute | solution.py:494
  146.0 15.2 %collective-permute-start.30 = (f32[4,160,256]{2,1,0:T(8,128)S(1)}, f32[4,160,256]{2,1,0:T(8,128)S(1)}, u32[]{:S(2)}, u32[]{:S(2)}) collective-permute-start(f32[4,160,256]{2,1,0:T(8,128)S(1)} %get-tuple-element.96), channel_id=1, source_target_pairs={{0,2},{1,3},{2,0},{3,1},{4,6},{5,7},{6,4},{7,5},{8,10},{9,11},{10,... | collective-permute-start | bytes 1966088 | tf_op jit(solution)/shard_map/ppermute | solution.py:486
  163.5 16.3 %collective-permute-start.31 = (f32[4,160,256]{2,1,0:T(8,128)S(1)}, f32[4,160,256]{2,1,0:T(8,128)S(1)}, u32[]{:S(2)}, u32[]{:S(2)}) collective-permute-start(f32[4,160,256]{2,1,0:T(8,128)S(1)} %get-tuple-element.98), channel_id=1, source_target_pairs={{0,2},{1,3},{2,0},{3,1},{4,6},{5,7},{6,4},{7,5},{8,10},{9,11},{10,... | collective-permute-start | bytes 1966088 | tf_op jit(solution)/shard_map/ppermute | solution.py:486
  (18 other events, 231.8 us)

commit v3 on v2

--- a/solution.py
+++ b/solution.py
@@ -67,8 +67,8 @@
         self.wide = self.half + EXTRA
         self.pair = (2, rows, self.wide, depth)
         self.block = (rows, self.wide, depth)
-        self.moved = (rows * self.wide + 8, depth)
-        self.moved_first = (rows * self.wide + 16, depth)
+        self.edge = (rows * self.wide + 8, depth)
+        self.moved = (rows * self.wide + 16, depth)
         self.sent = (rows, self.half, depth)
         self.whole = (rows, cols, depth)
 
@@ -100,9 +100,13 @@
     return pl.ds(first, 8)
 
 
+def flat(sizes, row, first):
+    return pl.ds(pl.multiple_of(first + row * sizes.wide, 8), 8), slice(None)
+
+
 def merged(sizes, own, moved, slot, row, first):
     _, half, _ = place()
-    received = moved[pl.ds(pl.multiple_of(first + row * sizes.wide, 8), 8), :]
+    received = moved[flat(sizes, row, first)]
     return jnp.where(half == slot, own[row, cut(first), :], received)
 
 
@@ -142,7 +146,11 @@
 
                 def columns(first):
                     near = [
-                        block[row, cut(first), :]
+                        block[
+                            flat(sizes, row, first)
+                            if block is beside
+                            else (row, cut(first), slice(None))
+                        ]
                         for block in order[2 * slot : 2 * slot + 3]
                         for row in range(rows)
                     ]
@@ -177,32 +185,52 @@
     )(*operands)
 
 
-def pack(sizes, velocity, adjoint, wave, traces):
-    def body(v_ref, a_ref, w_ref, traces_ref, *rest):
-        outs, sems = rest[:5], rest[5]
+def pack_first(sizes, velocity, traces):
+    def body(field, traces_ref, out, sems):
         _, half, _ = place()
         copies = Copies(sems)
-        fields = (v_ref, a_ref.at[0, 0], a_ref.at[1, 0], w_ref.at[1, 0], w_ref.at[0, 0])
+        copies.start(
+            field.at[:, sizes.window(1 - half), :],
+            out.at[pl.ds(0, sizes.rows * sizes.wide)].reshape(sizes.block),
+        )
+        each, steps = traces_ref.shape
+        out[sizes.moved_tail, :] = jnp.zeros((16, sizes.depth), F32)
+        out[pl.ds(sizes.rows * sizes.wide, each), :steps] = traces_ref[...]
+        copies.wait()
+
+    return run(
+        body,
+        "pack_first",
+        (velocity, traces),
+        [ANY, VMEM],
+        [(sizes.moved, VMEM)],
+        limit=PACK_LIMIT,
+        sems=1,
+    )
+
+
+def pack(sizes, adjoint, wave):
+    def body(a_ref, w_ref, *rest):
+        outs, sems = rest[:4], rest[4]
+        _, half, _ = place()
+        copies = Copies(sems)
+        fields = (a_ref.at[0, 0], a_ref.at[1, 0], w_ref.at[1, 0], w_ref.at[0, 0])
         for field, out in zip(fields, outs):
-            for row in range(sizes.rows):
-                copies.start(
-                    field.at[row, sizes.window(1 - half), :], out.at[sizes.moved_row(row)]
-                )
-        each, steps = traces_ref.shape
-        for out in outs[1:]:
-            out[sizes.rows * sizes.wide :, :] = jnp.zeros((8, sizes.depth), F32)
-        outs[0][sizes.rows * sizes.wide :, :] = jnp.zeros((16, sizes.depth), F32)
-        outs[0][pl.ds(sizes.rows * sizes.wide, each), :steps] = traces_ref[...]
+            copies.start(
+                field.at[:, sizes.window(1 - half), :],
+                out.at[pl.ds(0, sizes.rows * sizes.wide)].reshape(sizes.block),
+            )
+            out[sizes.moved_tail, :] = jnp.zeros((16, sizes.depth), F32)
         copies.wait()
 
     return run(
         body,
         "pack",
-        (velocity, adjoint, wave, traces),
-        [ANY] * 3 + [VMEM],
-        [(sizes.moved_first, VMEM)] + [(sizes.moved, VMEM)] * 4,
+        (adjoint, wave),
+        [ANY] * 2,
+        [(sizes.moved, VMEM)] * 4,
         limit=PACK_LIMIT,
-        sems=20,
+        sems=4,
     )
 
 
@@ -263,7 +291,7 @@
                     here = v_ref[slot, row, cut(first), :]
                     u_out[row, cut(first), :] = here * here * value
             for row in range(sizes.rows):
-                z_out[row, cut(first), :] = jnp.where(
+                z_out[flat(sizes, row, first)] = jnp.where(
                     core == 0, u0_out[row, cut(first), :], u1_out[row, cut(first), :]
                 )
 
@@ -274,7 +302,7 @@
         "adjoint_begin",
         (speed, own, moved, settled),
         [VMEM] * 3 + [ANY],
-        [(sizes.pair, VMEM)] + [(sizes.block, VMEM)] * 3,
+        [(sizes.pair, VMEM)] + [(sizes.block, VMEM)] * 2 + [(sizes.edge, VMEM)],
     )
 
 
@@ -326,18 +354,23 @@
                 value = here * here * value
                 (u0_out, u1_out)[slot][row, cut(first), :] = value
                 if which == slot:
-                    z_out[row, cut(first), :] = value
+                    z_out[flat(sizes, row, first)] = value
 
         sweep(sizes, u_refs, mixed, finish)
         if ends:
             kept_out[...] = next_out[half, :, sizes.own(half), :]
-            sent_out[...] = next_out[1 - half, :, sizes.own(half), :]
+            for row in range(sizes.rows):
+                sent_out[pl.ds(row * sizes.half, sizes.half), :] = next_out[
+                    1 - half, row, sizes.own(half), :
+                ]
+            rest = sizes.moved[0] - sizes.rows * sizes.half
+            sent_out[pl.ds(sizes.rows * sizes.half, rest), :] = jnp.zeros((rest, sizes.depth), F32)
 
     outs = []
     if more:
-        outs += [(sizes.pair, VMEM)] + [(sizes.block, VMEM)] * 3
+        outs += [(sizes.pair, VMEM)] + [(sizes.block, VMEM)] * 2 + [(sizes.edge, VMEM)]
     if ends:
-        outs += [(sizes.sent, VMEM)] * 2
+        outs += [(sizes.sent, VMEM), (sizes.moved, VMEM)]
     return run(
         body,
         f"adjoint_{step_no}",
@@ -348,8 +381,9 @@
     )
 
 
-def forward_begin(sizes, own, moved):
-    def body(own_ref, moved_ref, c0_out, c1_out, z_out):
+def forward_begin(sizes, own, moved, settled):
+    def body(own_ref, moved_ref, *rest):
+        c0_out, c1_out, z_out = rest[len(settled) :]
         _, _, core = place()
 
         def columns(first):
@@ -357,12 +391,16 @@
                 pair = [merged(sizes, own_ref, moved_ref, slot, row, first) for slot in range(2)]
                 c0_out[row, cut(first), :] = pair[0]
                 c1_out[row, cut(first), :] = pair[1]
-                z_out[row, cut(first), :] = jnp.where(core == 0, *pair)
+                z_out[flat(sizes, row, first)] = jnp.where(core == 0, *pair)
 
         over_columns(sizes, columns)
 
     return run(
-        body, "forward_begin", (own, moved), [VMEM] * 2, [(sizes.block, VMEM)] * 3
+        body,
+        "forward_begin",
+        (own, moved, *settled),
+        [VMEM] * 2 + [ANY] * len(settled),
+        [(sizes.block, VMEM)] * 2 + [(sizes.edge, VMEM)],
     )
 
 
@@ -409,7 +447,7 @@
                 value = 2.0 * centre - last + here * here * total
                 (c0_out, c1_out)[slot][row, cut(first), :] = value
                 if which == slot:
-                    z_out[row, cut(first), :] = value
+                    z_out[flat(sizes, row, first)] = value
 
         sweep(sizes, c_refs, mixed, finish)
         if not more:
@@ -422,13 +460,14 @@
             row = cells_ref[0, 0] - ((level * 2 + slot) * 2 + core) * sizes.rows
             inside = (row >= 0) & (row < sizes.rows) & (col >= 0) & (col < sizes.wide)
 
-            def put(out):
-                at = (row, pl.ds(col, 1), slice(None))
+            def put(out, at):
                 hit = iota((1, sizes.depth), 1) == cells_ref[0, 2]
                 out[at] = out[at] + jnp.where(hit, pulse, 0.0)
 
-            pl.when(inside)(functools.partial(put, c_out))
-            pl.when(inside & (core == slot))(functools.partial(put, z_out))
+            pl.when(inside)(functools.partial(put, c_out, (row, pl.ds(col, 1), slice(None))))
+            pl.when(inside & (core == slot))(
+                functools.partial(put, z_out, (pl.ds(col + row * sizes.wide, 1), slice(None)))
+            )
 
     operands = (*current, speed, *later)
     if not first_step:
@@ -439,7 +478,7 @@
     if more:
         operands += source
         specs += [SMEM] * 3
-        outs = [(sizes.block, VMEM)] * 3 + [(sizes.pair, VMEM)]
+        outs = [(sizes.block, VMEM)] * 2 + [(sizes.edge, VMEM), (sizes.pair, VMEM)]
     else:
         outs = [(sizes.sent, VMEM)] * 2
     return run(
@@ -460,6 +499,8 @@
         for index, ref in enumerate(refs[:-2]):
             target = out.at[index // 2, 0] if len(shape) == 5 else out
             side = half if index % 2 == 0 else 1 - half
+            if len(ref.shape) == 2:
+                ref = ref.at[pl.ds(0, sizes.rows * sizes.half)].reshape(sizes.sent)
             copies.start(ref, target.at[:, sizes.final(side), :])
         copies.wait()
 
@@ -495,7 +536,7 @@
         )
 
     each, steps = traces.shape[2], traces.shape[1]
-    sent = pack(sizes, velocity, adjoint_state, wave_state, traces[0].T)
+    sent = pack_first(sizes, velocity, traces[0].T) + pack(sizes, adjoint_state, wave_state)
     velocity_in, later_in, latest_in, current_in, before_in = map(over, sent)
     kept = keep(sizes, velocity, adjoint_state, wave_state)
 
@@ -511,32 +552,29 @@
     source = (source_cells, wavelet, start_step)
     later4, *scaled = adjoint_begin(sizes, speed, kept[1], later_in, samples)
     later3, *scaled = adjoint(4, exchange(*scaled), later4, (kept[2], latest_in), *common)
-    current1 = forward_begin(sizes, kept[3], current_in)
-    later2, *scaled = adjoint(3, exchange(*scaled), later3, (later4,), *common)
-    scaled2 = exchange(*scaled)
+    scaled = exchange(*scaled)
+    current1 = exchange(*forward_begin(sizes, kept[3], current_in, scaled[:1]))
+    later2, *scaled = adjoint(3, scaled, later3, (later4,), *common, current1[:1])
+    scaled = exchange(*scaled)
     *current2, image = forward(
-        1, exchange(*current1), (kept[4], before_in), speed, (), None, source, scaled2[2:]
-    )
+        1, current1, (kept[4], before_in), speed, (), None, source
+    )
+    current2 = exchange(*current2)
     later1, *scaled, mine1, sent1 = adjoint(
-        2, scaled2, later2, (later3,), *common, tuple(current2[2:])
+        2, scaled, later2, (later3,), *common, current2[:1]
     )
     got1 = over(sent1)
+    scaled = exchange(*scaled)
     *current3, gradient = forward(
-        2, exchange(*current2), tuple(current1[:2]), speed, (later1, later2), image, source
-    )
+        2, current2, current1[:2], speed, (later1, later2), image, source, scaled[2:4]
+    )
+    current3 = exchange(*current3)
     mine0, sent0 = adjoint(
-        1, exchange(*scaled), later1, (later2,), *common, tuple(current3[2:])
+        1, scaled, later1, (later2,), *common, current3[2:4]
     )
     got0 = over(sent0)
     *current4, gradient = forward(
-        3,
-        exchange(*current3),
-        tuple(current2[:2]),
-        speed,
-        (later3,),
-        gradient,
-        source,
-        (mine0, got1),
+        3, current3, current2[:2], speed, (later3,), gradient, source, (mine0, got1)
     )
     mine, sent = forward(4, exchange(*current4), (), speed, (later4,), gradient, None, (got0,))
     got = over(sent)

time: 182 us -> 156 us (0.86)
  waiting for transfers between devices: 79.5 us -> 50.4 us
  local copies, waits for them, and re-layouts: 1.35 us -> 5.55 us
  starting transfers between devices: 43.8 us -> 40.9 us
    ppermute x8, waiting for transfers between devices: 65.6 us -> 30.4 us  [over(): return lax.ppermute(field, 'gx', across)]
    unnamed x22 -> x28, local copies, waits for them, and re-layouts: 1.24 us -> 5.44 us
    ppermute x8, waiting for transfers between devices: 13.9 us -> 16.3 us  [exchange(): lax.ppermute(edge, 'gx', levels)]
    ppermute x8, starting transfers between devices: 5.41 us -> 3.29 us  [exchange(): lax.ppermute(block0, 'gx', cores)]
    ppermute x8, waiting for transfers between devices: 0.02 us -> 1.91 us  [exchange(): lax.ppermute(block1, 'gx', cores)]
    pallas_call x15 -> x16, Pallas kernels: 37.4 us -> 37.7 us  [run(): pl.pallas_call(body, name=name, out_shape=[jax.ShapeDtypeStruct(shape, F3...]
  transfers between devices with their start and end apart: 32 -> 32, of which waited for: 10 -> 14; matrix products, arithmetic and copies ran while one was open for 0% -> 0% of each run, Pallas kernels for 13% -> 21%
where the time goes in v3:
time: 156 us; the launch traced here: 153 us
  waiting for transfers between devices  50.4 us (32%)
  starting transfers between devices  40.9 us (26%)
  Pallas kernels  37.7 us (24%)
  blocking collectives  17 us (11%)
  local copies, waits for them, and re-layouts  5.55 us (4%)
  between operations  1.78 us (1%)
    pallas_call x16, Pallas kernels, run(): pl.pallas_call(body, name=name, out_shape=[jax.ShapeDtypeStruct(shape, F3...  37.7 us
    ppermute x8, waiting for transfers between devices, over(): return lax.ppermute(field, 'gx', across)  30.4 us
    ppermute x8, starting transfers between devices, exchange(): lax.ppermute(edge, 'gx', levels)  25.2 us
    all_gather x1, blocking collectives, on_device(): tails = lax.all_gather(tails, 'gx', axis_index_groups=halves)  17 us
    ppermute x8, waiting for transfers between devices, exchange(): lax.ppermute(edge, 'gx', levels)  16.3 us
    ppermute x8, starting transfers between devices, over(): return lax.ppermute(field, 'gx', across)  8.08 us
    unnamed x28, local copies, waits for them, and re-layouts  5.44 us
    ppermute x8, starting transfers between devices, exchange(): lax.ppermute(block1, 'gx', cores)  4.32 us
  transfers between devices with their start and end apart: 32, of which 14 were waited for; matrix products, arithmetic and copies ran while one was open for 0% of the time, Pallas kernels for 21%

profile of v3, /device:TPU:11, one launch (start us, length us, event | category | flops | bytes accessed | tf_op | source)
XLA Modules:
  0.0 153.3 jit_solution(6723359625444414011)
XLA Ops:
  4.6 3.4 %pack.1 = (f32[720,256]{1,0:T(8,128)}, f32[720,256]{1,0:T(8,128)}, f32[720,256]{1,0:T(8,128)}, f32[720,256]{1,0:T(8,128)}) custom-call(f32[2,1,4,320,256]{4,3,2,1,0:T(8,128)} %a_ref.3, f32[2,1,4,320,256]{4,3,2,1,0:T(8,128)} %w_ref.3), custom_call_target="tpu_custom_call" | custom-call | tf_op jit(solution)/shard_map/pack/pallas_call | solution.py:174
  9.6 3.8 %keep.1 = (f32[4,176,256]{2,1,0:T(8,128)}, f32[4,176,256]{2,1,0:T(8,128)}, f32[4,176,256]{2,1,0:T(8,128)}, f32[4,176,256]{2,1,0:T(8,128)}, f32[4,176,256]{2,1,0:T(8,128)}) custom-call(f32[4,320,256]{2,1,0:T(8,128)} %field.1, f32[2,1,4,320,256]{4,3,2,1,0:T(8,128)} %a_ref.3, f32[2,1,4,320,256]{4,3,2,1,0:T(8,128)} %w_ref.3), custom_call_target="tpu_custom_call" | custom-call | tf_op jit(solution)/shard_map/keep/pallas_call | solution.py:174
  14.0 6.9 %collective-permute-done.1.moved_ref = f32[720,256]{1,0:T(8,128)S(1)} collective-permute-done((f32[720,256]{1,0:T(8,128)}, f32[720,256]{1,0:T(8,128)S(1)}, u32[]{:S(2)}, u32[]{:S(2)}) %collective-permute-start.1) | collective-permute-done | bytes 737312 | tf_op jit(solution)/shard_map/ppermute | solution.py:527
  25.3 17.0 %all-gather = f32[16,16,256]{2,1,0:T(8,128)S(1)} all-gather(f32[2,16,256]{2,1,0:T(8,128)S(1)} %get-tuple-element.56), channel_id=2, replica_groups={{0,1,4,5,8,9,12,13},{2,3,6,7,10,11,14,15},{16,17,20,21,24,25,28,29},{18..., dimensions={0}, use_global_device_ids=true | all-gather | bytes 294912 | tf_op jit(solution)/shard_map/all_gather | solution.py:544
  49.3 3.4 %collective-permute-done.6.refs_10_ = f32[720,256]{1,0:T(8,128)} collective-permute-done((f32[720,256]{1,0:T(8,128)}, f32[720,256]{1,0:T(8,128)}, u32[]{:S(2)}, u32[]{:S(2)}) %collective-permute-start.6) | collective-permute-done | bytes 737312 | tf_op jit(solution)/shard_map/ppermute | solution.py:527
  53.9 4.4 %collective-permute-done.5.refs_4_ = f32[712,256]{1,0:T(8,128)S(1)} collective-permute-done((f32[712,256]{1,0:T(8,128)S(1)}, f32[712,256]{1,0:T(8,128)S(1)}, u32[]{:S(2)}, u32[]{:S(2)}) %collective-permute-start.5) | collective-permute-done | bytes 729120 | tf_op jit(solution)/shard_map/ppermute | solution.py:535
  58.3 4.0 %adjoint_4.1 = (f32[2,4,176,256]{3,2,1,0:T(8,128)S(1)}, f32[4,176,256]{2,1,0:T(8,128)S(1)}, f32[4,176,256]{2,1,0:T(8,128)S(1)}, f32[712,256]{1,0:T(8,128)S(1)}) custom-call(f32[4,176,256]{2,1,0:T(8,128)S(1)} %get-tuple-element.57.refs_0_, f32[4,176,256]{2,1,0:T(8,128)S(1)} %get-tuple-element.58.refs_1_, f32[4,176,256]{2,1,0:T(8,128)S(1)} %collective-permute-done.3.refs_2_, ...), custom_call_target="tpu_custom_call" | custom-call | tf_op jit(solution)/shard_map/adjoint_4/pallas_call | solution.py:174
  62.4 3.0 %collective-permute-start.16 = (f32[712,256]{1,0:T(8,128)S(1)}, f32[712,256]{1,0:T(8,128)S(1)}, u32[]{:S(2)}, u32[]{:S(2)}) collective-permute-start(f32[712,256]{1,0:T(8,128)S(1)} %get-tuple-element.73), channel_id=1, source_target_pairs={{1,4},{4,1},{3,6},{6,3},{5,8},{8,5},{7,10},{10,7},{9,12},{12,9},{1... | collective-permute-start | bytes 2187272 | tf_op jit(solution)/shard_map/ppermute | solution.py:535
  65.5 2.9 %collective-permute-done.moved_ref = f32[720,256]{1,0:T(8,128)S(1)} collective-permute-done((f32[720,256]{1,0:T(8,128)S(1)}, f32[720,256]{1,0:T(8,128)S(1)}, u32[]{:S(2)}, u32[]{:S(2)}) %collective-permute-start) | collective-permute-done | bytes 737312 | tf_op jit(solution)/shard_map/ppermute | solution.py:527
  71.4 3.1 %collective-permute-start.9 = (f32[712,256]{1,0:T(8,128)S(1)}, f32[712,256]{1,0:T(8,128)S(1)}, u32[]{:S(2)}, u32[]{:S(2)}) collective-permute-start(f32[712,256]{1,0:T(8,128)S(1)} %get-tuple-element.66), channel_id=1, source_target_pairs={{1,4},{4,1},{3,6},{6,3},{5,8},{8,5},{7,10},{10,7},{9,12},{12,9},{1... | collective-permute-start | bytes 2187272 | tf_op jit(solution)/shard_map/ppermute | solution.py:535
  75.4 2.8 %adjoint_3.1 = (f32[2,4,176,256]{3,2,1,0:T(8,128)S(1)}, f32[4,176,256]{2,1,0:T(8,128)S(1)}, f32[4,176,256]{2,1,0:T(8,128)S(1)}, f32[712,256]{1,0:T(8,128)S(1)}) custom-call(f32[4,176,256]{2,1,0:T(8,128)S(1)} %get-tuple-element.63.rest_0_.refs_0_, f32[4,176,256]{2,1,0:T(8,128)S(1)} %get-tuple-element.72.refs_1_, ...), custom_call_target="tpu_custom_call" | custom-call | tf_op jit(solution)/shard_map/adjoint_3/pallas_call | solution.py:174
  78.2 2.9 %collective-permute-start.19 = (f32[712,256]{1,0:T(8,128)S(1)}, f32[712,256]{1,0:T(8,128)S(1)}, u32[]{:S(2)}, u32[]{:S(2)}) collective-permute-start(f32[712,256]{1,0:T(8,128)S(1)} %get-tuple-element.77), channel_id=1, source_target_pairs={{1,4},{4,1},{3,6},{6,3},{5,8},{8,5},{7,10},{10,7},{9,12},{12,9},{1... | collective-permute-start | bytes 2187272 | tf_op jit(solution)/shard_map/ppermute | solution.py:535
  81.1 3.0 %collective-permute-done.10.refs_7_ = f32[720,256]{1,0:T(8,128)S(1)} collective-permute-done((f32[720,256]{1,0:T(8,128)S(1)}, f32[720,256]{1,0:T(8,128)S(1)}, u32[]{:S(2)}, u32[]{:S(2)}) %collective-permute-start.10) | collective-permute-done | bytes 737312 | tf_op jit(solution)/shard_map/ppermute | solution.py:527
  85.7 2.8 %forward_1.1 = (f32[4,176,256]{2,1,0:T(8,128)S(1)}, f32[4,176,256]{2,1,0:T(8,128)S(1)}, f32[712,256]{1,0:T(8,128)S(1)}, f32[2,4,176,256]{3,2,1,0:T(8,128)S(1)}) custom-call(f32[4,176,256]{2,1,0:T(8,128)S(1)} %get-tuple-element.64.refs_0_.refs_10_.refs_9_, f32[4,176,256]{2,1,0:T(8,128)S(1)} %get-tuple-element.65.refs_1_.refs_10_, ...), custom_call_target="tpu_custom_call" | custom-call | tf_op jit(solution)/shard_map/forward_1/pallas_call | solution.py:174
  88.5 3.7 %collective-permute-start.13 = (f32[712,256]{1,0:T(8,128)S(1)}, f32[712,256]{1,0:T(8,128)S(1)}, u32[]{:S(2)}, u32[]{:S(2)}) collective-permute-start(f32[712,256]{1,0:T(8,128)S(1)} %get-tuple-element.71), channel_id=1, source_target_pairs={{1,4},{4,1},{3,6},{6,3},{5,8},{8,5},{7,10},{10,7},{9,12},{12,9},{1... | collective-permute-start | bytes 2187272 | tf_op jit(solution)/shard_map/ppermute | solution.py:535
  92.8 2.9 %adjoint_2.1 = (f32[2,4,176,256]{3,2,1,0:T(8,128)S(1)}, f32[4,176,256]{2,1,0:T(8,128)S(1)}, f32[4,176,256]{2,1,0:T(8,128)S(1)}, f32[712,256]{1,0:T(8,128)S(1)}, ...) custom-call(f32[4,176,256]{2,1,0:T(8,128)S(1)} %get-tuple-element.75.refs_0_, ...), custom_call_target="tpu_custom_call" | custom-call | tf_op jit(solution)/shard_map/adjoint_2/pallas_call | solution.py:174
  97.5 3.6 %collective-permute-start.25 = (f32[712,256]{1,0:T(8,128)S(1)}, f32[712,256]{1,0:T(8,128)S(1)}, u32[]{:S(2)}, u32[]{:S(2)}) collective-permute-start(f32[712,256]{1,0:T(8,128)S(1)} %get-tuple-element.87), channel_id=1, source_target_pairs={{1,4},{4,1},{3,6},{6,3},{5,8},{8,5},{7,10},{10,7},{9,12},{12,9},{1... | collective-permute-start | bytes 2187272 | tf_op jit(solution)/shard_map/ppermute | solution.py:535
  101.6 2.9 %forward_2.1 = (f32[4,176,256]{2,1,0:T(8,128)S(1)}, f32[4,176,256]{2,1,0:T(8,128)S(1)}, f32[712,256]{1,0:T(8,128)S(1)}, f32[2,4,176,256]{3,2,1,0:T(8,128)S(1)}) custom-call(f32[4,176,256]{2,1,0:T(8,128)S(1)} %get-tuple-element.69.refs_10_.refs_0_.refs_8_, f32[4,176,256]{2,1,0:T(8,128)S(1)} %get-tuple-element.70.refs_1_.refs_9_, ...), custom_call_target="tpu_custom_call" | custom-call | tf_op jit(solution)/shard_map/forward_2/pallas_call | solution.py:174
  104.4 3.6 %collective-permute-start.24 = (f32[712,256]{1,0:T(8,128)S(1)}, f32[712,256]{1,0:T(8,128)S(1)}, u32[]{:S(2)}, u32[]{:S(2)}) collective-permute-start(f32[712,256]{1,0:T(8,128)S(1)} %get-tuple-element.85), channel_id=1, source_target_pairs={{1,4},{4,1},{3,6},{6,3},{5,8},{8,5},{7,10},{10,7},{9,12},{12,9},{1... | collective-permute-start | bytes 2187272 | tf_op jit(solution)/shard_map/ppermute | solution.py:535
  115.5 2.8 %collective-permute-done.24.refs_4_ = f32[712,256]{1,0:T(8,128)S(1)} collective-permute-done((f32[712,256]{1,0:T(8,128)S(1)}, f32[712,256]{1,0:T(8,128)S(1)}, u32[]{:S(2)}, u32[]{:S(2)}) %collective-permute-start.24) | collective-permute-done | bytes 729120 | tf_op jit(solution)/shard_map/ppermute | solution.py:535
  118.3 2.8 %forward_3.1 = (f32[4,176,256]{2,1,0:T(8,128)S(1)}, f32[4,176,256]{2,1,0:T(8,128)S(1)}, f32[712,256]{1,0:T(8,128)S(1)}, f32[2,4,176,256]{3,2,1,0:T(8,128)S(1)}) custom-call(f32[4,176,256]{2,1,0:T(8,128)S(1)} %get-tuple-element.83.refs_0_, f32[4,176,256]{2,1,0:T(8,128)S(1)} %get-tuple-element.84.refs_1_, ...), custom_call_target="tpu_custom_call" | custom-call | tf_op jit(solution)/shard_map/forward_3/pallas_call | solution.py:174
  121.1 3.4 %collective-permute-start.29 = (f32[712,256]{1,0:T(8,128)S(1)}, f32[712,256]{1,0:T(8,128)S(1)}, u32[]{:S(2)}, u32[]{:S(2)}) collective-permute-start(f32[712,256]{1,0:T(8,128)S(1)} %get-tuple-element.92), channel_id=1, source_target_pairs={{1,4},{4,1},{3,6},{6,3},{5,8},{8,5},{7,10},{10,7},{9,12},{12,9},{1... | collective-permute-start | bytes 2187272 | tf_op jit(solution)/shard_map/ppermute | solution.py:535
  127.8 6.0 %collective-permute-done.29.refs_4_ = f32[712,256]{1,0:T(8,128)S(1)} collective-permute-done((f32[712,256]{1,0:T(8,128)S(1)}, f32[712,256]{1,0:T(8,128)S(1)}, u32[]{:S(2)}, u32[]{:S(2)}) %collective-permute-start.29) | collective-permute-done | bytes 729120 | tf_op jit(solution)/shard_map/ppermute | solution.py:535
  137.8 14.3 %collective-permute-done.31.refs_1_ = f32[4,160,256]{2,1,0:T(8,128)S(1)} collective-permute-done((f32[4,160,256]{2,1,0:T(8,128)S(1)}, f32[4,160,256]{2,1,0:T(8,128)S(1)}, u32[]{:S(2)}, u32[]{:S(2)}) %collective-permute-start.31) | collective-permute-done | bytes 655392 | tf_op jit(solution)/shard_map/ppermute | solution.py:527
  (88 shorter events, 42.3 us)
Async XLA Ops:
  3.3 17.6 %collective-permute-start.1 = (f32[720,256]{1,0:T(8,128)}, f32[720,256]{1,0:T(8,128)S(1)}, u32[]{:S(2)}, u32[]{:S(2)}) collective-permute-start(f32[720,256]{1,0:T(8,128)} %pack_first.1.sent_ref), channel_id=1, source_target_pairs={{0,2},{1,3},{2,0},{3,1},{4,6},{5,7},{6,4},{7,5},{8,10},{9,11},{10,... | collective-permute-start | bytes 2211848 | tf_op jit(solution)/shard_map/ppermute | solution.py:527
  8.0 34.5 %collective-permute-start.2 = (f32[720,256]{1,0:T(8,128)}, f32[720,256]{1,0:T(8,128)}, u32[]{:S(2)}, u32[]{:S(2)}) collective-permute-start(f32[720,256]{1,0:T(8,128)} %get-tuple-element.55), channel_id=1, source_target_pairs={{0,2},{1,3},{2,0},{3,1},{4,6},{5,7},{6,4},{7,5},{8,10},{9,11},{10,... | collective-permute-start | bytes 2211848 | tf_op jit(solution)/shard_map/ppermute | solution.py:527
  8.3 44.3 %collective-permute-start.6 = (f32[720,256]{1,0:T(8,128)}, f32[720,256]{1,0:T(8,128)}, u32[]{:S(2)}, u32[]{:S(2)}) collective-permute-start(f32[720,256]{1,0:T(8,128)} %get-tuple-element.62), channel_id=1, source_target_pairs={{0,2},{1,3},{2,0},{3,1},{4,6},{5,7},{6,4},{7,5},{8,10},{9,11},{10,... | collective-permute-start | bytes 2211848 | tf_op jit(solution)/shard_map/ppermute | solution.py:527
  45.3 13.0 %collective-permute-start.5 = (f32[712,256]{1,0:T(8,128)S(1)}, f32[712,256]{1,0:T(8,128)S(1)}, u32[]{:S(2)}, u32[]{:S(2)}) collective-permute-start(f32[712,256]{1,0:T(8,128)S(1)} %get-tuple-element.59), channel_id=1, source_target_pairs={{1,4},{4,1},{3,6},{6,3},{5,8},{8,5},{7,10},{10,7},{9,12},{12,9},{1... | collective-permute-start | bytes 2187272 | tf_op jit(solution)/shard_map/ppermute | solution.py:535
  47.2 6.7 %collective-permute-start.3 = (f32[4,176,256]{2,1,0:T(8,128)S(1)}, f32[4,176,256]{2,1,0:T(8,128)S(1)}, u32[]{:S(2)}, u32[]{:S(2)}) collective-permute-start(f32[4,176,256]{2,1,0:T(8,128)S(1)} %get-tuple-element.57.refs_0_), channel_id=1, source_target_pairs={{0,1},{1,0},{2,3},{3,2},{4,5},{5,4},{6,7},{7,6},{8,9},{9,8},{10,11... | collective-permute-start | bytes 2162696 | tf_op jit(solution)/shard_map/ppermute | solution.py:533
  47.9 6.0 %collective-permute-start.4 = (f32[4,176,256]{2,1,0:T(8,128)S(1)}, f32[4,176,256]{2,1,0:T(8,128)S(1)}, u32[]{:S(2)}, u32[]{:S(2)}) collective-permute-start(f32[4,176,256]{2,1,0:T(8,128)S(1)} %get-tuple-element.58.refs_1_), channel_id=1, source_target_pairs={{0,1},{1,0},{2,3},{3,2},{4,5},{5,4},{6,7},{7,6},{8,9},{9,8},{10,11... | collective-permute-start | bytes 2162696 | tf_op jit(solution)/shard_map/ppermute | solution.py:534
  48.0 20.3 %collective-permute-start = (f32[720,256]{1,0:T(8,128)S(1)}, f32[720,256]{1,0:T(8,128)S(1)}, u32[]{:S(2)}, u32[]{:S(2)}) collective-permute-start(f32[720,256]{1,0:T(8,128)S(1)} %copy-done.12), channel_id=1, source_target_pairs={{0,2},{1,3},{2,0},{3,1},{4,6},{5,7},{6,4},{7,5},{8,10},{9,11},{10,... | collective-permute-start | bytes 2211848 | tf_op jit(solution)/shard_map/ppermute | solution.py:527
  52.6 31.5 %collective-permute-start.10 = (f32[720,256]{1,0:T(8,128)S(1)}, f32[720,256]{1,0:T(8,128)S(1)}, u32[]{:S(2)}, u32[]{:S(2)}) collective-permute-start(f32[720,256]{1,0:T(8,128)S(1)} %copy-done.11), channel_id=1, source_target_pairs={{0,2},{1,3},{2,0},{3,1},{4,6},{5,7},{6,4},{7,5},{8,10},{9,11},{10,... | collective-permute-start | bytes 2211848 | tf_op jit(solution)/shard_map/ppermute | solution.py:527
  62.3 9.1 %collective-permute-start.15 = (f32[4,176,256]{2,1,0:T(8,128)S(1)}, f32[4,176,256]{2,1,0:T(8,128)S(1)}, u32[]{:S(2)}, u32[]{:S(2)}) collective-permute-start(f32[4,176,256]{2,1,0:T(8,128)S(1)} %get-tuple-element.72.refs_1_), channel_id=1, source_target_pairs={{0,1},{1,0},{2,3},{3,2},{4,5},{5,4},{6,7},{7,6},{8,9},{9,8},{10,11... | collective-permute-start | bytes 2162696 | tf_op jit(solution)/shard_map/ppermute | solution.py:534
  62.4 13.0 %collective-permute-start.16 = (f32[712,256]{1,0:T(8,128)S(1)}, f32[712,256]{1,0:T(8,128)S(1)}, u32[]{:S(2)}, u32[]{:S(2)}) collective-permute-start(f32[712,256]{1,0:T(8,128)S(1)} %get-tuple-element.73), channel_id=1, source_target_pairs={{1,4},{4,1},{3,6},{6,3},{5,8},{8,5},{7,10},{10,7},{9,12},{12,9},{1... | collective-permute-start | bytes 2187272 | tf_op jit(solution)/shard_map/ppermute | solution.py:535
  65.4 9.1 %collective-permute-start.14 = (f32[4,176,256]{2,1,0:T(8,128)S(1)}, f32[4,176,256]{2,1,0:T(8,128)S(1)}, u32[]{:S(2)}, u32[]{:S(2)}) collective-permute-start(f32[4,176,256]{2,1,0:T(8,128)S(1)} %get-tuple-element.63.rest_0_.refs_0_), channel_id=1, source_target_pairs={{0,1},{1,0},{2,3},{3,2},{4,5},{5,4},{6,7},{7,6},{8,9},{9,8},{10,11... | collective-permute-start | bytes 2162696 | tf_op jit(solution)/shard_map/ppermute | solution.py:533
  68.6 17.0 %collective-permute-start.8 = (f32[4,176,256]{2,1,0:T(8,128)S(1)}, f32[4,176,256]{2,1,0:T(8,128)S(1)}, u32[]{:S(2)}, u32[]{:S(2)}) collective-permute-start(f32[4,176,256]{2,1,0:T(8,128)S(1)} %get-tuple-element.65.refs_1_.refs_10_), channel_id=1, source_target_pairs={{0,1},{1,0},{2,3},{3,2},{4,5},{5,4},{6,7},{7,6},{8,9},{9,8},{10,11... | collective-permute-start | bytes 2162696 | tf_op jit(solution)/shard_map/ppermute | solution.py:534
  71.4 14.3 %collective-permute-start.9 = (f32[712,256]{1,0:T(8,128)S(1)}, f32[712,256]{1,0:T(8,128)S(1)}, u32[]{:S(2)}, u32[]{:S(2)}) collective-permute-start(f32[712,256]{1,0:T(8,128)S(1)} %get-tuple-element.66), channel_id=1, source_target_pairs={{1,4},{4,1},{3,6},{6,3},{5,8},{8,5},{7,10},{10,7},{9,12},{12,9},{1... | collective-permute-start | bytes 2187272 | tf_op jit(solution)/shard_map/ppermute | solution.py:535
  74.5 11.2 %collective-permute-start.7 = (f32[4,176,256]{2,1,0:T(8,128)S(1)}, f32[4,176,256]{2,1,0:T(8,128)S(1)}, u32[]{:S(2)}, u32[]{:S(2)}) collective-permute-start(f32[4,176,256]{2,1,0:T(8,128)S(1)} %get-tuple-element.64.refs_0_.refs_10_.refs_9_), channel_id=1, source_target_pairs={{0,1},{1,0},{2,3},{3,2},{4,5},{5,4},{6,7},{7,6},{8,9},{9,8},{10,11... | collective-permute-start | bytes 2162696 | tf_op jit(solution)/shard_map/ppermute | solution.py:533
  78.2 14.6 %collective-permute-start.19 = (f32[712,256]{1,0:T(8,128)S(1)}, f32[712,256]{1,0:T(8,128)S(1)}, u32[]{:S(2)}, u32[]{:S(2)}) collective-permute-start(f32[712,256]{1,0:T(8,128)S(1)} %get-tuple-element.77), channel_id=1, source_target_pairs={{1,4},{4,1},{3,6},{6,3},{5,8},{8,5},{7,10},{10,7},{9,12},{12,9},{1... | collective-permute-start | bytes 2187272 | tf_op jit(solution)/shard_map/ppermute | solution.py:535
  84.1 8.2 %collective-permute-start.17 = (f32[4,176,256]{2,1,0:T(8,128)S(1)}, f32[4,176,256]{2,1,0:T(8,128)S(1)}, u32[]{:S(2)}, u32[]{:S(2)}) collective-permute-start(f32[4,176,256]{2,1,0:T(8,128)S(1)} %get-tuple-element.75.refs_0_), channel_id=1, source_target_pairs={{0,1},{1,0},{2,3},{3,2},{4,5},{5,4},{6,7},{7,6},{8,9},{9,8},{10,11... | collective-permute-start | bytes 2162696 | tf_op jit(solution)/shard_map/ppermute | solution.py:533
  85.7 7.1 %collective-permute-start.18 = (f32[4,176,256]{2,1,0:T(8,128)S(1)}, f32[4,176,256]{2,1,0:T(8,128)S(1)}, u32[]{:S(2)}, u32[]{:S(2)}) collective-permute-start(f32[4,176,256]{2,1,0:T(8,128)S(1)} %get-tuple-element.76.refs_1_), channel_id=1, source_target_pairs={{0,1},{1,0},{2,3},{3,2},{4,5},{5,4},{6,7},{7,6},{8,9},{9,8},{10,11... | collective-permute-start | bytes 2162696 | tf_op jit(solution)/shard_map/ppermute | solution.py:534
  88.5 13.0 %collective-permute-start.13 = (f32[712,256]{1,0:T(8,128)S(1)}, f32[712,256]{1,0:T(8,128)S(1)}, u32[]{:S(2)}, u32[]{:S(2)}) collective-permute-start(f32[712,256]{1,0:T(8,128)S(1)} %get-tuple-element.71), channel_id=1, source_target_pairs={{1,4},{4,1},{3,6},{6,3},{5,8},{8,5},{7,10},{10,7},{9,12},{12,9},{1... | collective-permute-start | bytes 2187272 | tf_op jit(solution)/shard_map/ppermute | solution.py:535
  96.3 19.2 %collective-permute-start.26 = (f32[720,256]{1,0:T(8,128)S(1)}, f32[720,256]{1,0:T(8,128)S(1)}, u32[]{:S(2)}, u32[]{:S(2)}) collective-permute-start(f32[720,256]{1,0:T(8,128)S(1)} %get-tuple-element.89), channel_id=1, source_target_pairs={{0,2},{1,3},{2,0},{3,1},{4,6},{5,7},{6,4},{7,5},{8,10},{9,11},{10,... | collective-permute-start | bytes 2211848 | tf_op jit(solution)/shard_map/ppermute | solution.py:527
  97.5 13.0 %collective-permute-start.25 = (f32[712,256]{1,0:T(8,128)S(1)}, f32[712,256]{1,0:T(8,128)S(1)}, u32[]{:S(2)}, u32[]{:S(2)}) collective-permute-start(f32[712,256]{1,0:T(8,128)S(1)} %get-tuple-element.87), channel_id=1, source_target_pairs={{1,4},{4,1},{3,6},{6,3},{5,8},{8,5},{7,10},{10,7},{9,12},{12,9},{1... | collective-permute-start | bytes 2187272 | tf_op jit(solution)/shard_map/ppermute | solution.py:535
  104.4 13.9 %collective-permute-start.24 = (f32[712,256]{1,0:T(8,128)S(1)}, f32[712,256]{1,0:T(8,128)S(1)}, u32[]{:S(2)}, u32[]{:S(2)}) collective-permute-start(f32[712,256]{1,0:T(8,128)S(1)} %get-tuple-element.85), channel_id=1, source_target_pairs={{1,4},{4,1},{3,6},{6,3},{5,8},{8,5},{7,10},{10,7},{9,12},{12,9},{1... | collective-permute-start | bytes 2187272 | tf_op jit(solution)/shard_map/ppermute | solution.py:535
  114.2 19.7 %collective-permute-start.30 = (f32[720,256]{1,0:T(8,128)S(1)}, f32[720,256]{1,0:T(8,128)S(1)}, u32[]{:S(2)}, u32[]{:S(2)}) collective-permute-start(f32[720,256]{1,0:T(8,128)S(1)} %get-tuple-element.94), channel_id=1, source_target_pairs={{0,2},{1,3},{2,0},{3,1},{4,6},{5,7},{6,4},{7,5},{8,10},{9,11},{10,... | collective-permute-start | bytes 2211848 | tf_op jit(solution)/shard_map/ppermute | solution.py:527
  121.1 12.7 %collective-permute-start.29 = (f32[712,256]{1,0:T(8,128)S(1)}, f32[712,256]{1,0:T(8,128)S(1)}, u32[]{:S(2)}, u32[]{:S(2)}) collective-permute-start(f32[712,256]{1,0:T(8,128)S(1)} %get-tuple-element.92), channel_id=1, source_target_pairs={{1,4},{4,1},{3,6},{6,3},{5,8},{8,5},{7,10},{10,7},{9,12},{12,9},{1... | collective-permute-start | bytes 2187272 | tf_op jit(solution)/shard_map/ppermute | solution.py:535
  136.0 16.0 %collective-permute-start.31 = (f32[4,160,256]{2,1,0:T(8,128)S(1)}, f32[4,160,256]{2,1,0:T(8,128)S(1)}, u32[]{:S(2)}, u32[]{:S(2)}) collective-permute-start(f32[4,160,256]{2,1,0:T(8,128)S(1)} %get-tuple-element.96), channel_id=1, source_target_pairs={{0,2},{1,3},{2,0},{3,1},{4,6},{5,7},{6,4},{7,5},{8,10},{9,11},{10,... | collective-permute-start | bytes 1966088 | tf_op jit(solution)/shard_map/ppermute | solution.py:527
  (21 other events, 116.4 us)

commit v4 on v3

--- a/solution.py
+++ b/solution.py
@@ -71,6 +71,9 @@
         self.moved = (rows * self.wide + 16, depth)
         self.sent = (rows, self.half, depth)
         self.whole = (rows, cols, depth)
+        self.quarter = cols // 4
+        self.quarters = (rows, self.quarter, depth)
+        self.edges = (rows * self.quarter, depth)
 
     def window(self, half):
         return pl.ds(pl.multiple_of(half * (self.half - EXTRA), 16), self.wide)
@@ -130,13 +133,13 @@
             mixed[slot, row] = total
 
 
-def sweep(sizes, refs, mixed, finish):
-    mine0, mine1, other0, other1, beside = refs
+def along_rows(sizes, blocks, mixed, partial):
+    mine0, mine1, other0, other1 = blocks
     rows = sizes.rows
     _, _, core = place()
     orders = (
-        (beside, mine0, other0, mine1, other1),
-        (other0, mine0, other1, mine1, beside),
+        (None, mine0, other0, mine1, other1),
+        (other0, mine0, other1, mine1, None),
     )
     for which, order in enumerate(orders):
 
@@ -146,28 +149,83 @@
 
                 def columns(first):
                     near = [
-                        block[
-                            flat(sizes, row, first)
-                            if block is beside
-                            else (row, cut(first), slice(None))
-                        ]
+                        None if block is None else block[row, cut(first), :]
                         for block in order[2 * slot : 2 * slot + 3]
                         for row in range(rows)
                     ]
                     for row in range(rows):
-                        centre = near[rows + row]
-                        parts = [
-                            WEIGHTS[offset]
-                            * (near[rows + row + offset] + near[rows + row - offset])
-                            for offset in range(1, REACH + 1)
-                        ]
-                        total = (parts[0] + parts[1]) + (parts[2] + parts[3])
-                        total = total + (
-                            3.0 * WEIGHTS[0] * centre + mixed[slot, row, cut(first), :]
-                        )
-                        finish(which, slot, row, first, centre, total)
+                        parts = []
+                        for offset in range(1, REACH + 1):
+                            pair = (near[rows + row + offset], near[rows + row - offset])
+                            pair = [value for value in pair if value is not None]
+                            if pair:
+                                parts.append(WEIGHTS[offset] * sum(pair[1:], pair[0]))
+                        total = 3.0 * WEIGHTS[0] * near[rows + row]
+                        total = total + mixed[slot, row, cut(first), :]
+                        partial[slot, row, cut(first), :] = sum(parts[1:], parts[0]) + total
 
                 over_columns(sizes, columns)
+
+
+def prepare(sizes, blocks, name, inject=None, settled=()):
+    def body(*refs):
+        b_refs = refs[:4]
+        partial, mixed = refs[-2:]
+        added = None
+        if inject is not None:
+            step_no = inject[0]
+            cells_ref, samples_ref = refs[4:6]
+            level, half, core = place()
+            where_x, where_y, where_z = (cells_ref[0, axis : axis + 1, :] for axis in range(3))
+            count = where_x.shape[1]
+            values = jnp.where(
+                where_z == iota((sizes.depth, count), 0),
+                samples_ref[0, step_no - 1 : step_no, :],
+                0.0,
+            )
+            values = jnp.concatenate(two_terms(values), 1)
+            col_ids = iota((sizes.wide, count), 0) + half * (sizes.half - EXTRA)
+
+            def added(slot, row):
+                this_row = ((level * 2 + slot) * 2 + core) * sizes.rows + row
+                col_of = jnp.where(where_x == this_row, where_y, -1)
+                hit = jnp.where(col_of == col_ids, 1.0, 0.0).astype(BF16)
+                return dot(jnp.concatenate((hit, hit), 1), values, ((1,), (1,)))
+
+        differences(sizes, b_refs, mixed, added)
+        along_rows(sizes, b_refs, mixed, partial)
+
+    operands = (*blocks, *(inject[1:] if inject is not None else ()))
+    specs = [VMEM] * len(operands) + [ANY] * len(settled)
+    return run(
+        body,
+        name,
+        (*operands, *settled),
+        specs,
+        [(sizes.pair, VMEM)],
+        [sizes.pair],
+    )[0]
+
+
+def sweep(sizes, partial, beside, finish):
+    rows = sizes.rows
+    _, _, core = place()
+    for which in range(2):
+
+        @pl.when(core == which)
+        def _():
+            def columns(first):
+                far = [beside[flat(sizes, row, first)] for row in range(rows)]
+                for slot in range(2):
+                    for row in range(rows):
+                        total = partial[slot, row, cut(first), :]
+                        for offset in range(1, REACH + 1):
+                            at = row + offset - rows if which else row - offset + rows
+                            if slot == which and 0 <= at < rows:
+                                total = total + WEIGHTS[offset] * far[at]
+                        finish(which, slot, row, first, total)
+
+            over_columns(sizes, columns)
 
 
 def run(body, name, operands, specs, outs, scratch=(), aliases=None, limit=24, sems=0):
@@ -204,7 +262,7 @@
         (velocity, traces),
         [ANY, VMEM],
         [(sizes.moved, VMEM)],
-        limit=PACK_LIMIT,
+        limit=16,
         sems=1,
     )
 
@@ -306,42 +364,24 @@
     )
 
 
-def adjoint_step(sizes, step_no, scaled, later, latest, speed, cells, samples, settled=()):
+def adjoint_step(sizes, step_no, partial, beside, later, latest, speed, settled=()):
     split = len(latest) == 2
     more = step_no > 1
     ends = step_no <= 2
 
     def body(*refs):
         refs = list(refs)
-        u_refs, (later_ref, v_ref, cells_ref, samples_ref) = refs[:5], refs[5:9]
-        latest_refs, refs = refs[9 : 9 + len(latest)], refs[9 + len(latest) + len(settled) :]
+        partial_ref, beside_ref, later_ref, v_ref = refs[:4]
+        latest_refs, refs = refs[4 : 4 + len(latest)], refs[4 + len(latest) + len(settled) :]
         if more:
             (next_out, u0_out, u1_out, z_out), refs = refs[:4], refs[4:]
         if ends:
             (kept_out, sent_out), refs = refs[:2], refs[2:]
-        mixed = refs.pop(0)
         if not more:
             next_out = refs.pop(0)
-        level, half, core = place()
-        where_x, where_y, where_z = (cells_ref[0, axis : axis + 1, :] for axis in range(3))
-        count = where_x.shape[1]
-        values = jnp.where(
-            where_z == iota((sizes.depth, count), 0),
-            samples_ref[0, step_no - 1 : step_no, :],
-            0.0,
-        )
-        values = jnp.concatenate(two_terms(values), 1)
-        col_ids = iota((sizes.wide, count), 0) + half * (sizes.half - EXTRA)
-
-        def added(slot, row):
-            this_row = ((level * 2 + slot) * 2 + core) * sizes.rows + row
-            col_of = jnp.where(where_x == this_row, where_y, -1)
-            hit = jnp.where(col_of == col_ids, 1.0, 0.0).astype(BF16)
-            return dot(jnp.concatenate((hit, hit), 1), values, ((1,), (1,)))
-
-        differences(sizes, u_refs, mixed, added)
-
-        def finish(which, slot, row, first, centre, total):
+        _, half, _ = place()
+
+        def finish(which, slot, row, first, total):
             at = (slot, row, cut(first), slice(None))
             if split:
                 last = merged(sizes, *latest_refs, slot, row, first)
@@ -356,7 +396,7 @@
                 if which == slot:
                     z_out[flat(sizes, row, first)] = value
 
-        sweep(sizes, u_refs, mixed, finish)
+        sweep(sizes, partial_ref, beside_ref, finish)
         if ends:
             kept_out[...] = next_out[half, :, sizes.own(half), :]
             for row in range(sizes.rows):
@@ -374,10 +414,10 @@
     return run(
         body,
         f"adjoint_{step_no}",
-        (*scaled, later, speed, cells, samples, *latest, *settled),
-        [VMEM] * (9 + len(latest)) + [ANY] * len(settled),
+        (partial, beside, later, speed, *latest, *settled),
+        [VMEM] * (4 + len(latest)) + [ANY] * len(settled),
         outs,
-        [sizes.pair] * (1 if more else 2),
+        [] if more else [sizes.pair],
     )
 
 
@@ -404,56 +444,43 @@
     )
 
 
-def forward_step(sizes, step_no, current, before, speed, later, gradient, source, settled=()):
+def forward_step(
+    sizes, step_no, partial, current, before, speed, later, gradient, source, settled=()
+):
     first_step = step_no == 1
-    more = step_no < STEPS
+    last_step = step_no == STEPS - 1
 
     def body(*refs):
         refs = list(refs)
-        c_refs, v_ref, refs = refs[:5], refs[5], refs[6:]
+        partial_ref, c_refs, beside_ref, v_ref, refs = refs[0], refs[1:3], refs[3], refs[4], refs[5:]
         late, refs = refs[: len(later)], refs[len(later) :]
         if not first_step:
             g_ref, refs = refs[0], refs[1:]
-        if more:
-            before_refs, refs = refs[:2], refs[2:]
-            (cells_ref, wavelet_ref, start_ref), refs = refs[:3], refs[3:]
-        refs = refs[len(settled) :]
-        if more:
-            (c0_out, c1_out, z_out, g_out), refs = refs[:4], refs[4:]
-        else:
-            (kept_out, sent_out), refs = refs[:2], refs[2:]
-        mixed = refs.pop(0)
-        if not more:
-            g_out = refs.pop(0)
+        before_refs, refs = refs[:2], refs[2:]
+        (cells_ref, wavelet_ref, start_ref), refs = refs[:3], refs[3:]
+        c0_out, c1_out, g_out, *z_outs = refs[len(settled) :]
         level, half, core = place()
-        differences(sizes, c_refs, mixed)
-
-        def finish(which, slot, row, first, centre, total):
+
+        def finish(which, slot, row, first, total):
             at = (slot, row, cut(first), slice(None))
             if first_step:
                 g_out[at] = total
             elif step_no == 2:
                 g_out[at] = late[0][at] * g_ref[at] + late[1][at] * total
-            elif more:
+            else:
                 g_out[at] = g_ref[at] + late[0][at] * total
+            if first_step:
+                last = merged(sizes, *before_refs, slot, row, first)
             else:
-                g_out[at] = 2.0 * v_ref[at] * (g_ref[at] + late[0][at] * total)
-            if more:
-                if first_step:
-                    last = merged(sizes, *before_refs, slot, row, first)
-                else:
-                    last = before_refs[slot][row, cut(first), :]
-                here = v_ref[at]
-                value = 2.0 * centre - last + here * here * total
-                (c0_out, c1_out)[slot][row, cut(first), :] = value
-                if which == slot:
-                    z_out[flat(sizes, row, first)] = value
-
-        sweep(sizes, c_refs, mixed, finish)
-        if not more:
-            kept_out[...] = g_out[half, :, sizes.own(half), :]
-            sent_out[...] = g_out[1 - half, :, sizes.own(half), :]
-            return
+                last = before_refs[slot][row, cut(first), :]
+            here = v_ref[at]
+            centre = c_refs[slot][row, cut(first), :]
+            value = 2.0 * centre - last + here * here * total
+            (c0_out, c1_out)[slot][row, cut(first), :] = value
+            if which == slot and not last_step:
+                z_outs[0][flat(sizes, row, first)] = value
+
+        sweep(sizes, partial_ref, beside_ref, finish)
         col = cells_ref[0, 1] - half * (sizes.half - EXTRA)
         pulse = wavelet_ref[0, start_ref[0] + step_no]
         for slot, c_out in enumerate((c0_out, c1_out)):
@@ -465,30 +492,100 @@
                 out[at] = out[at] + jnp.where(hit, pulse, 0.0)
 
             pl.when(inside)(functools.partial(put, c_out, (row, pl.ds(col, 1), slice(None))))
-            pl.when(inside & (core == slot))(
-                functools.partial(put, z_out, (pl.ds(col + row * sizes.wide, 1), slice(None)))
-            )
-
-    operands = (*current, speed, *later)
+            if last_step:
+
+                @pl.when(core == slot)
+                def _():
+                    for part, z_out in enumerate(z_outs):
+                        here = pl.ds(
+                            pl.multiple_of(half * EXTRA + part * sizes.quarter, 16), sizes.quarter
+                        )
+                        for line in range(sizes.rows):
+                            z_out[pl.ds(line * sizes.quarter, sizes.quarter), :] = c_out[
+                                line, here, :
+                            ]
+
+            else:
+                pl.when(inside & (core == slot))(
+                    functools.partial(
+                        put, z_outs[0], (pl.ds(col + row * sizes.wide, 1), slice(None))
+                    )
+                )
+
+    operands = (partial, *current, speed, *later)
     if not first_step:
         operands += (gradient,)
-    if more:
-        operands += before
-    specs = [VMEM] * len(operands)
-    if more:
-        operands += source
-        specs += [SMEM] * 3
-        outs = [(sizes.block, VMEM)] * 2 + [(sizes.edge, VMEM), (sizes.pair, VMEM)]
-    else:
-        outs = [(sizes.sent, VMEM)] * 2
-    return run(
-        body,
-        f"forward_{step_no}",
-        (*operands, *settled),
-        specs + [ANY] * len(settled),
-        outs,
-        [sizes.pair] * (1 if more else 2),
-    )
+    operands += before
+    specs = [VMEM] * len(operands) + [SMEM] * 3 + [ANY] * len(settled)
+    outs = [(sizes.block, VMEM)] * 2 + [(sizes.pair, VMEM)]
+    outs += [(sizes.edges, VMEM)] * 2 if last_step else [(sizes.edge, VMEM)]
+    return run(body, f"forward_{step_no}", (*operands, *source, *settled), specs, outs)
+
+
+def forward_end(sizes, part, partial, beside, speed, later, gradient, settled=()):
+    def body(partial_ref, beside_ref, v_ref, later_ref, g_ref, *rest):
+        kept_out, sent_out, both = rest[len(settled) :]
+        _, half, core = place()
+        rows = sizes.rows
+        for which in range(2):
+
+            @pl.when(core == which)
+            def _():
+                @pl.loop(0, sizes.quarter // 8)
+                def _(step):
+                    local = pl.multiple_of(step * 8, 8)
+                    first = pl.multiple_of(half * EXTRA + part * sizes.quarter + local, 8)
+                    far = [
+                        beside_ref[pl.ds(pl.multiple_of(local + row * sizes.quarter, 8), 8), :]
+                        for row in range(rows)
+                    ]
+                    for slot in range(2):
+                        for row in range(rows):
+                            at = (slot, row, cut(first), slice(None))
+                            total = partial_ref[at]
+                            for offset in range(1, REACH + 1):
+                                line = row + offset - rows if which else row - offset + rows
+                                if slot == which and 0 <= line < rows:
+                                    total = total + WEIGHTS[offset] * far[line]
+                            total = g_ref[at] + later_ref[at] * total
+                            both[slot, row, cut(local), :] = 2.0 * v_ref[at] * total
+
+        kept_out[...] = both[half]
+        sent_out[...] = both[1 - half]
+
+    return run(
+        body,
+        f"forward_end_{part}",
+        (partial, beside, speed, later, gradient, *settled),
+        [VMEM] * 5 + [ANY] * len(settled),
+        [(sizes.quarters, VMEM)] * 2,
+        [(2, *sizes.quarters)],
+    )
+
+
+def fill_gradient(sizes, parts, whole=None):
+    arrays = [array for _, _, array in parts]
+    given = () if whole is None else (whole,)
+
+    def body(*refs):
+        out, sems = refs[-2], refs[-1]
+        _, half, _ = place()
+        copies = Copies(sems)
+        for (part, received, _), ref in zip(parts, refs):
+            side = 1 - half if received else half
+            first = pl.multiple_of(side * sizes.half + part * sizes.quarter, 16)
+            copies.start(ref, out.at[:, pl.ds(first, sizes.quarter), :])
+        copies.wait()
+
+    return run(
+        body,
+        f"fill_gradient_{len(given)}",
+        (*arrays, *given),
+        [ANY] * (len(arrays) + len(given)),
+        [(sizes.whole, ANY)],
+        aliases={len(arrays): 0} if given else None,
+        sems=len(parts),
+    )[0]
 
 
 def fill(sizes, shape, parts, name):
@@ -547,38 +644,72 @@
     samples = lax.dynamic_slice_in_dim(samples, start_step[0] + 1, STEPS, 1)
 
     adjoint = functools.partial(adjoint_step, sizes)
-    common = (speed, receiver_cells, samples)
     forward = functools.partial(forward_step, sizes)
     source = (source_cells, wavelet, start_step)
+
+    def ready(step_no, blocks, settled=()):
+        return prepare(
+            sizes,
+            blocks[:4],
+            f"prepare_adjoint_{step_no}",
+            (step_no, receiver_cells, samples),
+            settled,
+        )
+
+    def ready_forward(step_no, blocks, settled=()):
+        partial = prepare(
+            sizes, blocks[:4], f"prepare_forward_{step_no}", settled=settled
+        )
+        return partial, (*blocks[:2], blocks[4])
+
     later4, *scaled = adjoint_begin(sizes, speed, kept[1], later_in, samples)
-    later3, *scaled = adjoint(4, exchange(*scaled), later4, (kept[2], latest_in), *common)
+    scaled = exchange(*scaled)
+    later3, *scaled = adjoint(
+        4, ready(4, scaled), scaled[4], later4, (kept[2], latest_in), speed
+    )
     scaled = exchange(*scaled)
     current1 = exchange(*forward_begin(sizes, kept[3], current_in, scaled[:1]))
-    later2, *scaled = adjoint(3, scaled, later3, (later4,), *common, current1[:1])
+    later2, *scaled = adjoint(
+        3, ready(3, scaled, scaled[4:]), scaled[4], later3, (later4,), speed, current1[:1]
+    )
     scaled = exchange(*scaled)
-    *current2, image = forward(
-        1, current1, (kept[4], before_in), speed, (), None, source
-    )
-    current2 = exchange(*current2)
+    *current2, image, edge = forward(
+        1, *ready_forward(1, current1, (before_in,)), (kept[4], before_in), speed, (), None, source
+    )
+    current2 = exchange(*current2, edge)
     later1, *scaled, mine1, sent1 = adjoint(
-        2, scaled, later2, (later3,), *common, current2[:1]
+        2, ready(2, scaled), scaled[4], later2, (later3,), speed, current2[:1]
     )
     got1 = over(sent1)
     scaled = exchange(*scaled)
-    *current3, gradient = forward(
-        2, current2, current1[:2], speed, (later1, later2), image, source, scaled[2:4]
-    )
-    current3 = exchange(*current3)
-    mine0, sent0 = adjoint(
-        1, scaled, later1, (later2,), *common, current3[2:4]
-    )
+    partial = ready(1, scaled)
+    *current3, gradient, edge = forward(
+        2,
+        *ready_forward(2, current2),
+        current1[:2],
+        speed,
+        (later1, later2),
+        image,
+        source,
+        scaled[2:4],
+    )
+    current3 = exchange(*current3, edge)
+    prepared = ready_forward(3, current3)
+    mine0, sent0 = adjoint(1, partial, scaled[4], later1, (later2,), speed, current3[2:4])
     got0 = over(sent0)
-    *current4, gradient = forward(
-        3, current3, current2[:2], speed, (later3,), gradient, source, (mine0, got1)
-    )
-    mine, sent = forward(4, exchange(*current4), (), speed, (later4,), gradient, None, (got0,))
-    got = over(sent)
-    return fill(sizes, sizes.whole, [mine, got], "fill_gradient"), fill(
+    *current4, gradient, edge0, edge1 = forward(
+        3, *prepared, current2[:2], speed, (later3,), gradient, source, (mine0, got1)
+    )
+    *current4, beside0 = exchange(*current4, edge0)
+    beside1 = lax.ppermute(edge1, "gx", levels)
+    partial, _ = ready_forward(4, (*current4, beside0))
+    ends = functools.partial(forward_end, sizes)
+    kept0, sent = ends(0, partial, beside0, speed, later4, gradient)
+    moved0 = over(sent)
+    kept1, sent = ends(1, partial, beside1, speed, later4, gradient, (kept0, got0))
+    moved1 = over(sent)
+    total = fill_gradient(sizes, [(0, False, kept0), (1, False, kept1), (0, True, moved0)])
+    return fill_gradient(sizes, [(1, True, moved1)], total), fill(
         sizes, adjoint_state.shape, [mine0, got0, mine1, got1], "fill_adjoint"
     )
 

time: 156 us -> 149 us (0.955); the launches traced: 153 us -> 148 us
  waiting for transfers between devices: 50.4 us -> 42.8 us
  starting transfers between devices: 40.9 us -> 44 us
    ppermute x8, waiting for transfers between devices: 16.3 us -> 4.87 us  [exchange(): lax.ppermute(edge, 'gx', levels)]
    ppermute x8 -> x9, waiting for transfers between devices: 30.4 us -> 35.5 us  [over(): return lax.ppermute(field, 'gx', across)]
    ppermute x8, starting transfers between devices: 3.29 us -> 5.78 us  [exchange(): lax.ppermute(block0, 'gx', cores)]
    ppermute x0 -> x1, starting transfers between devices: none -> 2.34 us  [on_device(): beside1 = lax.ppermute(edge1, 'gx', levels)]
    ppermute x8, starting transfers between devices: 4.32 us -> 2.32 us  [exchange(): lax.ppermute(block1, 'gx', cores)]
    ppermute x8, waiting for transfers between devices: 1.91 us -> 0.02 us  [exchange(): lax.ppermute(block1, 'gx', cores)]
    ppermute x0 -> x1, waiting for transfers between devices: none -> 1.89 us  [on_device(): beside1 = lax.ppermute(edge1, 'gx', levels)]
    ppermute x8 -> x9, starting transfers between devices: 8.08 us -> 9.86 us  [over(): return lax.ppermute(field, 'gx', across)]
  transfers between devices with their start and end apart: 32 -> 34, of which waited for: 14 -> 12; matrix products, arithmetic and copies ran while one was open for 0% -> 0% of each run, Pallas kernels for 21% -> 24%
where the time goes in v4:
time: 149 us; the launch traced here: 148 us
  starting transfers between devices  44 us (30%)
  waiting for transfers between devices  42.8 us (29%)
  Pallas kernels  36.8 us (25%)
  blocking collectives  17.1 us (11%)
  local copies, waits for them, and re-layouts  5.32 us (4%)
  between operations  1.98 us (1%)
    pallas_call x26, Pallas kernels, run(): pl.pallas_call(body, name=name, out_shape=[jax.ShapeDtypeStruct(shape, F3...  36.8 us
    ppermute x9, waiting for transfers between devices, over(): return lax.ppermute(field, 'gx', across)  35.5 us
    ppermute x8, starting transfers between devices, exchange(): lax.ppermute(edge, 'gx', levels)  23.7 us
    all_gather x1, blocking collectives, on_device(): tails = lax.all_gather(tails, 'gx', axis_index_groups=halves)  17.1 us
    ppermute x9, starting transfers between devices, over(): return lax.ppermute(field, 'gx', across)  9.86 us
    ppermute x8, starting transfers between devices, exchange(): lax.ppermute(block0, 'gx', cores)  5.78 us
    unnamed x30, local copies, waits for them, and re-layouts  5.21 us
    ppermute x8, waiting for transfers between devices, exchange(): lax.ppermute(edge, 'gx', levels)  4.87 us
  transfers between devices with their start and end apart: 34, of which 12 were waited for; matrix products, arithmetic and copies ran while one was open for 0% of the time, Pallas kernels for 24%

profile of v4, /device:TPU:11, one launch (start us, length us, event | category | flops | bytes accessed | tf_op | source)
XLA Modules:
  0.0 148.1 jit_solution(11746509587561339598)
XLA Ops:
  4.1 3.4 %pack.1 = (f32[720,256]{1,0:T(8,128)}, f32[720,256]{1,0:T(8,128)}, f32[720,256]{1,0:T(8,128)}, f32[720,256]{1,0:T(8,128)}) custom-call(f32[2,1,4,320,256]{4,3,2,1,0:T(8,128)} %a_ref.3, f32[2,1,4,320,256]{4,3,2,1,0:T(8,128)} %w_ref.3), custom_call_target="tpu_custom_call" | custom-call | tf_op jit(solution)/shard_map/pack/pallas_call | solution.py:232
  9.0 3.8 %keep.1 = (f32[4,176,256]{2,1,0:T(8,128)}, f32[4,176,256]{2,1,0:T(8,128)}, f32[4,176,256]{2,1,0:T(8,128)}, f32[4,176,256]{2,1,0:T(8,128)}, f32[4,176,256]{2,1,0:T(8,128)}) custom-call(f32[4,320,256]{2,1,0:T(8,128)} %field.1, f32[2,1,4,320,256]{4,3,2,1,0:T(8,128)} %a_ref.3, f32[2,1,4,320,256]{4,3,2,1,0:T(8,128)} %w_ref.3), custom_call_target="tpu_custom_call" | custom-call | tf_op jit(solution)/shard_map/keep/pallas_call | solution.py:232
  13.4 6.7 %collective-permute-done.1.moved_ref = f32[720,256]{1,0:T(8,128)S(1)} collective-permute-done((f32[720,256]{1,0:T(8,128)S(1)}, f32[720,256]{1,0:T(8,128)S(1)}, u32[]{:S(2)}, u32[]{:S(2)}) %collective-permute-start.1) | collective-permute-done | bytes 737312 | tf_op jit(solution)/shard_map/ppermute | solution.py:624
  23.5 17.1 %all-gather = f32[16,16,256]{2,1,0:T(8,128)S(1)} all-gather(f32[2,16,256]{2,1,0:T(8,128)S(1)} %get-tuple-element.59), channel_id=2, replica_groups={{0,1,4,5,8,9,12,13},{2,3,6,7,10,11,14,15},{16,17,20,21,24,25,28,29},{18..., dimensions={0}, use_global_device_ids=true | all-gather | bytes 294912 | tf_op jit(solution)/shard_map/all_gather | solution.py:641
  42.4 1.9 %collective-permute-start.5 = (f32[712,256]{1,0:T(8,128)S(1)}, f32[712,256]{1,0:T(8,128)S(1)}, u32[]{:S(2)}, u32[]{:S(2)}) collective-permute-start(f32[712,256]{1,0:T(8,128)S(1)} %get-tuple-element.62), channel_id=1, source_target_pairs={{1,4},{4,1},{3,6},{6,3},{5,8},{8,5},{7,10},{10,7},{9,12},{12,9},{1... | collective-permute-start | bytes 2187272 | tf_op jit(solution)/shard_map/ppermute | solution.py:632
  48.1 2.5 %prepare_adjoint_4.1.refs_0_ = f32[2,4,176,256]{3,2,1,0:T(8,128)S(1)} custom-call(f32[4,176,256]{2,1,0:T(8,128)S(1)} %get-tuple-element.60.refs_0_, f32[4,176,256]{2,1,0:T(8,128)S(1)} %get-tuple-element.61.refs_1_, f32[4,176,256]{2,1,0:T(8,128)S(1)} %collective-permute-done.3.refs_2_, f32[4,176,256]{2,1,0:T(8,128)S(1)} %collective-permute-done.4.refs_3_, ...), custom_call_target="tpu_custom_call" | custom-call | tf_op jit(solution)/shard_map/prepare_adjoint_4/pallas_call | solution.py:232
  51.8 3.6 %collective-permute-done.5.refs_1_ = f32[712,256]{1,0:T(8,128)S(1)} collective-permute-done((f32[712,256]{1,0:T(8,128)S(1)}, f32[712,256]{1,0:T(8,128)S(1)}, u32[]{:S(2)}, u32[]{:S(2)}) %collective-permute-start.5) | collective-permute-done | bytes 729120 | tf_op jit(solution)/shard_map/ppermute | solution.py:632
  56.0 2.3 %collective-permute-start.16 = (f32[712,256]{1,0:T(8,128)S(1)}, f32[712,256]{1,0:T(8,128)S(1)}, u32[]{:S(2)}, u32[]{:S(2)}) collective-permute-start(f32[712,256]{1,0:T(8,128)S(1)} %get-tuple-element.76), channel_id=1, source_target_pairs={{1,4},{4,1},{3,6},{6,3},{5,8},{8,5},{7,10},{10,7},{9,12},{12,9},{1... | collective-permute-start | bytes 2187272 | tf_op jit(solution)/shard_map/ppermute | solution.py:632
  58.9 8.7 %collective-permute-done.moved_ref = f32[720,256]{1,0:T(8,128)S(1)} collective-permute-done((f32[720,256]{1,0:T(8,128)S(1)}, f32[720,256]{1,0:T(8,128)S(1)}, u32[]{:S(2)}, u32[]{:S(2)}) %collective-permute-start) | collective-permute-done | bytes 737312 | tf_op jit(solution)/shard_map/ppermute | solution.py:624
  67.9 2.8 %collective-permute-start.7 = (f32[4,176,256]{2,1,0:T(8,128)S(1)}, f32[4,176,256]{2,1,0:T(8,128)S(1)}, u32[]{:S(2)}, u32[]{:S(2)}) collective-permute-start(f32[4,176,256]{2,1,0:T(8,128)S(1)} %get-tuple-element.67.refs_0_.refs_1_.refs_5_.refs_8_), channel_id=1, source_target_pairs={{0,1},{1,0},{2,3},{3,2},{4,5},{5,4},{6,7},{7,6},{8,9},{9,8},{10,11... | collective-permute-start | bytes 2162696 | tf_op jit(solution)/shard_map/ppermute | solution.py:630
  70.7 3.1 %collective-permute-start.10 = (f32[712,256]{1,0:T(8,128)S(1)}, f32[712,256]{1,0:T(8,128)S(1)}, u32[]{:S(2)}, u32[]{:S(2)}) collective-permute-start(f32[712,256]{1,0:T(8,128)S(1)} %get-tuple-element.70), channel_id=1, source_target_pairs={{1,4},{4,1},{3,6},{6,3},{5,8},{8,5},{7,10},{10,7},{9,12},{12,9},{1... | collective-permute-start | bytes 2187272 | tf_op jit(solution)/shard_map/ppermute | solution.py:632
  73.9 2.5 %prepare_adjoint_3.1.refs_0_ = f32[2,4,176,256]{3,2,1,0:T(8,128)S(1)} custom-call(f32[4,176,256]{2,1,0:T(8,128)S(1)} %get-tuple-element.66.rest_0_.refs_0_, f32[4,176,256]{2,1,0:T(8,128)S(1)} %get-tuple-element.75.refs_1_, f32[4,176,256]{2,1,0:T(8,128)S(1)} %collective-permute-done.14.refs_2_, f32[4,176,256]{2,1,0:T(8,128)S(1)} %collective-permute-done.15.refs_3_, ...), custom_call_target="tpu_custom_call" | custom-call | tf_op jit(solution)/shard_map/prepare_adjoint_3/pallas_call | solution.py:232
  76.9 3.6 %collective-permute-start.19 = (f32[712,256]{1,0:T(8,128)S(1)}, f32[712,256]{1,0:T(8,128)S(1)}, u32[]{:S(2)}, u32[]{:S(2)}) collective-permute-start(f32[712,256]{1,0:T(8,128)S(1)} %get-tuple-element.80), channel_id=1, source_target_pairs={{1,4},{4,1},{3,6},{6,3},{5,8},{8,5},{7,10},{10,7},{9,12},{12,9},{1... | collective-permute-start | bytes 2187272 | tf_op jit(solution)/shard_map/ppermute | solution.py:632
  80.6 2.8 %collective-permute-done.9.refs_4_.refs_6_ = f32[720,256]{1,0:T(8,128)S(1)} collective-permute-done((f32[720,256]{1,0:T(8,128)S(1)}, f32[720,256]{1,0:T(8,128)S(1)}, u32[]{:S(2)}, u32[]{:S(2)}) %collective-permute-start.9) | collective-permute-done | bytes 737312 | tf_op jit(solution)/shard_map/ppermute | solution.py:624
  88.1 3.6 %collective-permute-start.13 = (f32[712,256]{1,0:T(8,128)S(1)}, f32[712,256]{1,0:T(8,128)S(1)}, u32[]{:S(2)}, u32[]{:S(2)}) collective-permute-start(f32[712,256]{1,0:T(8,128)S(1)} %get-tuple-element.74), channel_id=1, source_target_pairs={{1,4},{4,1},{3,6},{6,3},{5,8},{8,5},{7,10},{10,7},{9,12},{12,9},{1... | collective-permute-start | bytes 2187272 | tf_op jit(solution)/shard_map/ppermute | solution.py:632
  92.3 2.5 %prepare_adjoint_2.1.refs_0_ = f32[2,4,176,256]{3,2,1,0:T(8,128)S(1)} custom-call(f32[4,176,256]{2,1,0:T(8,128)S(1)} %get-tuple-element.78.refs_0_, f32[4,176,256]{2,1,0:T(8,128)S(1)} %get-tuple-element.79.refs_1_, f32[4,176,256]{2,1,0:T(8,128)S(1)} %collective-permute-done.17.refs_2_, f32[4,176,256]{2,1,0:T(8,128)S(1)} %collective-permute-done.18.refs_3_, ...), custom_call_target="tpu_custom_call" | custom-call | tf_op jit(solution)/shard_map/prepare_adjoint_2/pallas_call | solution.py:232
  96.1 3.2 %collective-permute-start.25 = (f32[712,256]{1,0:T(8,128)S(1)}, f32[712,256]{1,0:T(8,128)S(1)}, u32[]{:S(2)}, u32[]{:S(2)}) collective-permute-start(f32[712,256]{1,0:T(8,128)S(1)} %get-tuple-element.90), channel_id=1, source_target_pairs={{1,4},{4,1},{3,6},{6,3},{5,8},{8,5},{7,10},{10,7},{9,12},{12,9},{1... | collective-permute-start | bytes 2187272 | tf_op jit(solution)/shard_map/ppermute | solution.py:632
  104.5 2.8 %collective-permute-start.24 = (f32[712,256]{1,0:T(8,128)S(1)}, f32[712,256]{1,0:T(8,128)S(1)}, u32[]{:S(2)}, u32[]{:S(2)}) collective-permute-start(f32[712,256]{1,0:T(8,128)S(1)} %get-tuple-element.88), channel_id=1, source_target_pairs={{1,4},{4,1},{3,6},{6,3},{5,8},{8,5},{7,10},{10,7},{9,12},{12,9},{1... | collective-permute-start | bytes 2187272 | tf_op jit(solution)/shard_map/ppermute | solution.py:632
  107.3 2.5 %prepare_adjoint_1.1.refs_0_ = f32[2,4,176,256]{3,2,1,0:T(8,128)S(1)} custom-call(f32[4,176,256]{2,1,0:T(8,128)S(1)} %get-tuple-element.84.refs_0_, f32[4,176,256]{2,1,0:T(8,128)S(1)} %get-tuple-element.85.refs_1_, f32[4,176,256]{2,1,0:T(8,128)S(1)} %collective-permute-done.20.refs_13_.refs_2_, f32[4,176,256]{2,1,0:T(8,128)S(1)} %collective-permute-done.21.refs_14_.refs_3_, ...), custom_call_target="tpu_custom_call" | custom-call | tf_op jit(solution)/shard_map/prepare_adjoint_1/pallas_call | solution.py:232
  112.9 5.0 %collective-permute-done.26.refs_13_.refs_3_ = f32[720,256]{1,0:T(8,128)S(1)} collective-permute-done((f32[720,256]{1,0:T(8,128)S(1)}, f32[720,256]{1,0:T(8,128)S(1)}, u32[]{:S(2)}, u32[]{:S(2)}) %collective-permute-start.26) | collective-permute-done | bytes 737312 | tf_op jit(solution)/shard_map/ppermute | solution.py:624
  119.8 3.2 %collective-permute-start.30 = (f32[320,256]{1,0:T(8,128)S(1)}, f32[320,256]{1,0:T(8,128)S(1)}, u32[]{:S(2)}, u32[]{:S(2)}) collective-permute-start(f32[320,256]{1,0:T(8,128)S(1)} %get-tuple-element.97), channel_id=1, source_target_pairs={{1,4},{4,1},{3,6},{6,3},{5,8},{8,5},{7,10},{10,7},{9,12},{12,9},{1... | collective-permute-start | bytes 983048 | tf_op jit(solution)/shard_map/ppermute | solution.py:632
  123.0 2.3 %collective-permute-start.29 = (f32[320,256]{1,0:T(8,128)S(1)}, f32[320,256]{1,0:T(8,128)S(1)}, u32[]{:S(2)}, u32[]{:S(2)}) collective-permute-start(f32[320,256]{1,0:T(8,128)S(1)} %get-tuple-element.95), channel_id=1, source_target_pairs={{1,4},{4,1},{3,6},{6,3},{5,8},{8,5},{7,10},{10,7},{9,12},{12,9},{1... | collective-permute-start | bytes 983048 | tf_op jit(solution)/shard_map/ppermute | solution.py:704
  136.8 3.9 %collective-permute-done.33.refs_2_ = f32[4,80,256]{2,1,0:T(8,128)S(1)} collective-permute-done((f32[4,80,256]{2,1,0:T(8,128)S(1)}, f32[4,80,256]{2,1,0:T(8,128)S(1)}, u32[]{:S(2)}, u32[]{:S(2)}) %collective-permute-start.33) | collective-permute-done | bytes 327712 | tf_op jit(solution)/shard_map/ppermute | solution.py:624
  141.7 5.5 %collective-permute-done.32.refs_0_ = f32[4,80,256]{2,1,0:T(8,128)S(1)} collective-permute-done((f32[4,80,256]{2,1,0:T(8,128)S(1)}, f32[4,80,256]{2,1,0:T(8,128)S(1)}, u32[]{:S(2)}, u32[]{:S(2)}) %collective-permute-start.32) | collective-permute-done | bytes 327712 | tf_op jit(solution)/shard_map/ppermute | solution.py:624
  (104 shorter events, 46.8 us)
Async XLA Ops:
  2.8 17.4 %collective-permute-start.1 = (f32[720,256]{1,0:T(8,128)S(1)}, f32[720,256]{1,0:T(8,128)S(1)}, u32[]{:S(2)}, u32[]{:S(2)}) collective-permute-start(f32[720,256]{1,0:T(8,128)S(1)} %pack_first.1.sent_ref), channel_id=1, source_target_pairs={{0,2},{1,3},{2,0},{3,1},{4,6},{5,7},{6,4},{7,5},{8,10},{9,11},{10,... | collective-permute-start | bytes 2211848 | tf_op jit(solution)/shard_map/ppermute | solution.py:624
  7.5 33.3 %collective-permute-start.2 = (f32[720,256]{1,0:T(8,128)}, f32[720,256]{1,0:T(8,128)}, u32[]{:S(2)}, u32[]{:S(2)}) collective-permute-start(f32[720,256]{1,0:T(8,128)} %get-tuple-element.58), channel_id=1, source_target_pairs={{0,2},{1,3},{2,0},{3,1},{4,6},{5,7},{6,4},{7,5},{8,10},{9,11},{10,... | collective-permute-start | bytes 2211848 | tf_op jit(solution)/shard_map/ppermute | solution.py:624
  7.8 44.0 %collective-permute-start.6 = (f32[720,256]{1,0:T(8,128)}, f32[720,256]{1,0:T(8,128)S(1)}, u32[]{:S(2)}, u32[]{:S(2)}) collective-permute-start(f32[720,256]{1,0:T(8,128)} %get-tuple-element.65), channel_id=1, source_target_pairs={{0,2},{1,3},{2,0},{3,1},{4,6},{5,7},{6,4},{7,5},{8,10},{9,11},{10,... | collective-permute-start | bytes 2211848 | tf_op jit(solution)/shard_map/ppermute | solution.py:624
  42.4 13.0 %collective-permute-start.5 = (f32[712,256]{1,0:T(8,128)S(1)}, f32[712,256]{1,0:T(8,128)S(1)}, u32[]{:S(2)}, u32[]{:S(2)}) collective-permute-start(f32[712,256]{1,0:T(8,128)S(1)} %get-tuple-element.62), channel_id=1, source_target_pairs={{1,4},{4,1},{3,6},{6,3},{5,8},{8,5},{7,10},{10,7},{9,12},{12,9},{1... | collective-permute-start | bytes 2187272 | tf_op jit(solution)/shard_map/ppermute | solution.py:632
  45.1 22.4 %collective-permute-start = (f32[720,256]{1,0:T(8,128)S(1)}, f32[720,256]{1,0:T(8,128)S(1)}, u32[]{:S(2)}, u32[]{:S(2)}) collective-permute-start(f32[720,256]{1,0:T(8,128)S(1)} %copy-done.13), channel_id=1, source_target_pairs={{0,2},{1,3},{2,0},{3,1},{4,6},{5,7},{6,4},{7,5},{8,10},{9,11},{10,... | collective-permute-start | bytes 2211848 | tf_op jit(solution)/shard_map/ppermute | solution.py:624
  46.9 36.5 %collective-permute-start.9 = (f32[720,256]{1,0:T(8,128)S(1)}, f32[720,256]{1,0:T(8,128)S(1)}, u32[]{:S(2)}, u32[]{:S(2)}) collective-permute-start(f32[720,256]{1,0:T(8,128)S(1)} %copy-done.12), channel_id=1, source_target_pairs={{0,2},{1,3},{2,0},{3,1},{4,6},{5,7},{6,4},{7,5},{8,10},{9,11},{10,... | collective-permute-start | bytes 2211848 | tf_op jit(solution)/shard_map/ppermute | solution.py:624
  56.0 17.8 %collective-permute-start.16 = (f32[712,256]{1,0:T(8,128)S(1)}, f32[712,256]{1,0:T(8,128)S(1)}, u32[]{:S(2)}, u32[]{:S(2)}) collective-permute-start(f32[712,256]{1,0:T(8,128)S(1)} %get-tuple-element.76), channel_id=1, source_target_pairs={{1,4},{4,1},{3,6},{6,3},{5,8},{8,5},{7,10},{10,7},{9,12},{12,9},{1... | collective-permute-start | bytes 2187272 | tf_op jit(solution)/shard_map/ppermute | solution.py:632
  58.3 12.3 %collective-permute-start.14 = (f32[4,176,256]{2,1,0:T(8,128)S(1)}, f32[4,176,256]{2,1,0:T(8,128)S(1)}, u32[]{:S(2)}, u32[]{:S(2)}) collective-permute-start(f32[4,176,256]{2,1,0:T(8,128)S(1)} %get-tuple-element.66.rest_0_.refs_0_), channel_id=1, source_target_pairs={{0,1},{1,0},{2,3},{3,2},{4,5},{5,4},{6,7},{7,6},{8,9},{9,8},{10,11... | collective-permute-start | bytes 2162696 | tf_op jit(solution)/shard_map/ppermute | solution.py:630
  58.7 15.1 %collective-permute-start.15 = (f32[4,176,256]{2,1,0:T(8,128)S(1)}, f32[4,176,256]{2,1,0:T(8,128)S(1)}, u32[]{:S(2)}, u32[]{:S(2)}) collective-permute-start(f32[4,176,256]{2,1,0:T(8,128)S(1)} %get-tuple-element.75.refs_1_), channel_id=1, source_target_pairs={{0,1},{1,0},{2,3},{3,2},{4,5},{5,4},{6,7},{7,6},{8,9},{9,8},{10,11... | collective-permute-start | bytes 2162696 | tf_op jit(solution)/shard_map/ppermute | solution.py:631
  67.9 17.0 %collective-permute-start.7 = (f32[4,176,256]{2,1,0:T(8,128)S(1)}, f32[4,176,256]{2,1,0:T(8,128)S(1)}, u32[]{:S(2)}, u32[]{:S(2)}) collective-permute-start(f32[4,176,256]{2,1,0:T(8,128)S(1)} %get-tuple-element.67.refs_0_.refs_1_.refs_5_.refs_8_), channel_id=1, source_target_pairs={{0,1},{1,0},{2,3},{3,2},{4,5},{5,4},{6,7},{7,6},{8,9},{9,8},{10,11... | collective-permute-start | bytes 2162696 | tf_op jit(solution)/shard_map/ppermute | solution.py:630
  70.7 16.2 %collective-permute-start.10 = (f32[712,256]{1,0:T(8,128)S(1)}, f32[712,256]{1,0:T(8,128)S(1)}, u32[]{:S(2)}, u32[]{:S(2)}) collective-permute-start(f32[712,256]{1,0:T(8,128)S(1)} %get-tuple-element.70), channel_id=1, source_target_pairs={{1,4},{4,1},{3,6},{6,3},{5,8},{8,5},{7,10},{10,7},{9,12},{12,9},{1... | collective-permute-start | bytes 2187272 | tf_op jit(solution)/shard_map/ppermute | solution.py:632
  73.8 11.2 %collective-permute-start.8 = (f32[4,176,256]{2,1,0:T(8,128)S(1)}, f32[4,176,256]{2,1,0:T(8,128)S(1)}, u32[]{:S(2)}, u32[]{:S(2)}) collective-permute-start(f32[4,176,256]{2,1,0:T(8,128)S(1)} %get-tuple-element.68.refs_1_.refs_2_.refs_9_), channel_id=1, source_target_pairs={{0,1},{1,0},{2,3},{3,2},{4,5},{5,4},{6,7},{7,6},{8,9},{9,8},{10,11... | collective-permute-start | bytes 2162696 | tf_op jit(solution)/shard_map/ppermute | solution.py:631
  76.9 17.9 %collective-permute-start.19 = (f32[712,256]{1,0:T(8,128)S(1)}, f32[712,256]{1,0:T(8,128)S(1)}, u32[]{:S(2)}, u32[]{:S(2)}) collective-permute-start(f32[712,256]{1,0:T(8,128)S(1)} %get-tuple-element.80), channel_id=1, source_target_pairs={{1,4},{4,1},{3,6},{6,3},{5,8},{8,5},{7,10},{10,7},{9,12},{12,9},{1... | collective-permute-start | bytes 2187272 | tf_op jit(solution)/shard_map/ppermute | solution.py:632
  83.4 8.4 %collective-permute-start.17 = (f32[4,176,256]{2,1,0:T(8,128)S(1)}, f32[4,176,256]{2,1,0:T(8,128)S(1)}, u32[]{:S(2)}, u32[]{:S(2)}) collective-permute-start(f32[4,176,256]{2,1,0:T(8,128)S(1)} %get-tuple-element.78.refs_0_), channel_id=1, source_target_pairs={{0,1},{1,0},{2,3},{3,2},{4,5},{5,4},{6,7},{7,6},{8,9},{9,8},{10,11... | collective-permute-start | bytes 2162696 | tf_op jit(solution)/shard_map/ppermute | solution.py:630
  88.1 14.4 %collective-permute-start.13 = (f32[712,256]{1,0:T(8,128)S(1)}, f32[712,256]{1,0:T(8,128)S(1)}, u32[]{:S(2)}, u32[]{:S(2)}) collective-permute-start(f32[712,256]{1,0:T(8,128)S(1)} %get-tuple-element.74), channel_id=1, source_target_pairs={{1,4},{4,1},{3,6},{6,3},{5,8},{8,5},{7,10},{10,7},{9,12},{12,9},{1... | collective-permute-start | bytes 2187272 | tf_op jit(solution)/shard_map/ppermute | solution.py:632
  91.8 7.5 %collective-permute-start.12 = (f32[4,176,256]{2,1,0:T(8,128)S(1)}, f32[4,176,256]{2,1,0:T(8,128)S(1)}, u32[]{:S(2)}, u32[]{:S(2)}) collective-permute-start(f32[4,176,256]{2,1,0:T(8,128)S(1)} %get-tuple-element.73.refs_1_.refs_2_.refs_8_), channel_id=1, source_target_pairs={{0,1},{1,0},{2,3},{3,2},{4,5},{5,4},{6,7},{7,6},{8,9},{9,8},{10,11... | collective-permute-start | bytes 2162696 | tf_op jit(solution)/shard_map/ppermute | solution.py:631
  96.1 13.7 %collective-permute-start.25 = (f32[712,256]{1,0:T(8,128)S(1)}, f32[712,256]{1,0:T(8,128)S(1)}, u32[]{:S(2)}, u32[]{:S(2)}) collective-permute-start(f32[712,256]{1,0:T(8,128)S(1)} %get-tuple-element.90), channel_id=1, source_target_pairs={{1,4},{4,1},{3,6},{6,3},{5,8},{8,5},{7,10},{10,7},{9,12},{12,9},{1... | collective-permute-start | bytes 2187272 | tf_op jit(solution)/shard_map/ppermute | solution.py:632
  99.3 18.6 %collective-permute-start.26 = (f32[720,256]{1,0:T(8,128)S(1)}, f32[720,256]{1,0:T(8,128)S(1)}, u32[]{:S(2)}, u32[]{:S(2)}) collective-permute-start(f32[720,256]{1,0:T(8,128)S(1)} %get-tuple-element.92), channel_id=1, source_target_pairs={{0,2},{1,3},{2,0},{3,1},{4,6},{5,7},{6,4},{7,5},{8,10},{9,11},{10,... | collective-permute-start | bytes 2211848 | tf_op jit(solution)/shard_map/ppermute | solution.py:624
  104.5 13.4 %collective-permute-start.24 = (f32[712,256]{1,0:T(8,128)S(1)}, f32[712,256]{1,0:T(8,128)S(1)}, u32[]{:S(2)}, u32[]{:S(2)}) collective-permute-start(f32[712,256]{1,0:T(8,128)S(1)} %get-tuple-element.88), channel_id=1, source_target_pairs={{1,4},{4,1},{3,6},{6,3},{5,8},{8,5},{7,10},{10,7},{9,12},{12,9},{1... | collective-permute-start | bytes 2187272 | tf_op jit(solution)/shard_map/ppermute | solution.py:632
  110.4 23.3 %collective-permute-start.31 = (f32[720,256]{1,0:T(8,128)S(1)}, f32[720,256]{1,0:T(8,128)S(1)}, u32[]{:S(2)}, u32[]{:S(2)}) collective-permute-start(f32[720,256]{1,0:T(8,128)S(1)} %get-tuple-element.99), channel_id=1, source_target_pairs={{0,2},{1,3},{2,0},{3,1},{4,6},{5,7},{6,4},{7,5},{8,10},{9,11},{10,... | collective-permute-start | bytes 2211848 | tf_op jit(solution)/shard_map/ppermute | solution.py:624
  119.8 8.7 %collective-permute-start.30 = (f32[320,256]{1,0:T(8,128)S(1)}, f32[320,256]{1,0:T(8,128)S(1)}, u32[]{:S(2)}, u32[]{:S(2)}) collective-permute-start(f32[320,256]{1,0:T(8,128)S(1)} %get-tuple-element.97), channel_id=1, source_target_pairs={{1,4},{4,1},{3,6},{6,3},{5,8},{8,5},{7,10},{10,7},{9,12},{12,9},{1... | collective-permute-start | bytes 983048 | tf_op jit(solution)/shard_map/ppermute | solution.py:632
  123.0 9.0 %collective-permute-start.29 = (f32[320,256]{1,0:T(8,128)S(1)}, f32[320,256]{1,0:T(8,128)S(1)}, u32[]{:S(2)}, u32[]{:S(2)}) collective-permute-start(f32[320,256]{1,0:T(8,128)S(1)} %get-tuple-element.95), channel_id=1, source_target_pairs={{1,4},{4,1},{3,6},{6,3},{5,8},{8,5},{7,10},{10,7},{9,12},{12,9},{1... | collective-permute-start | bytes 983048 | tf_op jit(solution)/shard_map/ppermute | solution.py:704
  128.8 11.9 %collective-permute-start.33 = (f32[4,80,256]{2,1,0:T(8,128)S(1)}, f32[4,80,256]{2,1,0:T(8,128)S(1)}, u32[]{:S(2)}, u32[]{:S(2)}) collective-permute-start(f32[4,80,256]{2,1,0:T(8,128)S(1)} %get-tuple-element.102), channel_id=1, source_target_pairs={{0,2},{1,3},{2,0},{3,1},{4,6},{5,7},{6,4},{7,5},{8,10},{9,11},{10,... | collective-permute-start | bytes 983048 | tf_op jit(solution)/shard_map/ppermute | solution.py:624
  134.0 13.2 %collective-permute-start.32 = (f32[4,80,256]{2,1,0:T(8,128)S(1)}, f32[4,80,256]{2,1,0:T(8,128)S(1)}, u32[]{:S(2)}, u32[]{:S(2)}) collective-permute-start(f32[4,80,256]{2,1,0:T(8,128)S(1)} %get-tuple-element.100), channel_id=1, source_target_pairs={{0,2},{1,3},{2,0},{3,1},{4,6},{5,7},{6,4},{7,5},{8,10},{9,11},{10,... | collective-permute-start | bytes 983048 | tf_op jit(solution)/shard_map/ppermute | solution.py:624
  (24 other events, 120.1 us)

commit v5 on v4

--- a/solution.py
+++ b/solution.py
@@ -71,6 +71,7 @@
         self.moved = (rows * self.wide + 16, depth)
         self.sent = (rows, self.half, depth)
         self.whole = (rows, cols, depth)
+        self.back = (rows * self.half + 8, depth)
         self.quarter = cols // 4
         self.quarters = (rows, self.quarter, depth)
         self.edges = (rows * self.quarter, depth)
@@ -92,8 +93,8 @@
         return pl.ds(self.rows * self.wide, 16)
 
 
-def over_columns(sizes, body):
-    @pl.loop(0, sizes.wide // 16)
+def over_columns(count, body):
+    @pl.loop(0, count // 16)
     def _(step):
         for part in range(2):
             body(pl.multiple_of(step * 16 + part * 8, 8))
@@ -133,10 +134,10 @@
             mixed[slot, row] = total
 
 
-def along_rows(sizes, blocks, mixed, partial):
+def along_rows(sizes, blocks, mixed, partial, narrow=False):
     mine0, mine1, other0, other1 = blocks
     rows = sizes.rows
-    _, _, core = place()
+    _, half, core = place()
     orders = (
         (None, mine0, other0, mine1, other1),
         (other0, mine0, other1, mine1, None),
@@ -147,9 +148,16 @@
         def _():
             for slot in range(2):
 
-                def columns(first):
+                def columns(local):
+                    first = local
+                    if narrow:
+                        first = pl.multiple_of(half * EXTRA + local, 8)
                     near = [
-                        None if block is None else block[row, cut(first), :]
+                        None
+                        if block is None
+                        else block[
+                            row, cut(first if block is mine0 or block is mine1 else local), :
+                        ]
                         for block in order[2 * slot : 2 * slot + 3]
                         for row in range(rows)
                     ]
@@ -164,10 +172,10 @@
                         total = total + mixed[slot, row, cut(first), :]
                         partial[slot, row, cut(first), :] = sum(parts[1:], parts[0]) + total
 
-                over_columns(sizes, columns)
-
-
-def prepare(sizes, blocks, name, inject=None, settled=()):
+                over_columns(sizes.half if narrow else sizes.wide, columns)
+
+
+def prepare(sizes, blocks, name, inject=None, settled=(), narrow=False):
     def body(*refs):
         b_refs = refs[:4]
         partial, mixed = refs[-2:]
@@ -193,7 +201,7 @@
                 return dot(jnp.concatenate((hit, hit), 1), values, ((1,), (1,)))
 
         differences(sizes, b_refs, mixed, added)
-        along_rows(sizes, b_refs, mixed, partial)
+        along_rows(sizes, b_refs, mixed, partial, narrow)
 
     operands = (*blocks, *(inject[1:] if inject is not None else ()))
     specs = [VMEM] * len(operands) + [ANY] * len(settled)
@@ -225,7 +233,7 @@
                                 total = total + WEIGHTS[offset] * far[at]
                         finish(which, slot, row, first, total)
 
-            over_columns(sizes, columns)
+            over_columns(sizes.wide, columns)
 
 
 def run(body, name, operands, specs, outs, scratch=(), aliases=None, limit=24, sems=0):
@@ -326,7 +334,7 @@
                         sizes, own_ref, moved_ref, slot, row, first
                     )
 
-        over_columns(sizes, columns)
+        over_columns(sizes.wide, columns)
 
     return run(
         body,
@@ -353,7 +361,7 @@
                     core == 0, u0_out[row, cut(first), :], u1_out[row, cut(first), :]
                 )
 
-        over_columns(sizes, columns)
+        over_columns(sizes.wide, columns)
 
     return run(
         body,
@@ -403,14 +411,14 @@
                 sent_out[pl.ds(row * sizes.half, sizes.half), :] = next_out[
                     1 - half, row, sizes.own(half), :
                 ]
-            rest = sizes.moved[0] - sizes.rows * sizes.half
+            rest = sent_out.shape[0] - sizes.rows * sizes.half
             sent_out[pl.ds(sizes.rows * sizes.half, rest), :] = jnp.zeros((rest, sizes.depth), F32)
 
     outs = []
     if more:
         outs += [(sizes.pair, VMEM)] + [(sizes.block, VMEM)] * 2 + [(sizes.edge, VMEM)]
     if ends:
-        outs += [(sizes.sent, VMEM), (sizes.moved, VMEM)]
+        outs += [(sizes.sent, VMEM), (sizes.moved if more else sizes.back, VMEM)]
     return run(
         body,
         f"adjoint_{step_no}",
@@ -433,7 +441,7 @@
                 c1_out[row, cut(first), :] = pair[1]
                 z_out[flat(sizes, row, first)] = jnp.where(core == 0, *pair)
 
-        over_columns(sizes, columns)
+        over_columns(sizes.wide, columns)
 
     return run(
         body,
@@ -494,9 +502,11 @@
             pl.when(inside)(functools.partial(put, c_out, (row, pl.ds(col, 1), slice(None))))
             if last_step:
 
+                z_outs[slot][...] = c_out[:, sizes.own(half), :]
+
                 @pl.when(core == slot)
                 def _():
-                    for part, z_out in enumerate(z_outs):
+                    for part, z_out in enumerate(z_outs[2:]):
                         here = pl.ds(
                             pl.multiple_of(half * EXTRA + part * sizes.quarter, 16), sizes.quarter
                         )
@@ -518,7 +528,10 @@
     operands += before
     specs = [VMEM] * len(operands) + [SMEM] * 3 + [ANY] * len(settled)
     outs = [(sizes.block, VMEM)] * 2 + [(sizes.pair, VMEM)]
-    outs += [(sizes.edges, VMEM)] * 2 if last_step else [(sizes.edge, VMEM)]
+    if last_step:
+        outs += [(sizes.sent, VMEM)] * 2 + [(sizes.edges, VMEM)] * 2
+    else:
+        outs += [(sizes.edge, VMEM)]
     return run(body, f"forward_{step_no}", (*operands, *source, *settled), specs, outs)
 
 
@@ -697,12 +710,12 @@
     prepared = ready_forward(3, current3)
     mine0, sent0 = adjoint(1, partial, scaled[4], later1, (later2,), speed, current3[2:4])
     got0 = over(sent0)
-    *current4, gradient, edge0, edge1 = forward(
+    *current4, gradient, narrow0, narrow1, edge0, edge1 = forward(
         3, *prepared, current2[:2], speed, (later3,), gradient, source, (mine0, got1)
     )
-    *current4, beside0 = exchange(*current4, edge0)
+    *narrow4, beside0 = exchange(narrow0, narrow1, edge0)[2:]
     beside1 = lax.ppermute(edge1, "gx", levels)
-    partial, _ = ready_forward(4, (*current4, beside0))
+    partial = prepare(sizes, (*current4, *narrow4), "prepare_forward_4", narrow=True)
     ends = functools.partial(forward_end, sizes)
     kept0, sent = ends(0, partial, beside0, speed, later4, gradient)
     moved0 = over(sent)

time: 149 us -> 147 us (0.987)
  starting transfers between devices: 44 us -> 41.4 us
    ppermute x8, waiting for transfers between devices: 4.87 us -> 9.85 us  [exchange(): lax.ppermute(edge, 'gx', levels)]
    ppermute x9, waiting for transfers between devices: 35.5 us -> 30.6 us  [over(): return lax.ppermute(field, 'gx', across)]
    ppermute x9, starting transfers between devices: 9.86 us -> 7.48 us  [over(): return lax.ppermute(field, 'gx', across)]
  transfers between devices with their start and end apart: 34 -> 34, of which waited for: 12 -> 13; matrix products, arithmetic and copies ran while one was open for 0% -> 0% of each run, Pallas kernels for 24% -> 25%
where the time goes in v5:
time: 147 us; the launch traced here: 146 us
  waiting for transfers between devices  43.9 us (30%)
  starting transfers between devices  41.4 us (28%)
  Pallas kernels  36.8 us (25%)
  blocking collectives  17.1 us (12%)
  local copies, waits for them, and re-layouts  5.32 us (4%)
  between operations  1.94 us (1%)
    pallas_call x26, Pallas kernels, run(): pl.pallas_call(body, name=name, out_shape=[jax.ShapeDtypeStruct(shape, F3...  36.8 us
    ppermute x9, waiting for transfers between devices, over(): return lax.ppermute(field, 'gx', across)  30.6 us
    ppermute x8, starting transfers between devices, exchange(): lax.ppermute(edge, 'gx', levels)  23.5 us
    all_gather x1, blocking collectives, on_device(): tails = lax.all_gather(tails, 'gx', axis_index_groups=halves)  17.1 us
    ppermute x8, waiting for transfers between devices, exchange(): lax.ppermute(edge, 'gx', levels)  9.85 us
    ppermute x9, starting transfers between devices, over(): return lax.ppermute(field, 'gx', across)  7.48 us
    ppermute x8, starting transfers between devices, exchange(): lax.ppermute(block0, 'gx', cores)  6.38 us
    unnamed x30, local copies, waits for them, and re-layouts  5.21 us
  transfers between devices with their start and end apart: 34, of which 13 were waited for; matrix products, arithmetic and copies ran while one was open for 0% of the time, Pallas kernels for 25%

profile of v5, /device:TPU:11, one launch (start us, length us, event | category | flops | bytes accessed | tf_op | source)
XLA Modules:
  0.0 146.5 jit_solution(17488114253005693001)
XLA Ops:
  4.1 3.4 %pack.1 = (f32[720,256]{1,0:T(8,128)}, f32[720,256]{1,0:T(8,128)}, f32[720,256]{1,0:T(8,128)}, f32[720,256]{1,0:T(8,128)}) custom-call(f32[2,1,4,320,256]{4,3,2,1,0:T(8,128)} %a_ref.3, f32[2,1,4,320,256]{4,3,2,1,0:T(8,128)} %w_ref.3), custom_call_target="tpu_custom_call" | custom-call | tf_op jit(solution)/shard_map/pack/pallas_call | solution.py:240
  9.0 3.8 %keep.1 = (f32[4,176,256]{2,1,0:T(8,128)}, f32[4,176,256]{2,1,0:T(8,128)}, f32[4,176,256]{2,1,0:T(8,128)}, f32[4,176,256]{2,1,0:T(8,128)}, f32[4,176,256]{2,1,0:T(8,128)}) custom-call(f32[4,320,256]{2,1,0:T(8,128)} %field.1, f32[2,1,4,320,256]{4,3,2,1,0:T(8,128)} %a_ref.3, f32[2,1,4,320,256]{4,3,2,1,0:T(8,128)} %w_ref.3), custom_call_target="tpu_custom_call" | custom-call | tf_op jit(solution)/shard_map/keep/pallas_call | solution.py:240
  13.4 6.7 %collective-permute-done.1.moved_ref = f32[720,256]{1,0:T(8,128)S(1)} collective-permute-done((f32[720,256]{1,0:T(8,128)S(1)}, f32[720,256]{1,0:T(8,128)S(1)}, u32[]{:S(2)}, u32[]{:S(2)}) %collective-permute-start.1) | collective-permute-done | bytes 737312 | tf_op jit(solution)/shard_map/ppermute | solution.py:637
  23.5 17.1 %all-gather = f32[16,16,256]{2,1,0:T(8,128)S(1)} all-gather(f32[2,16,256]{2,1,0:T(8,128)S(1)} %get-tuple-element.61), channel_id=2, replica_groups={{0,1,4,5,8,9,12,13},{2,3,6,7,10,11,14,15},{16,17,20,21,24,25,28,29},{18..., dimensions={0}, use_global_device_ids=true | all-gather | bytes 294912 | tf_op jit(solution)/shard_map/all_gather | solution.py:654
  48.1 2.5 %prepare_adjoint_4.1.refs_0_ = f32[2,4,176,256]{3,2,1,0:T(8,128)S(1)} custom-call(f32[4,176,256]{2,1,0:T(8,128)S(1)} %get-tuple-element.62.refs_0_, f32[4,176,256]{2,1,0:T(8,128)S(1)} %get-tuple-element.63.refs_1_, f32[4,176,256]{2,1,0:T(8,128)S(1)} %collective-permute-done.3.refs_2_, f32[4,176,256]{2,1,0:T(8,128)S(1)} %collective-permute-done.4.refs_3_, ...), custom_call_target="tpu_custom_call" | custom-call | tf_op jit(solution)/shard_map/prepare_adjoint_4/pallas_call | solution.py:240
  51.8 3.6 %collective-permute-done.5.refs_1_ = f32[712,256]{1,0:T(8,128)S(1)} collective-permute-done((f32[712,256]{1,0:T(8,128)S(1)}, f32[712,256]{1,0:T(8,128)S(1)}, u32[]{:S(2)}, u32[]{:S(2)}) %collective-permute-start.5) | collective-permute-done | bytes 729120 | tf_op jit(solution)/shard_map/ppermute | solution.py:645
  56.0 2.3 %collective-permute-start.16 = (f32[712,256]{1,0:T(8,128)S(1)}, f32[712,256]{1,0:T(8,128)S(1)}, u32[]{:S(2)}, u32[]{:S(2)}) collective-permute-start(f32[712,256]{1,0:T(8,128)S(1)} %get-tuple-element.78), channel_id=1, source_target_pairs={{1,4},{4,1},{3,6},{6,3},{5,8},{8,5},{7,10},{10,7},{9,12},{12,9},{1... | collective-permute-start | bytes 2187272 | tf_op jit(solution)/shard_map/ppermute | solution.py:645
  58.9 8.7 %collective-permute-done.moved_ref = f32[720,256]{1,0:T(8,128)S(1)} collective-permute-done((f32[720,256]{1,0:T(8,128)S(1)}, f32[720,256]{1,0:T(8,128)S(1)}, u32[]{:S(2)}, u32[]{:S(2)}) %collective-permute-start) | collective-permute-done | bytes 737312 | tf_op jit(solution)/shard_map/ppermute | solution.py:637
  67.9 2.8 %collective-permute-start.7 = (f32[4,176,256]{2,1,0:T(8,128)S(1)}, f32[4,176,256]{2,1,0:T(8,128)S(1)}, u32[]{:S(2)}, u32[]{:S(2)}) collective-permute-start(f32[4,176,256]{2,1,0:T(8,128)S(1)} %get-tuple-element.69.refs_0_.refs_1_.refs_5_.refs_8_), channel_id=1, source_target_pairs={{0,1},{1,0},{2,3},{3,2},{4,5},{5,4},{6,7},{7,6},{8,9},{9,8},{10,11... | collective-permute-start | bytes 2162696 | tf_op jit(solution)/shard_map/ppermute | solution.py:643
  70.7 3.1 %collective-permute-start.10 = (f32[712,256]{1,0:T(8,128)S(1)}, f32[712,256]{1,0:T(8,128)S(1)}, u32[]{:S(2)}, u32[]{:S(2)}) collective-permute-start(f32[712,256]{1,0:T(8,128)S(1)} %get-tuple-element.72), channel_id=1, source_target_pairs={{1,4},{4,1},{3,6},{6,3},{5,8},{8,5},{7,10},{10,7},{9,12},{12,9},{1... | collective-permute-start | bytes 2187272 | tf_op jit(solution)/shard_map/ppermute | solution.py:645
  73.9 2.5 %prepare_adjoint_3.1.refs_0_ = f32[2,4,176,256]{3,2,1,0:T(8,128)S(1)} custom-call(f32[4,176,256]{2,1,0:T(8,128)S(1)} %get-tuple-element.68.rest_0_.refs_0_, f32[4,176,256]{2,1,0:T(8,128)S(1)} %get-tuple-element.77.refs_1_, f32[4,176,256]{2,1,0:T(8,128)S(1)} %collective-permute-done.14.refs_2_, f32[4,176,256]{2,1,0:T(8,128)S(1)} %collective-permute-done.15.refs_3_, ...), custom_call_target="tpu_custom_call" | custom-call | tf_op jit(solution)/shard_map/prepare_adjoint_3/pallas_call | solution.py:240
  76.9 3.6 %collective-permute-start.19 = (f32[712,256]{1,0:T(8,128)S(1)}, f32[712,256]{1,0:T(8,128)S(1)}, u32[]{:S(2)}, u32[]{:S(2)}) collective-permute-start(f32[712,256]{1,0:T(8,128)S(1)} %get-tuple-element.82), channel_id=1, source_target_pairs={{1,4},{4,1},{3,6},{6,3},{5,8},{8,5},{7,10},{10,7},{9,12},{12,9},{1... | collective-permute-start | bytes 2187272 | tf_op jit(solution)/shard_map/ppermute | solution.py:645
  80.6 2.8 %collective-permute-done.9.refs_4_.refs_6_ = f32[720,256]{1,0:T(8,128)S(1)} collective-permute-done((f32[720,256]{1,0:T(8,128)S(1)}, f32[720,256]{1,0:T(8,128)S(1)}, u32[]{:S(2)}, u32[]{:S(2)}) %collective-permute-start.9) | collective-permute-done | bytes 737312 | tf_op jit(solution)/shard_map/ppermute | solution.py:637
  88.1 3.6 %collective-permute-start.13 = (f32[712,256]{1,0:T(8,128)S(1)}, f32[712,256]{1,0:T(8,128)S(1)}, u32[]{:S(2)}, u32[]{:S(2)}) collective-permute-start(f32[712,256]{1,0:T(8,128)S(1)} %get-tuple-element.76), channel_id=1, source_target_pairs={{1,4},{4,1},{3,6},{6,3},{5,8},{8,5},{7,10},{10,7},{9,12},{12,9},{1... | collective-permute-start | bytes 2187272 | tf_op jit(solution)/shard_map/ppermute | solution.py:645
  92.3 2.5 %prepare_adjoint_2.1.refs_0_ = f32[2,4,176,256]{3,2,1,0:T(8,128)S(1)} custom-call(f32[4,176,256]{2,1,0:T(8,128)S(1)} %get-tuple-element.80.refs_0_, f32[4,176,256]{2,1,0:T(8,128)S(1)} %get-tuple-element.81.refs_1_, f32[4,176,256]{2,1,0:T(8,128)S(1)} %collective-permute-done.17.refs_2_, f32[4,176,256]{2,1,0:T(8,128)S(1)} %collective-permute-done.18.refs_3_, ...), custom_call_target="tpu_custom_call" | custom-call | tf_op jit(solution)/shard_map/prepare_adjoint_2/pallas_call | solution.py:240
  97.3 3.5 %collective-permute-start.25 = (f32[712,256]{1,0:T(8,128)S(1)}, f32[712,256]{1,0:T(8,128)S(1)}, u32[]{:S(2)}, u32[]{:S(2)}) collective-permute-start(f32[712,256]{1,0:T(8,128)S(1)} %get-tuple-element.92), channel_id=1, source_target_pairs={{1,4},{4,1},{3,6},{6,3},{5,8},{8,5},{7,10},{10,7},{9,12},{12,9},{1... | collective-permute-start | bytes 2187272 | tf_op jit(solution)/shard_map/ppermute | solution.py:645
  104.2 2.2 %collective-permute-start.24 = (f32[712,256]{1,0:T(8,128)S(1)}, f32[712,256]{1,0:T(8,128)S(1)}, u32[]{:S(2)}, u32[]{:S(2)}) collective-permute-start(f32[712,256]{1,0:T(8,128)S(1)} %get-tuple-element.90), channel_id=1, source_target_pairs={{1,4},{4,1},{3,6},{6,3},{5,8},{8,5},{7,10},{10,7},{9,12},{12,9},{1... | collective-permute-start | bytes 2187272 | tf_op jit(solution)/shard_map/ppermute | solution.py:645
  107.0 2.5 %prepare_adjoint_1.1.refs_0_ = f32[2,4,176,256]{3,2,1,0:T(8,128)S(1)} custom-call(f32[4,176,256]{2,1,0:T(8,128)S(1)} %get-tuple-element.86.refs_0_, f32[4,176,256]{2,1,0:T(8,128)S(1)} %get-tuple-element.87.refs_1_, f32[4,176,256]{2,1,0:T(8,128)S(1)} %collective-permute-done.20.refs_13_.refs_2_, f32[4,176,256]{2,1,0:T(8,128)S(1)} %collective-permute-done.21.refs_14_.refs_3_, ...), custom_call_target="tpu_custom_call" | custom-call | tf_op jit(solution)/shard_map/prepare_adjoint_1/pallas_call | solution.py:240
  114.0 4.1 %collective-permute-done.24.refs_3_ = f32[712,256]{1,0:T(8,128)S(1)} collective-permute-done((f32[712,256]{1,0:T(8,128)S(1)}, f32[712,256]{1,0:T(8,128)S(1)}, u32[]{:S(2)}, u32[]{:S(2)}) %collective-permute-start.24) | collective-permute-done | bytes 729120 | tf_op jit(solution)/shard_map/ppermute | solution.py:645
  120.1 3.2 %collective-permute-start.30 = (f32[320,256]{1,0:T(8,128)S(1)}, f32[320,256]{1,0:T(8,128)S(1)}, u32[]{:S(2)}, u32[]{:S(2)}) collective-permute-start(f32[320,256]{1,0:T(8,128)S(1)} %get-tuple-element.101), channel_id=1, source_target_pairs={{1,4},{4,1},{3,6},{6,3},{5,8},{8,5},{7,10},{10,7},{9,12},{12,9},{1... | collective-permute-start | bytes 983048 | tf_op jit(solution)/shard_map/ppermute | solution.py:645
  123.4 2.3 %collective-permute-start.29 = (f32[320,256]{1,0:T(8,128)S(1)}, f32[320,256]{1,0:T(8,128)S(1)}, u32[]{:S(2)}, u32[]{:S(2)}) collective-permute-start(f32[320,256]{1,0:T(8,128)S(1)} %get-tuple-element.99), channel_id=1, source_target_pairs={{1,4},{4,1},{3,6},{6,3},{5,8},{8,5},{7,10},{10,7},{9,12},{12,9},{1... | collective-permute-start | bytes 983048 | tf_op jit(solution)/shard_map/ppermute | solution.py:717
  129.4 2.9 %collective-permute-done.29.beside_ref = f32[320,256]{1,0:T(8,128)S(1)} collective-permute-done((f32[320,256]{1,0:T(8,128)S(1)}, f32[320,256]{1,0:T(8,128)S(1)}, u32[]{:S(2)}, u32[]{:S(2)}) %collective-permute-start.29) | collective-permute-done | bytes 327712 | tf_op jit(solution)/shard_map/ppermute | solution.py:717
  134.4 4.1 %collective-permute-done.33.refs_2_ = f32[4,80,256]{2,1,0:T(8,128)S(1)} collective-permute-done((f32[4,80,256]{2,1,0:T(8,128)S(1)}, f32[4,80,256]{2,1,0:T(8,128)S(1)}, u32[]{:S(2)}, u32[]{:S(2)}) %collective-permute-start.33) | collective-permute-done | bytes 327712 | tf_op jit(solution)/shard_map/ppermute | solution.py:637
  139.5 6.0 %collective-permute-done.32.refs_0_ = f32[4,80,256]{2,1,0:T(8,128)S(1)} collective-permute-done((f32[4,80,256]{2,1,0:T(8,128)S(1)}, f32[4,80,256]{2,1,0:T(8,128)S(1)}, u32[]{:S(2)}, u32[]{:S(2)}) %collective-permute-start.32) | collective-permute-done | bytes 327712 | tf_op jit(solution)/shard_map/ppermute | solution.py:637
  (104 shorter events, 44.7 us)
Async XLA Ops:
  2.8 17.4 %collective-permute-start.1 = (f32[720,256]{1,0:T(8,128)S(1)}, f32[720,256]{1,0:T(8,128)S(1)}, u32[]{:S(2)}, u32[]{:S(2)}) collective-permute-start(f32[720,256]{1,0:T(8,128)S(1)} %pack_first.1.sent_ref), channel_id=1, source_target_pairs={{0,2},{1,3},{2,0},{3,1},{4,6},{5,7},{6,4},{7,5},{8,10},{9,11},{10,... | collective-permute-start | bytes 2211848 | tf_op jit(solution)/shard_map/ppermute | solution.py:637
  7.5 33.3 %collective-permute-start.2 = (f32[720,256]{1,0:T(8,128)}, f32[720,256]{1,0:T(8,128)}, u32[]{:S(2)}, u32[]{:S(2)}) collective-permute-start(f32[720,256]{1,0:T(8,128)} %get-tuple-element.60), channel_id=1, source_target_pairs={{0,2},{1,3},{2,0},{3,1},{4,6},{5,7},{6,4},{7,5},{8,10},{9,11},{10,... | collective-permute-start | bytes 2211848 | tf_op jit(solution)/shard_map/ppermute | solution.py:637
  7.8 44.0 %collective-permute-start.6 = (f32[720,256]{1,0:T(8,128)}, f32[720,256]{1,0:T(8,128)S(1)}, u32[]{:S(2)}, u32[]{:S(2)}) collective-permute-start(f32[720,256]{1,0:T(8,128)} %get-tuple-element.67), channel_id=1, source_target_pairs={{0,2},{1,3},{2,0},{3,1},{4,6},{5,7},{6,4},{7,5},{8,10},{9,11},{10,... | collective-permute-start | bytes 2211848 | tf_op jit(solution)/shard_map/ppermute | solution.py:637
  42.4 13.0 %collective-permute-start.5 = (f32[712,256]{1,0:T(8,128)S(1)}, f32[712,256]{1,0:T(8,128)S(1)}, u32[]{:S(2)}, u32[]{:S(2)}) collective-permute-start(f32[712,256]{1,0:T(8,128)S(1)} %get-tuple-element.64), channel_id=1, source_target_pairs={{1,4},{4,1},{3,6},{6,3},{5,8},{8,5},{7,10},{10,7},{9,12},{12,9},{1... | collective-permute-start | bytes 2187272 | tf_op jit(solution)/shard_map/ppermute | solution.py:645
  45.1 22.4 %collective-permute-start = (f32[720,256]{1,0:T(8,128)S(1)}, f32[720,256]{1,0:T(8,128)S(1)}, u32[]{:S(2)}, u32[]{:S(2)}) collective-permute-start(f32[720,256]{1,0:T(8,128)S(1)} %copy-done.13), channel_id=1, source_target_pairs={{0,2},{1,3},{2,0},{3,1},{4,6},{5,7},{6,4},{7,5},{8,10},{9,11},{10,... | collective-permute-start | bytes 2211848 | tf_op jit(solution)/shard_map/ppermute | solution.py:637
  46.9 36.5 %collective-permute-start.9 = (f32[720,256]{1,0:T(8,128)S(1)}, f32[720,256]{1,0:T(8,128)S(1)}, u32[]{:S(2)}, u32[]{:S(2)}) collective-permute-start(f32[720,256]{1,0:T(8,128)S(1)} %copy-done.12), channel_id=1, source_target_pairs={{0,2},{1,3},{2,0},{3,1},{4,6},{5,7},{6,4},{7,5},{8,10},{9,11},{10,... | collective-permute-start | bytes 2211848 | tf_op jit(solution)/shard_map/ppermute | solution.py:637
  56.0 17.8 %collective-permute-start.16 = (f32[712,256]{1,0:T(8,128)S(1)}, f32[712,256]{1,0:T(8,128)S(1)}, u32[]{:S(2)}, u32[]{:S(2)}) collective-permute-start(f32[712,256]{1,0:T(8,128)S(1)} %get-tuple-element.78), channel_id=1, source_target_pairs={{1,4},{4,1},{3,6},{6,3},{5,8},{8,5},{7,10},{10,7},{9,12},{12,9},{1... | collective-permute-start | bytes 2187272 | tf_op jit(solution)/shard_map/ppermute | solution.py:645
  58.3 12.3 %collective-permute-start.14 = (f32[4,176,256]{2,1,0:T(8,128)S(1)}, f32[4,176,256]{2,1,0:T(8,128)S(1)}, u32[]{:S(2)}, u32[]{:S(2)}) collective-permute-start(f32[4,176,256]{2,1,0:T(8,128)S(1)} %get-tuple-element.68.rest_0_.refs_0_), channel_id=1, source_target_pairs={{0,1},{1,0},{2,3},{3,2},{4,5},{5,4},{6,7},{7,6},{8,9},{9,8},{10,11... | collective-permute-start | bytes 2162696 | tf_op jit(solution)/shard_map/ppermute | solution.py:643
  58.7 15.1 %collective-permute-start.15 = (f32[4,176,256]{2,1,0:T(8,128)S(1)}, f32[4,176,256]{2,1,0:T(8,128)S(1)}, u32[]{:S(2)}, u32[]{:S(2)}) collective-permute-start(f32[4,176,256]{2,1,0:T(8,128)S(1)} %get-tuple-element.77.refs_1_), channel_id=1, source_target_pairs={{0,1},{1,0},{2,3},{3,2},{4,5},{5,4},{6,7},{7,6},{8,9},{9,8},{10,11... | collective-permute-start | bytes 2162696 | tf_op jit(solution)/shard_map/ppermute | solution.py:644
  67.9 17.0 %collective-permute-start.7 = (f32[4,176,256]{2,1,0:T(8,128)S(1)}, f32[4,176,256]{2,1,0:T(8,128)S(1)}, u32[]{:S(2)}, u32[]{:S(2)}) collective-permute-start(f32[4,176,256]{2,1,0:T(8,128)S(1)} %get-tuple-element.69.refs_0_.refs_1_.refs_5_.refs_8_), channel_id=1, source_target_pairs={{0,1},{1,0},{2,3},{3,2},{4,5},{5,4},{6,7},{7,6},{8,9},{9,8},{10,11... | collective-permute-start | bytes 2162696 | tf_op jit(solution)/shard_map/ppermute | solution.py:643
  70.7 16.2 %collective-permute-start.10 = (f32[712,256]{1,0:T(8,128)S(1)}, f32[712,256]{1,0:T(8,128)S(1)}, u32[]{:S(2)}, u32[]{:S(2)}) collective-permute-start(f32[712,256]{1,0:T(8,128)S(1)} %get-tuple-element.72), channel_id=1, source_target_pairs={{1,4},{4,1},{3,6},{6,3},{5,8},{8,5},{7,10},{10,7},{9,12},{12,9},{1... | collective-permute-start | bytes 2187272 | tf_op jit(solution)/shard_map/ppermute | solution.py:645
  73.8 11.2 %collective-permute-start.8 = (f32[4,176,256]{2,1,0:T(8,128)S(1)}, f32[4,176,256]{2,1,0:T(8,128)S(1)}, u32[]{:S(2)}, u32[]{:S(2)}) collective-permute-start(f32[4,176,256]{2,1,0:T(8,128)S(1)} %get-tuple-element.70.refs_1_.refs_2_.refs_9_), channel_id=1, source_target_pairs={{0,1},{1,0},{2,3},{3,2},{4,5},{5,4},{6,7},{7,6},{8,9},{9,8},{10,11... | collective-permute-start | bytes 2162696 | tf_op jit(solution)/shard_map/ppermute | solution.py:644
  76.9 17.9 %collective-permute-start.19 = (f32[712,256]{1,0:T(8,128)S(1)}, f32[712,256]{1,0:T(8,128)S(1)}, u32[]{:S(2)}, u32[]{:S(2)}) collective-permute-start(f32[712,256]{1,0:T(8,128)S(1)} %get-tuple-element.82), channel_id=1, source_target_pairs={{1,4},{4,1},{3,6},{6,3},{5,8},{8,5},{7,10},{10,7},{9,12},{12,9},{1... | collective-permute-start | bytes 2187272 | tf_op jit(solution)/shard_map/ppermute | solution.py:645
  83.4 8.4 %collective-permute-start.17 = (f32[4,176,256]{2,1,0:T(8,128)S(1)}, f32[4,176,256]{2,1,0:T(8,128)S(1)}, u32[]{:S(2)}, u32[]{:S(2)}) collective-permute-start(f32[4,176,256]{2,1,0:T(8,128)S(1)} %get-tuple-element.80.refs_0_), channel_id=1, source_target_pairs={{0,1},{1,0},{2,3},{3,2},{4,5},{5,4},{6,7},{7,6},{8,9},{9,8},{10,11... | collective-permute-start | bytes 2162696 | tf_op jit(solution)/shard_map/ppermute | solution.py:643
  84.9 7.4 %collective-permute-start.18 = (f32[4,176,256]{2,1,0:T(8,128)S(1)}, f32[4,176,256]{2,1,0:T(8,128)S(1)}, u32[]{:S(2)}, u32[]{:S(2)}) collective-permute-start(f32[4,176,256]{2,1,0:T(8,128)S(1)} %get-tuple-element.81.refs_1_), channel_id=1, source_target_pairs={{0,1},{1,0},{2,3},{3,2},{4,5},{5,4},{6,7},{7,6},{8,9},{9,8},{10,11... | collective-permute-start | bytes 2162696 | tf_op jit(solution)/shard_map/ppermute | solution.py:644
  88.1 14.6 %collective-permute-start.13 = (f32[712,256]{1,0:T(8,128)S(1)}, f32[712,256]{1,0:T(8,128)S(1)}, u32[]{:S(2)}, u32[]{:S(2)}) collective-permute-start(f32[712,256]{1,0:T(8,128)S(1)} %get-tuple-element.76), channel_id=1, source_target_pairs={{1,4},{4,1},{3,6},{6,3},{5,8},{8,5},{7,10},{10,7},{9,12},{12,9},{1... | collective-permute-start | bytes 2187272 | tf_op jit(solution)/shard_map/ppermute | solution.py:645
  96.1 18.0 %collective-permute-start.26 = (f32[720,256]{1,0:T(8,128)S(1)}, f32[720,256]{1,0:T(8,128)S(1)}, u32[]{:S(2)}, u32[]{:S(2)}) collective-permute-start(f32[720,256]{1,0:T(8,128)S(1)} %get-tuple-element.94), channel_id=1, source_target_pairs={{0,2},{1,3},{2,0},{3,1},{4,6},{5,7},{6,4},{7,5},{8,10},{9,11},{10,... | collective-permute-start | bytes 2211848 | tf_op jit(solution)/shard_map/ppermute | solution.py:637
  97.3 13.0 %collective-permute-start.25 = (f32[712,256]{1,0:T(8,128)S(1)}, f32[712,256]{1,0:T(8,128)S(1)}, u32[]{:S(2)}, u32[]{:S(2)}) collective-permute-start(f32[712,256]{1,0:T(8,128)S(1)} %get-tuple-element.92), channel_id=1, source_target_pairs={{1,4},{4,1},{3,6},{6,3},{5,8},{8,5},{7,10},{10,7},{9,12},{12,9},{1... | collective-permute-start | bytes 2187272 | tf_op jit(solution)/shard_map/ppermute | solution.py:645
  104.2 13.9 %collective-permute-start.24 = (f32[712,256]{1,0:T(8,128)S(1)}, f32[712,256]{1,0:T(8,128)S(1)}, u32[]{:S(2)}, u32[]{:S(2)}) collective-permute-start(f32[712,256]{1,0:T(8,128)S(1)} %get-tuple-element.90), channel_id=1, source_target_pairs={{1,4},{4,1},{3,6},{6,3},{5,8},{8,5},{7,10},{10,7},{9,12},{12,9},{1... | collective-permute-start | bytes 2187272 | tf_op jit(solution)/shard_map/ppermute | solution.py:645
  110.8 21.5 %collective-permute-start.31 = (f32[648,256]{1,0:T(8,128)S(1)}, f32[648,256]{1,0:T(8,128)S(1)}, u32[]{:S(2)}, u32[]{:S(2)}) collective-permute-start(f32[648,256]{1,0:T(8,128)S(1)} %get-tuple-element.103), channel_id=1, source_target_pairs={{0,2},{1,3},{2,0},{3,1},{4,6},{5,7},{6,4},{7,5},{8,10},{9,11},{10,... | collective-permute-start | bytes 1990664 | tf_op jit(solution)/shard_map/ppermute | solution.py:637
  120.1 8.7 %collective-permute-start.30 = (f32[320,256]{1,0:T(8,128)S(1)}, f32[320,256]{1,0:T(8,128)S(1)}, u32[]{:S(2)}, u32[]{:S(2)}) collective-permute-start(f32[320,256]{1,0:T(8,128)S(1)} %get-tuple-element.101), channel_id=1, source_target_pairs={{1,4},{4,1},{3,6},{6,3},{5,8},{8,5},{7,10},{10,7},{9,12},{12,9},{1... | collective-permute-start | bytes 983048 | tf_op jit(solution)/shard_map/ppermute | solution.py:645
  123.4 8.9 %collective-permute-start.29 = (f32[320,256]{1,0:T(8,128)S(1)}, f32[320,256]{1,0:T(8,128)S(1)}, u32[]{:S(2)}, u32[]{:S(2)}) collective-permute-start(f32[320,256]{1,0:T(8,128)S(1)} %get-tuple-element.99), channel_id=1, source_target_pairs={{1,4},{4,1},{3,6},{6,3},{5,8},{8,5},{7,10},{10,7},{9,12},{12,9},{1... | collective-permute-start | bytes 983048 | tf_op jit(solution)/shard_map/ppermute | solution.py:717
  129.1 9.5 %collective-permute-start.33 = (f32[4,80,256]{2,1,0:T(8,128)S(1)}, f32[4,80,256]{2,1,0:T(8,128)S(1)}, u32[]{:S(2)}, u32[]{:S(2)}) collective-permute-start(f32[4,80,256]{2,1,0:T(8,128)S(1)} %get-tuple-element.106), channel_id=1, source_target_pairs={{0,2},{1,3},{2,0},{3,1},{4,6},{5,7},{6,4},{7,5},{8,10},{9,11},{10,... | collective-permute-start | bytes 983048 | tf_op jit(solution)/shard_map/ppermute | solution.py:637
  132.6 13.0 %collective-permute-start.32 = (f32[4,80,256]{2,1,0:T(8,128)S(1)}, f32[4,80,256]{2,1,0:T(8,128)S(1)}, u32[]{:S(2)}, u32[]{:S(2)}) collective-permute-start(f32[4,80,256]{2,1,0:T(8,128)S(1)} %get-tuple-element.104), channel_id=1, source_target_pairs={{0,2},{1,3},{2,0},{3,1},{4,6},{5,7},{6,4},{7,5},{8,10},{9,11},{10,... | collective-permute-start | bytes 983048 | tf_op jit(solution)/shard_map/ppermute | solution.py:637
  (24 other events, 114.7 us)

commit v6 on v5

--- a/solution.py
+++ b/solution.py
@@ -286,7 +286,8 @@
                 field.at[:, sizes.window(1 - half), :],
                 out.at[pl.ds(0, sizes.rows * sizes.wide)].reshape(sizes.block),
             )
-            out[sizes.moved_tail, :] = jnp.zeros((16, sizes.depth), F32)
+            tail = pl.ds(sizes.rows * sizes.wide, 8)
+            out[tail, :] = jnp.zeros((8, sizes.depth), F32)
         copies.wait()
 
     return run(
@@ -294,7 +295,7 @@
         "pack",
         (adjoint, wave),
         [ANY] * 2,
-        [(sizes.moved, VMEM)] * 4,
+        [(sizes.edge, VMEM)] * 4,
         limit=PACK_LIMIT,
         sems=4,
     )

time: 147 us -> 146 us (level)
  starting transfers between devices: 41.4 us -> 44 us
  waiting for transfers between devices: 43.9 us -> 41.3 us
  local copies, waits for them, and re-layouts: 5.32 us -> 3.35 us
    ppermute x8, starting transfers between devices: 23.5 us -> 26 us  [exchange(): lax.ppermute(edge, 'gx', levels)]
    unnamed x30 -> x26, local copies, waits for them, and re-layouts: 5.21 us -> 3.24 us
    ppermute x9, waiting for transfers between devices: 30.6 us -> 28.7 us  [over(): return lax.ppermute(field, 'gx', across)]
    ppermute x8, waiting for transfers between devices: 9.85 us -> 8.2 us  [exchange(): lax.ppermute(edge, 'gx', levels)]
  transfers between devices with their start and end apart: 34 -> 34, of which waited for: 13 -> 14; matrix products, arithmetic and copies ran while one was open for 0% -> 0% of each run, Pallas kernels for 25% -> 26%
where the time goes in v6:
time: 146 us
  starting transfers between devices  44 us (30%)
  waiting for transfers between devices  41.3 us (28%)
  Pallas kernels  38 us (26%)
  blocking collectives  17.1 us (12%)
  local copies, waits for them, and re-layouts  3.35 us (2%)
  between operations  1.94 us (1%)
    pallas_call x26, Pallas kernels, run(): pl.pallas_call(body, name=name, out_shape=[jax.ShapeDtypeStruct(shape, F3...  38 us
    ppermute x9, waiting for transfers between devices, over(): return lax.ppermute(field, 'gx', across)  28.7 us
    ppermute x8, starting transfers between devices, exchange(): lax.ppermute(edge, 'gx', levels)  26 us
    all_gather x1, blocking collectives, on_device(): tails = lax.all_gather(tails, 'gx', axis_index_groups=halves)  17.1 us
    ppermute x8, waiting for transfers between devices, exchange(): lax.ppermute(edge, 'gx', levels)  8.2 us
    ppermute x9, starting transfers between devices, over(): return lax.ppermute(field, 'gx', across)  7.55 us
    ppermute x8, starting transfers between devices, exchange(): lax.ppermute(block0, 'gx', cores)  5.45 us
    unnamed x26, local copies, waits for them, and re-layouts  3.24 us
  transfers between devices with their start and end apart: 34, of which 14 were waited for; matrix products, arithmetic and copies ran while one was open for 0% of the time, Pallas kernels for 26%

profile of v6, /device:TPU:11, one launch (start us, length us, event | category | flops | bytes accessed | tf_op | source)
XLA Modules:
  0.0 145.8 jit_solution(5173030440335789863)
XLA Ops:
  4.1 3.4 %pack.1 = (f32[712,256]{1,0:T(8,128)}, f32[712,256]{1,0:T(8,128)}, f32[712,256]{1,0:T(8,128)}, f32[712,256]{1,0:T(8,128)}) custom-call(f32[2,1,4,320,256]{4,3,2,1,0:T(8,128)} %a_ref.3, f32[2,1,4,320,256]{4,3,2,1,0:T(8,128)} %w_ref.3), custom_call_target="tpu_custom_call" | custom-call | tf_op jit(solution)/shard_map/pack/pallas_call | solution.py:240
  9.0 3.8 %keep.1 = (f32[4,176,256]{2,1,0:T(8,128)}, f32[4,176,256]{2,1,0:T(8,128)}, f32[4,176,256]{2,1,0:T(8,128)}, f32[4,176,256]{2,1,0:T(8,128)}, f32[4,176,256]{2,1,0:T(8,128)}) custom-call(f32[4,320,256]{2,1,0:T(8,128)} %field.1, f32[2,1,4,320,256]{4,3,2,1,0:T(8,128)} %a_ref.3, f32[2,1,4,320,256]{4,3,2,1,0:T(8,128)} %w_ref.3), custom_call_target="tpu_custom_call" | custom-call | tf_op jit(solution)/shard_map/keep/pallas_call | solution.py:240
  13.5 6.7 %collective-permute-done.1.moved_ref = f32[720,256]{1,0:T(8,128)S(1)} collective-permute-done((f32[720,256]{1,0:T(8,128)S(1)}, f32[720,256]{1,0:T(8,128)S(1)}, u32[]{:S(2)}, u32[]{:S(2)}) %collective-permute-start.1) | collective-permute-done | bytes 737312 | tf_op jit(solution)/shard_map/ppermute | solution.py:638
  21.5 17.1 %all-gather = f32[16,16,256]{2,1,0:T(8,128)S(1)} all-gather(f32[2,16,256]{2,1,0:T(8,128)S(1)} %get-tuple-element.61), channel_id=2, replica_groups={{0,1,4,5,8,9,12,13},{2,3,6,7,10,11,14,15},{16,17,20,21,24,25,28,29},{18..., dimensions={0}, use_global_device_ids=true | all-gather | bytes 294912 | tf_op jit(solution)/shard_map/all_gather | solution.py:655
  40.4 2.9 %collective-permute-start.5 = (f32[712,256]{1,0:T(8,128)S(1)}, f32[712,256]{1,0:T(8,128)S(1)}, u32[]{:S(2)}, u32[]{:S(2)}) collective-permute-start(f32[712,256]{1,0:T(8,128)S(1)} %get-tuple-element.64), channel_id=1, source_target_pairs={{1,4},{4,1},{3,6},{6,3},{5,8},{8,5},{7,10},{10,7},{9,12},{12,9},{1... | collective-permute-start | bytes 2187272 | tf_op jit(solution)/shard_map/ppermute | solution.py:646
  46.6 2.5 %prepare_adjoint_4.1.refs_0_ = f32[2,4,176,256]{3,2,1,0:T(8,128)S(1)} custom-call(f32[4,176,256]{2,1,0:T(8,128)S(1)} %get-tuple-element.62.refs_0_, f32[4,176,256]{2,1,0:T(8,128)S(1)} %get-tuple-element.63.refs_1_, f32[4,176,256]{2,1,0:T(8,128)S(1)} %collective-permute-done.3.refs_2_, f32[4,176,256]{2,1,0:T(8,128)S(1)} %collective-permute-done.4.refs_3_, ...), custom_call_target="tpu_custom_call" | custom-call | tf_op jit(solution)/shard_map/prepare_adjoint_4/pallas_call | solution.py:240
  49.0 2.5 %collective-permute-done.6.refs_5_ = f32[712,256]{1,0:T(8,128)} collective-permute-done((f32[712,256]{1,0:T(8,128)}, f32[712,256]{1,0:T(8,128)}, u32[]{:S(2)}, u32[]{:S(2)}) %collective-permute-start.6) | collective-permute-done | bytes 729120 | tf_op jit(solution)/shard_map/ppermute | solution.py:638
  55.4 3.9 %collective-permute-start.16 = (f32[712,256]{1,0:T(8,128)S(1)}, f32[712,256]{1,0:T(8,128)S(1)}, u32[]{:S(2)}, u32[]{:S(2)}) collective-permute-start(f32[712,256]{1,0:T(8,128)S(1)} %get-tuple-element.78), channel_id=1, source_target_pairs={{1,4},{4,1},{3,6},{6,3},{5,8},{8,5},{7,10},{10,7},{9,12},{12,9},{1... | collective-permute-start | bytes 2187272 | tf_op jit(solution)/shard_map/ppermute | solution.py:646
  61.4 5.7 %collective-permute-done.moved_ref = f32[712,256]{1,0:T(8,128)S(1)} collective-permute-done((f32[712,256]{1,0:T(8,128)S(1)}, f32[712,256]{1,0:T(8,128)S(1)}, u32[]{:S(2)}, u32[]{:S(2)}) %collective-permute-start) | collective-permute-done | bytes 729120 | tf_op jit(solution)/shard_map/ppermute | solution.py:638
  67.4 2.8 %collective-permute-start.7 = (f32[4,176,256]{2,1,0:T(8,128)S(1)}, f32[4,176,256]{2,1,0:T(8,128)S(1)}, u32[]{:S(2)}, u32[]{:S(2)}) collective-permute-start(f32[4,176,256]{2,1,0:T(8,128)S(1)} %get-tuple-element.69.refs_0_.refs_1_.refs_5_.refs_8_), channel_id=1, source_target_pairs={{0,1},{1,0},{2,3},{3,2},{4,5},{5,4},{6,7},{7,6},{8,9},{9,8},{10,11... | collective-permute-start | bytes 2162696 | tf_op jit(solution)/shard_map/ppermute | solution.py:644
  70.1 3.1 %collective-permute-start.10 = (f32[712,256]{1,0:T(8,128)S(1)}, f32[712,256]{1,0:T(8,128)S(1)}, u32[]{:S(2)}, u32[]{:S(2)}) collective-permute-start(f32[712,256]{1,0:T(8,128)S(1)} %get-tuple-element.72), channel_id=1, source_target_pairs={{1,4},{4,1},{3,6},{6,3},{5,8},{8,5},{7,10},{10,7},{9,12},{12,9},{1... | collective-permute-start | bytes 2187272 | tf_op jit(solution)/shard_map/ppermute | solution.py:646
  73.3 2.5 %prepare_adjoint_3.1.refs_0_ = f32[2,4,176,256]{3,2,1,0:T(8,128)S(1)} custom-call(f32[4,176,256]{2,1,0:T(8,128)S(1)} %get-tuple-element.68.rest_0_.refs_0_, f32[4,176,256]{2,1,0:T(8,128)S(1)} %get-tuple-element.77.refs_1_, f32[4,176,256]{2,1,0:T(8,128)S(1)} %collective-permute-done.14.refs_2_, f32[4,176,256]{2,1,0:T(8,128)S(1)} %collective-permute-done.15.refs_3_, ...), custom_call_target="tpu_custom_call" | custom-call | tf_op jit(solution)/shard_map/prepare_adjoint_3/pallas_call | solution.py:240
  76.4 3.6 %collective-permute-start.19 = (f32[712,256]{1,0:T(8,128)S(1)}, f32[712,256]{1,0:T(8,128)S(1)}, u32[]{:S(2)}, u32[]{:S(2)}) collective-permute-start(f32[712,256]{1,0:T(8,128)S(1)} %get-tuple-element.82), channel_id=1, source_target_pairs={{1,4},{4,1},{3,6},{6,3},{5,8},{8,5},{7,10},{10,7},{9,12},{12,9},{1... | collective-permute-start | bytes 2187272 | tf_op jit(solution)/shard_map/ppermute | solution.py:646
  80.0 2.7 %collective-permute-done.9.refs_4_.refs_6_ = f32[712,256]{1,0:T(8,128)S(1)} collective-permute-done((f32[712,256]{1,0:T(8,128)S(1)}, f32[712,256]{1,0:T(8,128)S(1)}, u32[]{:S(2)}, u32[]{:S(2)}) %collective-permute-start.9) | collective-permute-done | bytes 729120 | tf_op jit(solution)/shard_map/ppermute | solution.py:638
  87.4 3.6 %collective-permute-start.13 = (f32[712,256]{1,0:T(8,128)S(1)}, f32[712,256]{1,0:T(8,128)S(1)}, u32[]{:S(2)}, u32[]{:S(2)}) collective-permute-start(f32[712,256]{1,0:T(8,128)S(1)} %get-tuple-element.76), channel_id=1, source_target_pairs={{1,4},{4,1},{3,6},{6,3},{5,8},{8,5},{7,10},{10,7},{9,12},{12,9},{1... | collective-permute-start | bytes 2187272 | tf_op jit(solution)/shard_map/ppermute | solution.py:646
  91.6 2.5 %prepare_adjoint_2.1.refs_0_ = f32[2,4,176,256]{3,2,1,0:T(8,128)S(1)} custom-call(f32[4,176,256]{2,1,0:T(8,128)S(1)} %get-tuple-element.80.refs_0_, f32[4,176,256]{2,1,0:T(8,128)S(1)} %get-tuple-element.81.refs_1_, f32[4,176,256]{2,1,0:T(8,128)S(1)} %collective-permute-done.17.refs_2_, f32[4,176,256]{2,1,0:T(8,128)S(1)} %collective-permute-done.18.refs_3_, ...), custom_call_target="tpu_custom_call" | custom-call | tf_op jit(solution)/shard_map/prepare_adjoint_2/pallas_call | solution.py:240
  96.6 3.5 %collective-permute-start.25 = (f32[712,256]{1,0:T(8,128)S(1)}, f32[712,256]{1,0:T(8,128)S(1)}, u32[]{:S(2)}, u32[]{:S(2)}) collective-permute-start(f32[712,256]{1,0:T(8,128)S(1)} %get-tuple-element.92), channel_id=1, source_target_pairs={{1,4},{4,1},{3,6},{6,3},{5,8},{8,5},{7,10},{10,7},{9,12},{12,9},{1... | collective-permute-start | bytes 2187272 | tf_op jit(solution)/shard_map/ppermute | solution.py:646
  106.3 2.5 %prepare_adjoint_1.1.refs_0_ = f32[2,4,176,256]{3,2,1,0:T(8,128)S(1)} custom-call(f32[4,176,256]{2,1,0:T(8,128)S(1)} %get-tuple-element.86.refs_0_, f32[4,176,256]{2,1,0:T(8,128)S(1)} %get-tuple-element.87.refs_1_, f32[4,176,256]{2,1,0:T(8,128)S(1)} %collective-permute-done.20.refs_13_.refs_2_, f32[4,176,256]{2,1,0:T(8,128)S(1)} %collective-permute-done.21.refs_14_.refs_3_, ...), custom_call_target="tpu_custom_call" | custom-call | tf_op jit(solution)/shard_map/prepare_adjoint_1/pallas_call | solution.py:240
  113.3 4.1 %collective-permute-done.24.refs_3_ = f32[712,256]{1,0:T(8,128)S(1)} collective-permute-done((f32[712,256]{1,0:T(8,128)S(1)}, f32[712,256]{1,0:T(8,128)S(1)}, u32[]{:S(2)}, u32[]{:S(2)}) %collective-permute-start.24) | collective-permute-done | bytes 729120 | tf_op jit(solution)/shard_map/ppermute | solution.py:646
  119.4 3.2 %collective-permute-start.30 = (f32[320,256]{1,0:T(8,128)S(1)}, f32[320,256]{1,0:T(8,128)S(1)}, u32[]{:S(2)}, u32[]{:S(2)}) collective-permute-start(f32[320,256]{1,0:T(8,128)S(1)} %get-tuple-element.101), channel_id=1, source_target_pairs={{1,4},{4,1},{3,6},{6,3},{5,8},{8,5},{7,10},{10,7},{9,12},{12,9},{1... | collective-permute-start | bytes 983048 | tf_op jit(solution)/shard_map/ppermute | solution.py:646
  122.6 2.3 %collective-permute-start.29 = (f32[320,256]{1,0:T(8,128)S(1)}, f32[320,256]{1,0:T(8,128)S(1)}, u32[]{:S(2)}, u32[]{:S(2)}) collective-permute-start(f32[320,256]{1,0:T(8,128)S(1)} %get-tuple-element.99), channel_id=1, source_target_pairs={{1,4},{4,1},{3,6},{6,3},{5,8},{8,5},{7,10},{10,7},{9,12},{12,9},{1... | collective-permute-start | bytes 983048 | tf_op jit(solution)/shard_map/ppermute | solution.py:718
  128.7 2.9 %collective-permute-done.29.beside_ref = f32[320,256]{1,0:T(8,128)S(1)} collective-permute-done((f32[320,256]{1,0:T(8,128)S(1)}, f32[320,256]{1,0:T(8,128)S(1)}, u32[]{:S(2)}, u32[]{:S(2)}) %collective-permute-start.29) | collective-permute-done | bytes 327712 | tf_op jit(solution)/shard_map/ppermute | solution.py:718
  133.7 4.1 %collective-permute-done.33.refs_2_ = f32[4,80,256]{2,1,0:T(8,128)S(1)} collective-permute-done((f32[4,80,256]{2,1,0:T(8,128)S(1)}, f32[4,80,256]{2,1,0:T(8,128)S(1)}, u32[]{:S(2)}, u32[]{:S(2)}) %collective-permute-start.33) | collective-permute-done | bytes 327712 | tf_op jit(solution)/shard_map/ppermute | solution.py:638
  138.8 6.0 %collective-permute-done.32.refs_0_ = f32[4,80,256]{2,1,0:T(8,128)S(1)} collective-permute-done((f32[4,80,256]{2,1,0:T(8,128)S(1)}, f32[4,80,256]{2,1,0:T(8,128)S(1)}, u32[]{:S(2)}, u32[]{:S(2)}) %collective-permute-start.32) | collective-permute-done | bytes 327712 | tf_op jit(solution)/shard_map/ppermute | solution.py:638
  (100 shorter events, 46.0 us)
Async XLA Ops:
  2.8 17.4 %collective-permute-start.1 = (f32[720,256]{1,0:T(8,128)S(1)}, f32[720,256]{1,0:T(8,128)S(1)}, u32[]{:S(2)}, u32[]{:S(2)}) collective-permute-start(f32[720,256]{1,0:T(8,128)S(1)} %pack_first.1.sent_ref), channel_id=1, source_target_pairs={{0,2},{1,3},{2,0},{3,1},{4,6},{5,7},{6,4},{7,5},{8,10},{9,11},{10,... | collective-permute-start | bytes 2211848 | tf_op jit(solution)/shard_map/ppermute | solution.py:638
  7.5 31.3 %collective-permute-start.2 = (f32[712,256]{1,0:T(8,128)}, f32[712,256]{1,0:T(8,128)}, u32[]{:S(2)}, u32[]{:S(2)}) collective-permute-start(f32[712,256]{1,0:T(8,128)} %get-tuple-element.60), channel_id=1, source_target_pairs={{0,2},{1,3},{2,0},{3,1},{4,6},{5,7},{6,4},{7,5},{8,10},{9,11},{10,... | collective-permute-start | bytes 2187272 | tf_op jit(solution)/shard_map/ppermute | solution.py:638
  7.8 43.8 %collective-permute-start.6 = (f32[712,256]{1,0:T(8,128)}, f32[712,256]{1,0:T(8,128)}, u32[]{:S(2)}, u32[]{:S(2)}) collective-permute-start(f32[712,256]{1,0:T(8,128)} %get-tuple-element.67), channel_id=1, source_target_pairs={{0,2},{1,3},{2,0},{3,1},{4,6},{5,7},{6,4},{7,5},{8,10},{9,11},{10,... | collective-permute-start | bytes 2187272 | tf_op jit(solution)/shard_map/ppermute | solution.py:638
  40.4 13.1 %collective-permute-start.5 = (f32[712,256]{1,0:T(8,128)S(1)}, f32[712,256]{1,0:T(8,128)S(1)}, u32[]{:S(2)}, u32[]{:S(2)}) collective-permute-start(f32[712,256]{1,0:T(8,128)S(1)} %get-tuple-element.64), channel_id=1, source_target_pairs={{1,4},{4,1},{3,6},{6,3},{5,8},{8,5},{7,10},{10,7},{9,12},{12,9},{1... | collective-permute-start | bytes 2187272 | tf_op jit(solution)/shard_map/ppermute | solution.py:646
  43.8 23.2 %collective-permute-start = (f32[712,256]{1,0:T(8,128)S(1)}, f32[712,256]{1,0:T(8,128)S(1)}, u32[]{:S(2)}, u32[]{:S(2)}) collective-permute-start(f32[712,256]{1,0:T(8,128)S(1)} %copy-done.11), channel_id=1, source_target_pairs={{0,2},{1,3},{2,0},{3,1},{4,6},{5,7},{6,4},{7,5},{8,10},{9,11},{10,... | collective-permute-start | bytes 2187272 | tf_op jit(solution)/shard_map/ppermute | solution.py:638
  55.4 18.0 %collective-permute-start.16 = (f32[712,256]{1,0:T(8,128)S(1)}, f32[712,256]{1,0:T(8,128)S(1)}, u32[]{:S(2)}, u32[]{:S(2)}) collective-permute-start(f32[712,256]{1,0:T(8,128)S(1)} %get-tuple-element.78), channel_id=1, source_target_pairs={{1,4},{4,1},{3,6},{6,3},{5,8},{8,5},{7,10},{10,7},{9,12},{12,9},{1... | collective-permute-start | bytes 2187272 | tf_op jit(solution)/shard_map/ppermute | solution.py:646
  59.3 10.9 %collective-permute-start.14 = (f32[4,176,256]{2,1,0:T(8,128)S(1)}, f32[4,176,256]{2,1,0:T(8,128)S(1)}, u32[]{:S(2)}, u32[]{:S(2)}) collective-permute-start(f32[4,176,256]{2,1,0:T(8,128)S(1)} %get-tuple-element.68.rest_0_.refs_0_), channel_id=1, source_target_pairs={{0,1},{1,0},{2,3},{3,2},{4,5},{5,4},{6,7},{7,6},{8,9},{9,8},{10,11... | collective-permute-start | bytes 2162696 | tf_op jit(solution)/shard_map/ppermute | solution.py:644
  59.4 23.3 %collective-permute-start.9 = (f32[712,256]{1,0:T(8,128)S(1)}, f32[712,256]{1,0:T(8,128)S(1)}, u32[]{:S(2)}, u32[]{:S(2)}) collective-permute-start(f32[712,256]{1,0:T(8,128)S(1)} %copy-done.10), channel_id=1, source_target_pairs={{0,2},{1,3},{2,0},{3,1},{4,6},{5,7},{6,4},{7,5},{8,10},{9,11},{10,... | collective-permute-start | bytes 2187272 | tf_op jit(solution)/shard_map/ppermute | solution.py:638
  60.7 12.6 %collective-permute-start.15 = (f32[4,176,256]{2,1,0:T(8,128)S(1)}, f32[4,176,256]{2,1,0:T(8,128)S(1)}, u32[]{:S(2)}, u32[]{:S(2)}) collective-permute-start(f32[4,176,256]{2,1,0:T(8,128)S(1)} %get-tuple-element.77.refs_1_), channel_id=1, source_target_pairs={{0,1},{1,0},{2,3},{3,2},{4,5},{5,4},{6,7},{7,6},{8,9},{9,8},{10,11... | collective-permute-start | bytes 2162696 | tf_op jit(solution)/shard_map/ppermute | solution.py:645
  67.4 16.9 %collective-permute-start.7 = (f32[4,176,256]{2,1,0:T(8,128)S(1)}, f32[4,176,256]{2,1,0:T(8,128)S(1)}, u32[]{:S(2)}, u32[]{:S(2)}) collective-permute-start(f32[4,176,256]{2,1,0:T(8,128)S(1)} %get-tuple-element.69.refs_0_.refs_1_.refs_5_.refs_8_), channel_id=1, source_target_pairs={{0,1},{1,0},{2,3},{3,2},{4,5},{5,4},{6,7},{7,6},{8,9},{9,8},{10,11... | collective-permute-start | bytes 2162696 | tf_op jit(solution)/shard_map/ppermute | solution.py:644
  70.1 16.1 %collective-permute-start.10 = (f32[712,256]{1,0:T(8,128)S(1)}, f32[712,256]{1,0:T(8,128)S(1)}, u32[]{:S(2)}, u32[]{:S(2)}) collective-permute-start(f32[712,256]{1,0:T(8,128)S(1)} %get-tuple-element.72), channel_id=1, source_target_pairs={{1,4},{4,1},{3,6},{6,3},{5,8},{8,5},{7,10},{10,7},{9,12},{12,9},{1... | collective-permute-start | bytes 2187272 | tf_op jit(solution)/shard_map/ppermute | solution.py:646
  73.3 11.1 %collective-permute-start.8 = (f32[4,176,256]{2,1,0:T(8,128)S(1)}, f32[4,176,256]{2,1,0:T(8,128)S(1)}, u32[]{:S(2)}, u32[]{:S(2)}) collective-permute-start(f32[4,176,256]{2,1,0:T(8,128)S(1)} %get-tuple-element.70.refs_1_.refs_2_.refs_9_), channel_id=1, source_target_pairs={{0,1},{1,0},{2,3},{3,2},{4,5},{5,4},{6,7},{7,6},{8,9},{9,8},{10,11... | collective-permute-start | bytes 2162696 | tf_op jit(solution)/shard_map/ppermute | solution.py:645
  76.4 17.7 %collective-permute-start.19 = (f32[712,256]{1,0:T(8,128)S(1)}, f32[712,256]{1,0:T(8,128)S(1)}, u32[]{:S(2)}, u32[]{:S(2)}) collective-permute-start(f32[712,256]{1,0:T(8,128)S(1)} %get-tuple-element.82), channel_id=1, source_target_pairs={{1,4},{4,1},{3,6},{6,3},{5,8},{8,5},{7,10},{10,7},{9,12},{12,9},{1... | collective-permute-start | bytes 2187272 | tf_op jit(solution)/shard_map/ppermute | solution.py:646
  82.7 8.4 %collective-permute-start.17 = (f32[4,176,256]{2,1,0:T(8,128)S(1)}, f32[4,176,256]{2,1,0:T(8,128)S(1)}, u32[]{:S(2)}, u32[]{:S(2)}) collective-permute-start(f32[4,176,256]{2,1,0:T(8,128)S(1)} %get-tuple-element.80.refs_0_), channel_id=1, source_target_pairs={{0,1},{1,0},{2,3},{3,2},{4,5},{5,4},{6,7},{7,6},{8,9},{9,8},{10,11... | collective-permute-start | bytes 2162696 | tf_op jit(solution)/shard_map/ppermute | solution.py:644
  84.2 7.4 %collective-permute-start.18 = (f32[4,176,256]{2,1,0:T(8,128)S(1)}, f32[4,176,256]{2,1,0:T(8,128)S(1)}, u32[]{:S(2)}, u32[]{:S(2)}) collective-permute-start(f32[4,176,256]{2,1,0:T(8,128)S(1)} %get-tuple-element.81.refs_1_), channel_id=1, source_target_pairs={{0,1},{1,0},{2,3},{3,2},{4,5},{5,4},{6,7},{7,6},{8,9},{9,8},{10,11... | collective-permute-start | bytes 2162696 | tf_op jit(solution)/shard_map/ppermute | solution.py:645
  87.4 14.6 %collective-permute-start.13 = (f32[712,256]{1,0:T(8,128)S(1)}, f32[712,256]{1,0:T(8,128)S(1)}, u32[]{:S(2)}, u32[]{:S(2)}) collective-permute-start(f32[712,256]{1,0:T(8,128)S(1)} %get-tuple-element.76), channel_id=1, source_target_pairs={{1,4},{4,1},{3,6},{6,3},{5,8},{8,5},{7,10},{10,7},{9,12},{12,9},{1... | collective-permute-start | bytes 2187272 | tf_op jit(solution)/shard_map/ppermute | solution.py:646
  95.4 18.0 %collective-permute-start.26 = (f32[720,256]{1,0:T(8,128)S(1)}, f32[720,256]{1,0:T(8,128)S(1)}, u32[]{:S(2)}, u32[]{:S(2)}) collective-permute-start(f32[720,256]{1,0:T(8,128)S(1)} %get-tuple-element.94), channel_id=1, source_target_pairs={{0,2},{1,3},{2,0},{3,1},{4,6},{5,7},{6,4},{7,5},{8,10},{9,11},{10,... | collective-permute-start | bytes 2211848 | tf_op jit(solution)/shard_map/ppermute | solution.py:638
  96.6 13.0 %collective-permute-start.25 = (f32[712,256]{1,0:T(8,128)S(1)}, f32[712,256]{1,0:T(8,128)S(1)}, u32[]{:S(2)}, u32[]{:S(2)}) collective-permute-start(f32[712,256]{1,0:T(8,128)S(1)} %get-tuple-element.92), channel_id=1, source_target_pairs={{1,4},{4,1},{3,6},{6,3},{5,8},{8,5},{7,10},{10,7},{9,12},{12,9},{1... | collective-permute-start | bytes 2187272 | tf_op jit(solution)/shard_map/ppermute | solution.py:646
  103.5 13.9 %collective-permute-start.24 = (f32[712,256]{1,0:T(8,128)S(1)}, f32[712,256]{1,0:T(8,128)S(1)}, u32[]{:S(2)}, u32[]{:S(2)}) collective-permute-start(f32[712,256]{1,0:T(8,128)S(1)} %get-tuple-element.90), channel_id=1, source_target_pairs={{1,4},{4,1},{3,6},{6,3},{5,8},{8,5},{7,10},{10,7},{9,12},{12,9},{1... | collective-permute-start | bytes 2187272 | tf_op jit(solution)/shard_map/ppermute | solution.py:646
  110.1 21.5 %collective-permute-start.31 = (f32[648,256]{1,0:T(8,128)S(1)}, f32[648,256]{1,0:T(8,128)S(1)}, u32[]{:S(2)}, u32[]{:S(2)}) collective-permute-start(f32[648,256]{1,0:T(8,128)S(1)} %get-tuple-element.103), channel_id=1, source_target_pairs={{0,2},{1,3},{2,0},{3,1},{4,6},{5,7},{6,4},{7,5},{8,10},{9,11},{10,... | collective-permute-start | bytes 1990664 | tf_op jit(solution)/shard_map/ppermute | solution.py:638
  119.4 8.7 %collective-permute-start.30 = (f32[320,256]{1,0:T(8,128)S(1)}, f32[320,256]{1,0:T(8,128)S(1)}, u32[]{:S(2)}, u32[]{:S(2)}) collective-permute-start(f32[320,256]{1,0:T(8,128)S(1)} %get-tuple-element.101), channel_id=1, source_target_pairs={{1,4},{4,1},{3,6},{6,3},{5,8},{8,5},{7,10},{10,7},{9,12},{12,9},{1... | collective-permute-start | bytes 983048 | tf_op jit(solution)/shard_map/ppermute | solution.py:646
  122.6 8.9 %collective-permute-start.29 = (f32[320,256]{1,0:T(8,128)S(1)}, f32[320,256]{1,0:T(8,128)S(1)}, u32[]{:S(2)}, u32[]{:S(2)}) collective-permute-start(f32[320,256]{1,0:T(8,128)S(1)} %get-tuple-element.99), channel_id=1, source_target_pairs={{1,4},{4,1},{3,6},{6,3},{5,8},{8,5},{7,10},{10,7},{9,12},{12,9},{1... | collective-permute-start | bytes 983048 | tf_op jit(solution)/shard_map/ppermute | solution.py:718
  128.4 9.5 %collective-permute-start.33 = (f32[4,80,256]{2,1,0:T(8,128)S(1)}, f32[4,80,256]{2,1,0:T(8,128)S(1)}, u32[]{:S(2)}, u32[]{:S(2)}) collective-permute-start(f32[4,80,256]{2,1,0:T(8,128)S(1)} %get-tuple-element.106), channel_id=1, source_target_pairs={{0,2},{1,3},{2,0},{3,1},{4,6},{5,7},{6,4},{7,5},{8,10},{9,11},{10,... | collective-permute-start | bytes 983048 | tf_op jit(solution)/shard_map/ppermute | solution.py:638
  131.9 13.0 %collective-permute-start.32 = (f32[4,80,256]{2,1,0:T(8,128)S(1)}, f32[4,80,256]{2,1,0:T(8,128)S(1)}, u32[]{:S(2)}, u32[]{:S(2)}) collective-permute-start(f32[4,80,256]{2,1,0:T(8,128)S(1)} %get-tuple-element.104), channel_id=1, source_target_pairs={{0,2},{1,3},{2,0},{3,1},{4,6},{5,7},{6,4},{7,5},{8,10},{9,11},{10,... | collective-permute-start | bytes 983048 | tf_op jit(solution)/shard_map/ppermute | solution.py:638
  (22 other events, 114.5 us)

commit v7 on v6

--- a/solution.py
+++ b/solution.py
@@ -709,7 +709,7 @@
     )
     current3 = exchange(*current3, edge)
     prepared = ready_forward(3, current3)
-    mine0, sent0 = adjoint(1, partial, scaled[4], later1, (later2,), speed, current3[2:4])
+    mine0, sent0 = adjoint(1, partial, scaled[4], later1, (later2,), speed, current3[:1])
     got0 = over(sent0)
     *current4, gradient, narrow0, narrow1, edge0, edge1 = forward(
         3, *prepared, current2[:2], speed, (later3,), gradient, source, (mine0, got1)

time: 146 us -> 146 us (level)
  no operation moved by 1% of the time
where the time goes in v7:
time: 146 us
  starting transfers between devices  43.9 us (30%)
  waiting for transfers between devices  41.4 us (28%)
  Pallas kernels  38.1 us (26%)
  blocking collectives  17.1 us (12%)
  local copies, waits for them, and re-layouts  3.35 us (2%)
  between operations  1.94 us (1%)
    pallas_call x26, Pallas kernels, run(): pl.pallas_call(body, name=name, out_shape=[jax.ShapeDtypeStruct(shape, F3...  38.1 us
    ppermute x9, waiting for transfers between devices, over(): return lax.ppermute(field, 'gx', across)  28.8 us
    ppermute x8, starting transfers between devices, exchange(): lax.ppermute(edge, 'gx', levels)  26 us
    all_gather x1, blocking collectives, on_device(): tails = lax.all_gather(tails, 'gx', axis_index_groups=halves)  17.1 us
    ppermute x8, waiting for transfers between devices, exchange(): lax.ppermute(edge, 'gx', levels)  8.19 us
    ppermute x9, starting transfers between devices, over(): return lax.ppermute(field, 'gx', across)  7.49 us
    ppermute x8, starting transfers between devices, exchange(): lax.ppermute(block0, 'gx', cores)  5.45 us
    unnamed x26, local copies, waits for them, and re-layouts  3.24 us
  transfers between devices with their start and end apart: 34, of which 14 were waited for; matrix products, arithmetic and copies ran while one was open for 0% of the time, Pallas kernels for 26%

profile of v7, /device:TPU:11, one launch (start us, length us, event | category | flops | bytes accessed | tf_op | source)
XLA Modules:
  0.0 145.8 jit_solution(13539298675370968079)
XLA Ops:
  4.1 3.4 %pack.1 = (f32[712,256]{1,0:T(8,128)}, f32[712,256]{1,0:T(8,128)}, f32[712,256]{1,0:T(8,128)}, f32[712,256]{1,0:T(8,128)}) custom-call(f32[2,1,4,320,256]{4,3,2,1,0:T(8,128)} %a_ref.3, f32[2,1,4,320,256]{4,3,2,1,0:T(8,128)} %w_ref.3), custom_call_target="tpu_custom_call" | custom-call | tf_op jit(solution)/shard_map/pack/pallas_call | solution.py:240
  9.0 3.8 %keep.1 = (f32[4,176,256]{2,1,0:T(8,128)}, f32[4,176,256]{2,1,0:T(8,128)}, f32[4,176,256]{2,1,0:T(8,128)}, f32[4,176,256]{2,1,0:T(8,128)}, f32[4,176,256]{2,1,0:T(8,128)}) custom-call(f32[4,320,256]{2,1,0:T(8,128)} %field.1, f32[2,1,4,320,256]{4,3,2,1,0:T(8,128)} %a_ref.3, f32[2,1,4,320,256]{4,3,2,1,0:T(8,128)} %w_ref.3), custom_call_target="tpu_custom_call" | custom-call | tf_op jit(solution)/shard_map/keep/pallas_call | solution.py:240
  13.5 6.7 %collective-permute-done.1.moved_ref = f32[720,256]{1,0:T(8,128)S(1)} collective-permute-done((f32[720,256]{1,0:T(8,128)S(1)}, f32[720,256]{1,0:T(8,128)S(1)}, u32[]{:S(2)}, u32[]{:S(2)}) %collective-permute-start.1) | collective-permute-done | bytes 737312 | tf_op jit(solution)/shard_map/ppermute | solution.py:638
  21.5 17.1 %all-gather = f32[16,16,256]{2,1,0:T(8,128)S(1)} all-gather(f32[2,16,256]{2,1,0:T(8,128)S(1)} %get-tuple-element.61), channel_id=2, replica_groups={{0,1,4,5,8,9,12,13},{2,3,6,7,10,11,14,15},{16,17,20,21,24,25,28,29},{18..., dimensions={0}, use_global_device_ids=true | all-gather | bytes 294912 | tf_op jit(solution)/shard_map/all_gather | solution.py:655
  40.4 2.9 %collective-permute-start.5 = (f32[712,256]{1,0:T(8,128)S(1)}, f32[712,256]{1,0:T(8,128)S(1)}, u32[]{:S(2)}, u32[]{:S(2)}) collective-permute-start(f32[712,256]{1,0:T(8,128)S(1)} %get-tuple-element.64), channel_id=1, source_target_pairs={{1,4},{4,1},{3,6},{6,3},{5,8},{8,5},{7,10},{10,7},{9,12},{12,9},{1... | collective-permute-start | bytes 2187272 | tf_op jit(solution)/shard_map/ppermute | solution.py:646
  46.6 2.5 %prepare_adjoint_4.1.refs_0_ = f32[2,4,176,256]{3,2,1,0:T(8,128)S(1)} custom-call(f32[4,176,256]{2,1,0:T(8,128)S(1)} %get-tuple-element.62.refs_0_, f32[4,176,256]{2,1,0:T(8,128)S(1)} %get-tuple-element.63.refs_1_, f32[4,176,256]{2,1,0:T(8,128)S(1)} %collective-permute-done.3.refs_2_, f32[4,176,256]{2,1,0:T(8,128)S(1)} %collective-permute-done.4.refs_3_, ...), custom_call_target="tpu_custom_call" | custom-call | tf_op jit(solution)/shard_map/prepare_adjoint_4/pallas_call | solution.py:240
  49.0 2.5 %collective-permute-done.6.refs_5_ = f32[712,256]{1,0:T(8,128)} collective-permute-done((f32[712,256]{1,0:T(8,128)}, f32[712,256]{1,0:T(8,128)}, u32[]{:S(2)}, u32[]{:S(2)}) %collective-permute-start.6) | collective-permute-done | bytes 729120 | tf_op jit(solution)/shard_map/ppermute | solution.py:638
  55.4 3.9 %collective-permute-start.16 = (f32[712,256]{1,0:T(8,128)S(1)}, f32[712,256]{1,0:T(8,128)S(1)}, u32[]{:S(2)}, u32[]{:S(2)}) collective-permute-start(f32[712,256]{1,0:T(8,128)S(1)} %get-tuple-element.78), channel_id=1, source_target_pairs={{1,4},{4,1},{3,6},{6,3},{5,8},{8,5},{7,10},{10,7},{9,12},{12,9},{1... | collective-permute-start | bytes 2187272 | tf_op jit(solution)/shard_map/ppermute | solution.py:646
  61.4 5.7 %collective-permute-done.moved_ref = f32[712,256]{1,0:T(8,128)S(1)} collective-permute-done((f32[712,256]{1,0:T(8,128)S(1)}, f32[712,256]{1,0:T(8,128)S(1)}, u32[]{:S(2)}, u32[]{:S(2)}) %collective-permute-start) | collective-permute-done | bytes 729120 | tf_op jit(solution)/shard_map/ppermute | solution.py:638
  67.4 2.8 %collective-permute-start.7 = (f32[4,176,256]{2,1,0:T(8,128)S(1)}, f32[4,176,256]{2,1,0:T(8,128)S(1)}, u32[]{:S(2)}, u32[]{:S(2)}) collective-permute-start(f32[4,176,256]{2,1,0:T(8,128)S(1)} %get-tuple-element.69.refs_0_.refs_1_.refs_5_.refs_8_), channel_id=1, source_target_pairs={{0,1},{1,0},{2,3},{3,2},{4,5},{5,4},{6,7},{7,6},{8,9},{9,8},{10,11... | collective-permute-start | bytes 2162696 | tf_op jit(solution)/shard_map/ppermute | solution.py:644
  70.1 3.1 %collective-permute-start.10 = (f32[712,256]{1,0:T(8,128)S(1)}, f32[712,256]{1,0:T(8,128)S(1)}, u32[]{:S(2)}, u32[]{:S(2)}) collective-permute-start(f32[712,256]{1,0:T(8,128)S(1)} %get-tuple-element.72), channel_id=1, source_target_pairs={{1,4},{4,1},{3,6},{6,3},{5,8},{8,5},{7,10},{10,7},{9,12},{12,9},{1... | collective-permute-start | bytes 2187272 | tf_op jit(solution)/shard_map/ppermute | solution.py:646
  73.3 2.5 %prepare_adjoint_3.1.refs_0_ = f32[2,4,176,256]{3,2,1,0:T(8,128)S(1)} custom-call(f32[4,176,256]{2,1,0:T(8,128)S(1)} %get-tuple-element.68.rest_0_.refs_0_, f32[4,176,256]{2,1,0:T(8,128)S(1)} %get-tuple-element.77.refs_1_, f32[4,176,256]{2,1,0:T(8,128)S(1)} %collective-permute-done.14.refs_2_, f32[4,176,256]{2,1,0:T(8,128)S(1)} %collective-permute-done.15.refs_3_, ...), custom_call_target="tpu_custom_call" | custom-call | tf_op jit(solution)/shard_map/prepare_adjoint_3/pallas_call | solution.py:240
  76.4 3.6 %collective-permute-start.19 = (f32[712,256]{1,0:T(8,128)S(1)}, f32[712,256]{1,0:T(8,128)S(1)}, u32[]{:S(2)}, u32[]{:S(2)}) collective-permute-start(f32[712,256]{1,0:T(8,128)S(1)} %get-tuple-element.82), channel_id=1, source_target_pairs={{1,4},{4,1},{3,6},{6,3},{5,8},{8,5},{7,10},{10,7},{9,12},{12,9},{1... | collective-permute-start | bytes 2187272 | tf_op jit(solution)/shard_map/ppermute | solution.py:646
  80.0 2.7 %collective-permute-done.9.refs_4_.refs_6_ = f32[712,256]{1,0:T(8,128)S(1)} collective-permute-done((f32[712,256]{1,0:T(8,128)S(1)}, f32[712,256]{1,0:T(8,128)S(1)}, u32[]{:S(2)}, u32[]{:S(2)}) %collective-permute-start.9) | collective-permute-done | bytes 729120 | tf_op jit(solution)/shard_map/ppermute | solution.py:638
  87.4 3.6 %collective-permute-start.13 = (f32[712,256]{1,0:T(8,128)S(1)}, f32[712,256]{1,0:T(8,128)S(1)}, u32[]{:S(2)}, u32[]{:S(2)}) collective-permute-start(f32[712,256]{1,0:T(8,128)S(1)} %get-tuple-element.76), channel_id=1, source_target_pairs={{1,4},{4,1},{3,6},{6,3},{5,8},{8,5},{7,10},{10,7},{9,12},{12,9},{1... | collective-permute-start | bytes 2187272 | tf_op jit(solution)/shard_map/ppermute | solution.py:646
  91.6 2.5 %prepare_adjoint_2.1.refs_0_ = f32[2,4,176,256]{3,2,1,0:T(8,128)S(1)} custom-call(f32[4,176,256]{2,1,0:T(8,128)S(1)} %get-tuple-element.80.refs_0_, f32[4,176,256]{2,1,0:T(8,128)S(1)} %get-tuple-element.81.refs_1_, f32[4,176,256]{2,1,0:T(8,128)S(1)} %collective-permute-done.17.refs_2_, f32[4,176,256]{2,1,0:T(8,128)S(1)} %collective-permute-done.18.refs_3_, ...), custom_call_target="tpu_custom_call" | custom-call | tf_op jit(solution)/shard_map/prepare_adjoint_2/pallas_call | solution.py:240
  96.6 3.5 %collective-permute-start.25 = (f32[712,256]{1,0:T(8,128)S(1)}, f32[712,256]{1,0:T(8,128)S(1)}, u32[]{:S(2)}, u32[]{:S(2)}) collective-permute-start(f32[712,256]{1,0:T(8,128)S(1)} %get-tuple-element.92), channel_id=1, source_target_pairs={{1,4},{4,1},{3,6},{6,3},{5,8},{8,5},{7,10},{10,7},{9,12},{12,9},{1... | collective-permute-start | bytes 2187272 | tf_op jit(solution)/shard_map/ppermute | solution.py:646
  106.3 2.5 %prepare_adjoint_1.1.refs_0_ = f32[2,4,176,256]{3,2,1,0:T(8,128)S(1)} custom-call(f32[4,176,256]{2,1,0:T(8,128)S(1)} %get-tuple-element.86.refs_0_, f32[4,176,256]{2,1,0:T(8,128)S(1)} %get-tuple-element.87.refs_1_, f32[4,176,256]{2,1,0:T(8,128)S(1)} %collective-permute-done.20.refs_13_.refs_2_, f32[4,176,256]{2,1,0:T(8,128)S(1)} %collective-permute-done.21.refs_14_.refs_3_, ...), custom_call_target="tpu_custom_call" | custom-call | tf_op jit(solution)/shard_map/prepare_adjoint_1/pallas_call | solution.py:240
  113.3 4.1 %collective-permute-done.24.refs_3_ = f32[712,256]{1,0:T(8,128)S(1)} collective-permute-done((f32[712,256]{1,0:T(8,128)S(1)}, f32[712,256]{1,0:T(8,128)S(1)}, u32[]{:S(2)}, u32[]{:S(2)}) %collective-permute-start.24) | collective-permute-done | bytes 729120 | tf_op jit(solution)/shard_map/ppermute | solution.py:646
  119.4 3.2 %collective-permute-start.30 = (f32[320,256]{1,0:T(8,128)S(1)}, f32[320,256]{1,0:T(8,128)S(1)}, u32[]{:S(2)}, u32[]{:S(2)}) collective-permute-start(f32[320,256]{1,0:T(8,128)S(1)} %get-tuple-element.101), channel_id=1, source_target_pairs={{1,4},{4,1},{3,6},{6,3},{5,8},{8,5},{7,10},{10,7},{9,12},{12,9},{1... | collective-permute-start | bytes 983048 | tf_op jit(solution)/shard_map/ppermute | solution.py:646
  122.6 2.3 %collective-permute-start.29 = (f32[320,256]{1,0:T(8,128)S(1)}, f32[320,256]{1,0:T(8,128)S(1)}, u32[]{:S(2)}, u32[]{:S(2)}) collective-permute-start(f32[320,256]{1,0:T(8,128)S(1)} %get-tuple-element.99), channel_id=1, source_target_pairs={{1,4},{4,1},{3,6},{6,3},{5,8},{8,5},{7,10},{10,7},{9,12},{12,9},{1... | collective-permute-start | bytes 983048 | tf_op jit(solution)/shard_map/ppermute | solution.py:718
  128.7 2.9 %collective-permute-done.29.beside_ref = f32[320,256]{1,0:T(8,128)S(1)} collective-permute-done((f32[320,256]{1,0:T(8,128)S(1)}, f32[320,256]{1,0:T(8,128)S(1)}, u32[]{:S(2)}, u32[]{:S(2)}) %collective-permute-start.29) | collective-permute-done | bytes 327712 | tf_op jit(solution)/shard_map/ppermute | solution.py:718
  133.7 4.1 %collective-permute-done.33.refs_2_ = f32[4,80,256]{2,1,0:T(8,128)S(1)} collective-permute-done((f32[4,80,256]{2,1,0:T(8,128)S(1)}, f32[4,80,256]{2,1,0:T(8,128)S(1)}, u32[]{:S(2)}, u32[]{:S(2)}) %collective-permute-start.33) | collective-permute-done | bytes 327712 | tf_op jit(solution)/shard_map/ppermute | solution.py:638
  138.8 6.0 %collective-permute-done.32.refs_0_ = f32[4,80,256]{2,1,0:T(8,128)S(1)} collective-permute-done((f32[4,80,256]{2,1,0:T(8,128)S(1)}, f32[4,80,256]{2,1,0:T(8,128)S(1)}, u32[]{:S(2)}, u32[]{:S(2)}) %collective-permute-start.32) | collective-permute-done | bytes 327712 | tf_op jit(solution)/shard_map/ppermute | solution.py:638
  (100 shorter events, 46.0 us)
Async XLA Ops:
  2.8 17.4 %collective-permute-start.1 = (f32[720,256]{1,0:T(8,128)S(1)}, f32[720,256]{1,0:T(8,128)S(1)}, u32[]{:S(2)}, u32[]{:S(2)}) collective-permute-start(f32[720,256]{1,0:T(8,128)S(1)} %pack_first.1.sent_ref), channel_id=1, source_target_pairs={{0,2},{1,3},{2,0},{3,1},{4,6},{5,7},{6,4},{7,5},{8,10},{9,11},{10,... | collective-permute-start | bytes 2211848 | tf_op jit(solution)/shard_map/ppermute | solution.py:638
  7.5 31.3 %collective-permute-start.2 = (f32[712,256]{1,0:T(8,128)}, f32[712,256]{1,0:T(8,128)}, u32[]{:S(2)}, u32[]{:S(2)}) collective-permute-start(f32[712,256]{1,0:T(8,128)} %get-tuple-element.60), channel_id=1, source_target_pairs={{0,2},{1,3},{2,0},{3,1},{4,6},{5,7},{6,4},{7,5},{8,10},{9,11},{10,... | collective-permute-start | bytes 2187272 | tf_op jit(solution)/shard_map/ppermute | solution.py:638
  7.8 43.8 %collective-permute-start.6 = (f32[712,256]{1,0:T(8,128)}, f32[712,256]{1,0:T(8,128)}, u32[]{:S(2)}, u32[]{:S(2)}) collective-permute-start(f32[712,256]{1,0:T(8,128)} %get-tuple-element.67), channel_id=1, source_target_pairs={{0,2},{1,3},{2,0},{3,1},{4,6},{5,7},{6,4},{7,5},{8,10},{9,11},{10,... | collective-permute-start | bytes 2187272 | tf_op jit(solution)/shard_map/ppermute | solution.py:638
  40.4 13.1 %collective-permute-start.5 = (f32[712,256]{1,0:T(8,128)S(1)}, f32[712,256]{1,0:T(8,128)S(1)}, u32[]{:S(2)}, u32[]{:S(2)}) collective-permute-start(f32[712,256]{1,0:T(8,128)S(1)} %get-tuple-element.64), channel_id=1, source_target_pairs={{1,4},{4,1},{3,6},{6,3},{5,8},{8,5},{7,10},{10,7},{9,12},{12,9},{1... | collective-permute-start | bytes 2187272 | tf_op jit(solution)/shard_map/ppermute | solution.py:646
  43.8 23.2 %collective-permute-start = (f32[712,256]{1,0:T(8,128)S(1)}, f32[712,256]{1,0:T(8,128)S(1)}, u32[]{:S(2)}, u32[]{:S(2)}) collective-permute-start(f32[712,256]{1,0:T(8,128)S(1)} %copy-done.11), channel_id=1, source_target_pairs={{0,2},{1,3},{2,0},{3,1},{4,6},{5,7},{6,4},{7,5},{8,10},{9,11},{10,... | collective-permute-start | bytes 2187272 | tf_op jit(solution)/shard_map/ppermute | solution.py:638
  55.4 18.0 %collective-permute-start.16 = (f32[712,256]{1,0:T(8,128)S(1)}, f32[712,256]{1,0:T(8,128)S(1)}, u32[]{:S(2)}, u32[]{:S(2)}) collective-permute-start(f32[712,256]{1,0:T(8,128)S(1)} %get-tuple-element.78), channel_id=1, source_target_pairs={{1,4},{4,1},{3,6},{6,3},{5,8},{8,5},{7,10},{10,7},{9,12},{12,9},{1... | collective-permute-start | bytes 2187272 | tf_op jit(solution)/shard_map/ppermute | solution.py:646
  59.3 10.9 %collective-permute-start.14 = (f32[4,176,256]{2,1,0:T(8,128)S(1)}, f32[4,176,256]{2,1,0:T(8,128)S(1)}, u32[]{:S(2)}, u32[]{:S(2)}) collective-permute-start(f32[4,176,256]{2,1,0:T(8,128)S(1)} %get-tuple-element.68.rest_0_.refs_0_), channel_id=1, source_target_pairs={{0,1},{1,0},{2,3},{3,2},{4,5},{5,4},{6,7},{7,6},{8,9},{9,8},{10,11... | collective-permute-start | bytes 2162696 | tf_op jit(solution)/shard_map/ppermute | solution.py:644
  59.4 23.3 %collective-permute-start.9 = (f32[712,256]{1,0:T(8,128)S(1)}, f32[712,256]{1,0:T(8,128)S(1)}, u32[]{:S(2)}, u32[]{:S(2)}) collective-permute-start(f32[712,256]{1,0:T(8,128)S(1)} %copy-done.10), channel_id=1, source_target_pairs={{0,2},{1,3},{2,0},{3,1},{4,6},{5,7},{6,4},{7,5},{8,10},{9,11},{10,... | collective-permute-start | bytes 2187272 | tf_op jit(solution)/shard_map/ppermute | solution.py:638
  60.7 12.6 %collective-permute-start.15 = (f32[4,176,256]{2,1,0:T(8,128)S(1)}, f32[4,176,256]{2,1,0:T(8,128)S(1)}, u32[]{:S(2)}, u32[]{:S(2)}) collective-permute-start(f32[4,176,256]{2,1,0:T(8,128)S(1)} %get-tuple-element.77.refs_1_), channel_id=1, source_target_pairs={{0,1},{1,0},{2,3},{3,2},{4,5},{5,4},{6,7},{7,6},{8,9},{9,8},{10,11... | collective-permute-start | bytes 2162696 | tf_op jit(solution)/shard_map/ppermute | solution.py:645
  67.4 16.9 %collective-permute-start.7 = (f32[4,176,256]{2,1,0:T(8,128)S(1)}, f32[4,176,256]{2,1,0:T(8,128)S(1)}, u32[]{:S(2)}, u32[]{:S(2)}) collective-permute-start(f32[4,176,256]{2,1,0:T(8,128)S(1)} %get-tuple-element.69.refs_0_.refs_1_.refs_5_.refs_8_), channel_id=1, source_target_pairs={{0,1},{1,0},{2,3},{3,2},{4,5},{5,4},{6,7},{7,6},{8,9},{9,8},{10,11... | collective-permute-start | bytes 2162696 | tf_op jit(solution)/shard_map/ppermute | solution.py:644
  70.1 16.1 %collective-permute-start.10 = (f32[712,256]{1,0:T(8,128)S(1)}, f32[712,256]{1,0:T(8,128)S(1)}, u32[]{:S(2)}, u32[]{:S(2)}) collective-permute-start(f32[712,256]{1,0:T(8,128)S(1)} %get-tuple-element.72), channel_id=1, source_target_pairs={{1,4},{4,1},{3,6},{6,3},{5,8},{8,5},{7,10},{10,7},{9,12},{12,9},{1... | collective-permute-start | bytes 2187272 | tf_op jit(solution)/shard_map/ppermute | solution.py:646
  73.3 11.1 %collective-permute-start.8 = (f32[4,176,256]{2,1,0:T(8,128)S(1)}, f32[4,176,256]{2,1,0:T(8,128)S(1)}, u32[]{:S(2)}, u32[]{:S(2)}) collective-permute-start(f32[4,176,256]{2,1,0:T(8,128)S(1)} %get-tuple-element.70.refs_1_.refs_2_.refs_9_), channel_id=1, source_target_pairs={{0,1},{1,0},{2,3},{3,2},{4,5},{5,4},{6,7},{7,6},{8,9},{9,8},{10,11... | collective-permute-start | bytes 2162696 | tf_op jit(solution)/shard_map/ppermute | solution.py:645
  76.4 17.7 %collective-permute-start.19 = (f32[712,256]{1,0:T(8,128)S(1)}, f32[712,256]{1,0:T(8,128)S(1)}, u32[]{:S(2)}, u32[]{:S(2)}) collective-permute-start(f32[712,256]{1,0:T(8,128)S(1)} %get-tuple-element.82), channel_id=1, source_target_pairs={{1,4},{4,1},{3,6},{6,3},{5,8},{8,5},{7,10},{10,7},{9,12},{12,9},{1... | collective-permute-start | bytes 2187272 | tf_op jit(solution)/shard_map/ppermute | solution.py:646
  82.7 8.4 %collective-permute-start.17 = (f32[4,176,256]{2,1,0:T(8,128)S(1)}, f32[4,176,256]{2,1,0:T(8,128)S(1)}, u32[]{:S(2)}, u32[]{:S(2)}) collective-permute-start(f32[4,176,256]{2,1,0:T(8,128)S(1)} %get-tuple-element.80.refs_0_), channel_id=1, source_target_pairs={{0,1},{1,0},{2,3},{3,2},{4,5},{5,4},{6,7},{7,6},{8,9},{9,8},{10,11... | collective-permute-start | bytes 2162696 | tf_op jit(solution)/shard_map/ppermute | solution.py:644
  84.2 7.4 %collective-permute-start.18 = (f32[4,176,256]{2,1,0:T(8,128)S(1)}, f32[4,176,256]{2,1,0:T(8,128)S(1)}, u32[]{:S(2)}, u32[]{:S(2)}) collective-permute-start(f32[4,176,256]{2,1,0:T(8,128)S(1)} %get-tuple-element.81.refs_1_), channel_id=1, source_target_pairs={{0,1},{1,0},{2,3},{3,2},{4,5},{5,4},{6,7},{7,6},{8,9},{9,8},{10,11... | collective-permute-start | bytes 2162696 | tf_op jit(solution)/shard_map/ppermute | solution.py:645
  87.4 14.6 %collective-permute-start.13 = (f32[712,256]{1,0:T(8,128)S(1)}, f32[712,256]{1,0:T(8,128)S(1)}, u32[]{:S(2)}, u32[]{:S(2)}) collective-permute-start(f32[712,256]{1,0:T(8,128)S(1)} %get-tuple-element.76), channel_id=1, source_target_pairs={{1,4},{4,1},{3,6},{6,3},{5,8},{8,5},{7,10},{10,7},{9,12},{12,9},{1... | collective-permute-start | bytes 2187272 | tf_op jit(solution)/shard_map/ppermute | solution.py:646
  95.4 18.0 %collective-permute-start.26 = (f32[720,256]{1,0:T(8,128)S(1)}, f32[720,256]{1,0:T(8,128)S(1)}, u32[]{:S(2)}, u32[]{:S(2)}) collective-permute-start(f32[720,256]{1,0:T(8,128)S(1)} %get-tuple-element.94), channel_id=1, source_target_pairs={{0,2},{1,3},{2,0},{3,1},{4,6},{5,7},{6,4},{7,5},{8,10},{9,11},{10,... | collective-permute-start | bytes 2211848 | tf_op jit(solution)/shard_map/ppermute | solution.py:638
  96.6 13.0 %collective-permute-start.25 = (f32[712,256]{1,0:T(8,128)S(1)}, f32[712,256]{1,0:T(8,128)S(1)}, u32[]{:S(2)}, u32[]{:S(2)}) collective-permute-start(f32[712,256]{1,0:T(8,128)S(1)} %get-tuple-element.92), channel_id=1, source_target_pairs={{1,4},{4,1},{3,6},{6,3},{5,8},{8,5},{7,10},{10,7},{9,12},{12,9},{1... | collective-permute-start | bytes 2187272 | tf_op jit(solution)/shard_map/ppermute | solution.py:646
  103.5 13.9 %collective-permute-start.24 = (f32[712,256]{1,0:T(8,128)S(1)}, f32[712,256]{1,0:T(8,128)S(1)}, u32[]{:S(2)}, u32[]{:S(2)}) collective-permute-start(f32[712,256]{1,0:T(8,128)S(1)} %get-tuple-element.90), channel_id=1, source_target_pairs={{1,4},{4,1},{3,6},{6,3},{5,8},{8,5},{7,10},{10,7},{9,12},{12,9},{1... | collective-permute-start | bytes 2187272 | tf_op jit(solution)/shard_map/ppermute | solution.py:646
  110.1 18.6 %collective-permute-start.31 = (f32[648,256]{1,0:T(8,128)S(1)}, f32[648,256]{1,0:T(8,128)S(1)}, u32[]{:S(2)}, u32[]{:S(2)}) collective-permute-start(f32[648,256]{1,0:T(8,128)S(1)} %get-tuple-element.103), channel_id=1, source_target_pairs={{0,2},{1,3},{2,0},{3,1},{4,6},{5,7},{6,4},{7,5},{8,10},{9,11},{10,... | collective-permute-start | bytes 1990664 | tf_op jit(solution)/shard_map/ppermute | solution.py:638
  119.4 8.7 %collective-permute-start.30 = (f32[320,256]{1,0:T(8,128)S(1)}, f32[320,256]{1,0:T(8,128)S(1)}, u32[]{:S(2)}, u32[]{:S(2)}) collective-permute-start(f32[320,256]{1,0:T(8,128)S(1)} %get-tuple-element.101), channel_id=1, source_target_pairs={{1,4},{4,1},{3,6},{6,3},{5,8},{8,5},{7,10},{10,7},{9,12},{12,9},{1... | collective-permute-start | bytes 983048 | tf_op jit(solution)/shard_map/ppermute | solution.py:646
  122.6 8.9 %collective-permute-start.29 = (f32[320,256]{1,0:T(8,128)S(1)}, f32[320,256]{1,0:T(8,128)S(1)}, u32[]{:S(2)}, u32[]{:S(2)}) collective-permute-start(f32[320,256]{1,0:T(8,128)S(1)} %get-tuple-element.99), channel_id=1, source_target_pairs={{1,4},{4,1},{3,6},{6,3},{5,8},{8,5},{7,10},{10,7},{9,12},{12,9},{1... | collective-permute-start | bytes 983048 | tf_op jit(solution)/shard_map/ppermute | solution.py:718
  128.4 9.5 %collective-permute-start.33 = (f32[4,80,256]{2,1,0:T(8,128)S(1)}, f32[4,80,256]{2,1,0:T(8,128)S(1)}, u32[]{:S(2)}, u32[]{:S(2)}) collective-permute-start(f32[4,80,256]{2,1,0:T(8,128)S(1)} %get-tuple-element.106), channel_id=1, source_target_pairs={{0,2},{1,3},{2,0},{3,1},{4,6},{5,7},{6,4},{7,5},{8,10},{9,11},{10,... | collective-permute-start | bytes 983048 | tf_op jit(solution)/shard_map/ppermute | solution.py:638
  131.9 13.0 %collective-permute-start.32 = (f32[4,80,256]{2,1,0:T(8,128)S(1)}, f32[4,80,256]{2,1,0:T(8,128)S(1)}, u32[]{:S(2)}, u32[]{:S(2)}) collective-permute-start(f32[4,80,256]{2,1,0:T(8,128)S(1)} %get-tuple-element.104), channel_id=1, source_target_pairs={{0,2},{1,3},{2,0},{3,1},{4,6},{5,7},{6,4},{7,5},{8,10},{9,11},{10,... | collective-permute-start | bytes 983048 | tf_op jit(solution)/shard_map/ppermute | solution.py:638
  (22 other events, 116.0 us)
